TPU v7x, 768 devices: a whole 4x8x12 slice. The times are simulated.
768 devices in a mesh: dp: 24 (over z, core), mp: 8 (over y), rep: 4 (over x).
Axes of the slice: x: 4, y: 8, z: 12, core: 2. Of those that a mesh axis runs over, the one named last changes fastest.
Arguments:
- tokens: bfloat16 [24576, 256], P(('dp', 'rep')), may hold values from -6 to 6
- cotangent: bfloat16 [24576, 53248], P(('dp', 'rep'), 'mp'), may hold values from -0.0390625 to 0.0390625
- token_counts: int32 [24, 4], P('dp', 'rep'), may hold values from 128 to 256, as said below
- old_bounds: int32 [8, 24, 2], P('mp', 'dp'), may hold values from 0 to 1916928, as said below
- old_first: float32 [8, 3833856], P('mp', 'dp'), may hold values from -3 to 3
- old_second: float32 [8, 3833856], P('mp', 'dp'), may hold values from 0.05 to 2
- old_master: float32 [8, 3833856], P('mp', 'dp'), may hold values from -6 to 6
Outputs:
- new_master: float32 [8, 1916928], P('mp', 'dp')
- new_first: float32 [8, 1916928], P('mp', 'dp')
- new_second: float32 [8, 1916928], P('mp', 'dp')
Inputs may be any that keep to these rules, and one draw needn't show every extreme that they name: `old_bounds`: for each slab s, row j holds the boundaries b_j and b_(j+1) of that slab's list with b_0 = 0 and b_(24) = 1916928; every b_j lies within 33280 of j * 79872; some b_j lies exactly 33280 away from it. `token_counts`: some data rank has all 256 tokens live.
All inputs are finite; a program needn't handle non-finite values.
Results may differ from a plain program's by a relative error of at most 0.0003.
Values sent between devices are 32-bit elements; how exact they have to be, the bound alone decides.
No kernel may reach another device: no remote copies, remote signals or barrier semaphores. Data moves between devices by JAX's collectives and lax.ppermute only.
A program may use at most 64 MiB of HBM per device.

v0:
```python
import jax
import jax.numpy as jnp
from jax import lax
from jax.sharding import PartitionSpec as P

ADAM_STEP = 1000


BETA_ONE = 0.9
BETA_TWO = 0.95
LEARN_RATE = 0.001
DECAY_RATE = 0.1
EPSILON = 1e-08


def from_behind(value, axis, by):
    size = lax.axis_size(axis)
    pairs = [(i, i + by) for i in range(size) if 0 <= i + by < size]
    return lax.ppermute(value, axis, pairs)


def adam_step(first, second, master, gradient):
    first_new = BETA_ONE * first + (1.0 - BETA_ONE) * gradient
    second_new = BETA_TWO * second + (1.0 - BETA_TWO) * gradient * gradient
    corr_one = 1.0 - BETA_ONE**ADAM_STEP
    corr_two = 1.0 - BETA_TWO**ADAM_STEP
    update = (
        first_new / corr_one / (jnp.sqrt(second_new / corr_two) + EPSILON) + DECAY_RATE * master
    )
    return (master - LEARN_RATE * update, first_new, second_new)


def local(tokens, cotangent, token_counts, old_bounds, old_first, old_second, old_master):
    shard_count = lax.axis_size("dp")
    buffer_len = old_first.shape[1]
    shard_len = buffer_len // 2
    col_count = cotangent.shape[1]
    half_span = shard_len // 2 - col_count
    tok_rows = tokens.shape[0]
    live_rows = jnp.arange(tok_rows, dtype=jnp.int32) < token_counts[0, 0]
    masked = jnp.where(live_rows[:, None], tokens, jnp.zeros_like(tokens))
    depth_rows = shard_count * shard_len // col_count
    padded_tokens = jnp.concatenate(
        [masked, jnp.zeros((tok_rows, depth_rows - tokens.shape[1]), jnp.bfloat16)], axis=1
    )
    shard_index = lax.axis_index("dp")
    lower_end = old_bounds[0, 0, 0]
    upper_end = old_bounds[0, 0, 1]
    stacked = jnp.concatenate([old_first, old_second, old_master], axis=0)
    buffer = jnp.pad(stacked, ((0, 0), (2 * half_span, half_span)))
    base_flat = shard_index * shard_len

    def window(flat_start, length):
        offset = flat_start - lower_end + 2 * half_span
        sliced = lax.dynamic_slice_in_dim(buffer, offset, length, 1)
        flat_pos = flat_start + jnp.arange(length, dtype=jnp.int32)
        keep_mask = (flat_pos >= lower_end) & (flat_pos < upper_end)
        return jnp.where(keep_mask[None, :], sliced, jnp.zeros_like(sliced))

    own_part = window(base_flat, shard_len)
    to_right = window(base_flat + shard_len, half_span)
    to_left = window(base_flat - half_span, half_span)
    left_in = from_behind(to_right, "dp", 1)
    right_in = from_behind(to_left, "dp", -1)
    state = own_part + jnp.pad(left_in, ((0, 0), (0, shard_len - half_span)))
    state = state + jnp.pad(right_in, ((0, 0), (shard_len - half_span, 0)))
    grad_part = lax.psum_scatter(
        lax.dot_general(
            padded_tokens, cotangent, (((0,), (0,)), ((), ())), preferred_element_type=jnp.float32
        ),
        "dp",
        scatter_dimension=0,
        tiled=True,
    )
    gradient = lax.psum(grad_part, "rep").reshape(1, shard_len)
    new_master, new_first, new_second = adam_step(state[0:1], state[1:2], state[2:3], gradient)
    return (new_master, new_first, new_second)


def solution(mesh):
    placed = (
        P(("dp", "rep"), None),
        P(("dp", "rep"), "mp"),
        P("dp", "rep"),
        P("mp", "dp", None),
        P("mp", "dp"),
        P("mp", "dp"),
        P("mp", "dp"),
    )
    return jax.shard_map(
        local,
        mesh=mesh,
        in_specs=placed,
        out_specs=(P("mp", "dp"), P("mp", "dp"), P("mp", "dp")),
        check_vma=False,
    )
```

profile of v0, /device:TPU:56, one launch (start us, length us, event | category | flops | bytes accessed | tf_op | source)
XLA Modules:
  0.0 291.1 jit_solution(8180782648090860356)
XLA Ops:
  7.2 0.0 copy-start
  7.2 0.0 all-reduce.8.cloned.1.call-start
  8.0 1.2 broadcast_select_fusion
  9.2 4.2 %fusion.7 = f32[288,6656]{1,0:T(8,128)} fusion(bf16[256,6656]{1,0:T(8,128)(2,1)S(1)} %copy-done, bf16[256,256]{1,0:T(8,128)(2,1)S(1)} %broadcast_select_fusion), kind=kOutput, calls=%fused_computation.19 | convolution fusion | flops 981467136 | bytes 11206656 | tf_op jit(solution)/shard_map/dot_general | solution.py:68
  13.4 72.6 %fusion = f32[16,6656]{1,0:T(8,128)} fusion(f32[288,6656]{1,0:T(8,128)} %fusion.7), kind=kCustom, calls=%all-reduce-scatter | all-reduce-scatter fusion | flops 2555905 | bytes 8097792
  86.0 2.0 collective-permute-start.2
  88.0 2.1 collective-permute-start.3
  90.1 2.1 collective-permute-start.4
  92.2 2.0 collective-permute-start.5
  94.2 1.9 slice.23
  96.1 9.8 %collective-permute-start.7 = (f32[12,6656]{1,0:T(8,128)}, f32[12,6656]{1,0:T(8,128)}, u32[]{:S(2)}, u32[]{:S(2)}) collective-permute-start(f32[12,6656]{1,0:T(8,128)} %slice.23), channel_id=1, source_target_pairs={{0,192},{32,224},{64,256},{96,288},{128,320},{160,352},{192,384},{... | collective-permute-start | bytes 958472
  105.8 0.6 fusion.18
  107.7 1.4 fusion.13
  109.1 6.3 %select_maximum_fusion = f32[3,259584]{1,0:T(4,128)S(1)} fusion(f32[1,159744]{1,0:T(1,128)} %param.13, f32[1,159744]{1,0:T(1,128)} %param.12, f32[1,159744]{1,0:T(1,128)} %param.11), kind=kLoop, calls=%fused_computation.2 | loop fusion | flops 6230016 | bytes 5031936 | tf_op jit(solution)/shard_map/concatenate | solution.py:49
  115.4 1.9 copy-done.1
  117.3 1.6 dynamic-slice_select_fusion.1
  119.0 8.3 %collective-permute-done.7 = f32[12,6656]{1,0:T(8,128)} collective-permute-done((f32[12,6656]{1,0:T(8,128)}, f32[12,6656]{1,0:T(8,128)}, u32[]{:S(2)}, u32[]{:S(2)}) %collective-permute-start.7) | collective-permute-done | bytes 319520
  127.2 45.7 %collective-permute-start.6 = (f32[16,6656]{1,0:T(8,128)}, f32[16,6656]{1,0:T(8,128)}, u32[]{:S(2)}, u32[]{:S(2)}) collective-permute-start(f32[16,6656]{1,0:T(8,128)} %fusion), channel_id=1, source_target_pairs={{0,160},{32,192},{64,224},{96,256},{128,288},{160,320},{192,352},{... | collective-permute-start | bytes 1277960
  173.0 1.4 fusion.6
  175.0 1.3 dynamic-slice.4
  176.9 0.0 collective-permute-done.2
  177.0 2.1 collective-permute-start
  179.1 0.0 collective-permute-done.3
  179.1 1.3 collective-permute-start.1
  180.4 0.0 collective-permute-done.4
  180.4 28.1 %concatenate.8 = f32[108,6656]{1,0:T(8,128)} concatenate(f32[12,6656]{1,0:T(8,128)} %collective-permute-done.7, f32[16,6656]{1,0:T(8,128)} %collective-permute-done.6, f32[16,6656]{1,0:T(8,128)} %collective-permute-done.5, f32[16,6656]{1,0:T(8,128)} %collective-permute-done.4, f32[16,6656]{1,0:T(8,128)} %collective-permute-done.3, f32[16,6656]{1,0:T(8,128)} %collective-permute-done.2, ...), dimensions={0} | concatenate | bytes 5750784
  208.5 1.1 dynamic-slice_bitcast_fusion
  209.6 1.1 copy.10
  210.7 0.0 all-reduce.8.cloned.1.call-update
  210.7 3.5 %pad_add_fusion = f32[3,79872]{1,0:T(4,128)} fusion(f32[3,33280]{1,0:T(4,128)} %collective-permute-done.1, f32[3,33280]{1,0:T(4,128)} %collective-permute-done, f32[3,259584]{1,0:T(4,128)} %copy-done.1, s32[]{:T(128)S(6)} %select_n.24, pred[79872]{0:T(1024)(128)(4,1)S(1)} %fusion.6), kind=kLoop, calls=%fused_computation.5 | loop fusion | flops 718848 | bytes 2795524 | tf_op jit(solution)/shard_map/add | solution.py:66
  214.2 64.9 %all-reduce.8.cloned.1.call-done = f32[1,79872]{1,0:T(1,128)} async-done(((f32[1,79872]{1,0:T(1,128)}), f32[1,79872]{1,0:T(1,128)}) %all-reduce.8.cloned.1.call-update) | async-done | bytes 319504 | tf_op jit(solution)/shard_map/psum | solution.py:75
  279.0 5.3 %multiply_subtract_fusion = (f32[1,79872]{1,0:T(1,128)}, f32[1,79872]{1,0:T(1,128)}, f32[1,79872]{1,0:T(1,128)}) fusion(f32[3,79872]{1,0:T(4,128)} %pad_add_fusion, f32[1,79872]{1,0:T(1,128)} %all-reduce.8.cloned.1.call-done), kind=kLoop, calls=%fused_computation.14 | loop fusion | flops 1038336 | bytes 2236416 | tf_op jit(solution)/shard_map/sub | solution.py:30
  (9 shorter events, 0.0 us)
Async XLA Ops:
  7.2 2.1 copy-start
  7.2 271.8 %all-reduce.8.cloned.1.call-start = ((), (), s32[]{:S(2)}) async-start(), calls=%async_computation | async-start | bytes 638976 | tf_op jit(solution)/shard_map/psum | solution.py:75
  13.4 92.4 %copy-start.2 = (s32[1,1,2]{2,1,0:T(1,128)S(1)}, s32[1,1,2]{2,1,0:T(1,128)}, u32[]{:S(2)}) copy-start(s32[1,1,2]{2,1,0:T(1,128)} %param.10) | copy-start | bytes 28
  86.0 91.0 %collective-permute-start.2 = (f32[16,6656]{1,0:T(8,128)}, f32[16,6656]{1,0:T(8,128)}, u32[]{:S(2)}, u32[]{:S(2)}) collective-permute-start(f32[16,6656]{1,0:T(8,128)} %fusion), channel_id=1, source_target_pairs={{0,32},{32,64},{64,96},{96,128},{128,160},{160,192},{192,224},{224... | collective-permute-start | bytes 1277960
  88.0 91.1 %collective-permute-start.3 = (f32[16,6656]{1,0:T(8,128)}, f32[16,6656]{1,0:T(8,128)}, u32[]{:S(2)}, u32[]{:S(2)}) collective-permute-start(f32[16,6656]{1,0:T(8,128)} %fusion), channel_id=1, source_target_pairs={{0,64},{32,96},{64,128},{96,160},{128,192},{160,224},{192,256},{22... | collective-permute-start | bytes 1277960
  90.1 90.3 %collective-permute-start.4 = (f32[16,6656]{1,0:T(8,128)}, f32[16,6656]{1,0:T(8,128)}, u32[]{:S(2)}, u32[]{:S(2)}) collective-permute-start(f32[16,6656]{1,0:T(8,128)} %fusion), channel_id=1, source_target_pairs={{0,96},{32,128},{64,160},{96,192},{128,224},{160,256},{192,288},{2... | collective-permute-start | bytes 1277960
  92.2 88.2 %collective-permute-start.5 = (f32[16,6656]{1,0:T(8,128)}, f32[16,6656]{1,0:T(8,128)}, u32[]{:S(2)}, u32[]{:S(2)}) collective-permute-start(f32[16,6656]{1,0:T(8,128)} %fusion), channel_id=1, source_target_pairs={{0,128},{32,160},{64,192},{96,224},{128,256},{160,288},{192,320},{... | collective-permute-start | bytes 1277960
  96.1 31.2 %collective-permute-start.7 = (f32[12,6656]{1,0:T(8,128)}, f32[12,6656]{1,0:T(8,128)}, u32[]{:S(2)}, u32[]{:S(2)}) collective-permute-start(f32[12,6656]{1,0:T(8,128)} %slice.23), channel_id=1, source_target_pairs={{0,192},{32,224},{64,256},{96,288},{128,320},{160,352},{192,384},{... | collective-permute-start | bytes 958472
  115.4 1.9 copy-start.1
  127.2 53.2 %collective-permute-start.6 = (f32[16,6656]{1,0:T(8,128)}, f32[16,6656]{1,0:T(8,128)}, u32[]{:S(2)}, u32[]{:S(2)}) collective-permute-start(f32[16,6656]{1,0:T(8,128)} %fusion), channel_id=1, source_target_pairs={{0,160},{32,192},{64,224},{96,256},{128,288},{160,320},{192,352},{... | collective-permute-start | bytes 1277960
  177.0 33.8 %collective-permute-start = (f32[3,33280]{1,0:T(4,128)}, f32[3,33280]{1,0:T(4,128)}, u32[]{:S(2)}, u32[]{:S(2)}) collective-permute-start(f32[3,33280]{1,0:T(4,128)} %get-tuple-element.6), channel_id=1, source_target_pairs={{0,32},{32,64},{64,96},{96,128},{128,160},{160,192},{192,224},{224... | collective-permute-start | bytes 1198088 | tf_op jit(solution)/shard_map/ppermute | solution.py:19
  179.1 31.6 %collective-permute-start.1 = (f32[3,33280]{1,0:T(4,128)}, f32[3,33280]{1,0:T(4,128)}, u32[]{:S(2)}, u32[]{:S(2)}) collective-permute-start(f32[3,33280]{1,0:T(4,128)} %get-tuple-element.7), channel_id=1, source_target_pairs={{32,0},{64,32},{96,64},{128,96},{160,128},{192,160},{224,192},{256... | collective-permute-start | bytes 1198088 | tf_op jit(solution)/shard_map/ppermute | solution.py:19
Sparse Core Ops, SparseCore 0:
  210.8 68.1 all-reduce.7
where the time goes:
time: 293 us; the launch traced here: 291 us
  waiting for transfers between devices  73.2 us (25%)
  blocking collectives  72.6 us (25%)
  starting transfers between devices  67.2 us (23%)
  local copies, waits for them, and re-layouts  35.9 us (12%)
  other arithmetic  20.5 us (7%)
  between operations  17.6 us (6%)
  matrix products  4.2 us (1%)
    unnamed x1, blocking collectives  72.6 us
    psum x1, waiting for transfers between devices, local(): gradient = lax.psum(grad_part, 'rep').reshape(1, shard_len)  64.9 us
    unnamed x6, starting transfers between devices  63.7 us
    unnamed x11, local copies, waits for them, and re-layouts  35.3 us
    unnamed x7, waiting for transfers between devices  8.31 us
    concatenate x1, other arithmetic, local(): stacked = jnp.concatenate([old_first, old_second, old_master], axis=0)  6.29 us
  transfers between devices with their start and end apart: 9, of which 2 were waited for; matrix products, arithmetic and copies ran while one was open for 17% of the time, Pallas kernels for 0%

commit v1 on v0

v1 whole, which is shorter than its diff:
```python
import functools

import jax
import jax.numpy as jnp
from jax import lax
from jax.experimental import pallas as pl
from jax.experimental.pallas import tpu as pltpu
from jax.sharding import PartitionSpec as P

ADAM_STEP = 1000
BETA_ONE = 0.9
BETA_TWO = 0.95
LEARN_RATE = 0.001
DECAY_RATE = 0.1
EPSILON = 1e-08

SHARDS = 24
COLS = 6656
BROWS = 256
LANES = 128
P_SIZE = 79872
HALF = 33280
CAP = 159744
ROWS = P_SIZE // LANES
HROWS = HALF // LANES
CROWS = CAP // LANES
FRONT = 264
SROWS = 39
SCOLS = 2048
STEP_COLS = 512
GROWS = P_SIZE // COLS


def grad_kernel(count_ref, tok_ref, c0_ref, c1_ref, c2_ref, c3_ref, out_ref, lhs_ref):
    step = pl.program_id(0)
    total = SHARDS * SROWS
    tok_row = lax.broadcasted_iota(jnp.int32, (BROWS, BROWS), 0)
    tok = jnp.where(tok_row < count_ref[0], tok_ref[...], jnp.zeros_like(tok_ref))
    row = lax.broadcasted_iota(jnp.int32, (total, BROWS), 0)
    col = lax.broadcasted_iota(jnp.int32, (total, BROWS), 1)
    shard = lax.shift_right_logical(row * 1681, 16)
    inner = row - shard * SROWS
    lead = col - shard * GROWS

    def picked(match):
        one = jnp.where(match, jnp.float32(1), jnp.float32(0)).astype(jnp.bfloat16)
        out = lax.dot_general(one, tok, (((1,), (1,)), ((), ())), preferred_element_type=jnp.float32)
        return out.astype(jnp.bfloat16)

    @pl.when(step == 0)
    def _():
        for q in range(3):
            fits = (inner >= GROWS * q) & (inner < GROWS * (q + 1))
            lhs_ref[q] = picked(fits & (lead == inner - GROWS * q))

    last = picked((inner >= 36) & (lead == 4 * (inner - 36) + step))

    def dot(a, b):
        return jnp.dot(a, b[...], preferred_element_type=jnp.float32)

    acc = dot(lhs_ref[0], c0_ref) + dot(lhs_ref[1], c1_ref)
    out_ref[...] = acc + dot(lhs_ref[2], c2_ref) + dot(last, c3_ref)


def local_gradient(tokens, cotangent, count):
    block = (BROWS, STEP_COLS)
    return pl.pallas_call(
        grad_kernel,
        grid=(4,),
        in_specs=[
            pl.BlockSpec(memory_space=pltpu.SMEM),
            pl.BlockSpec((BROWS, BROWS), lambda k: (0, 0)),
            pl.BlockSpec(block, lambda k: (0, k)),
            pl.BlockSpec(block, lambda k: (0, 4 + k)),
            pl.BlockSpec(block, lambda k: (0, 8 + k)),
            pl.BlockSpec(block, lambda k: (0, 12)),
        ],
        out_specs=pl.BlockSpec((SHARDS * SROWS, STEP_COLS), lambda k: (0, k)),
        out_shape=jax.ShapeDtypeStruct((SHARDS * SROWS, SCOLS), jnp.float32),
        scratch_shapes=[pltpu.VMEM((3, SHARDS * SROWS, BROWS), jnp.bfloat16)],
        compiler_params=pltpu.CompilerParams(vmem_limit_bytes=56 * 1024 * 1024),
        cost_estimate=pl.CostEstimate(flops=4 * 10**9, bytes_accessed=11 * 10**6, transcendentals=0),
    )(count, tokens, cotangent, cotangent, cotangent, cotangent)


def shifted(ref, start, rows):
    start = start + FRONT * LANES
    top = lax.shift_right_logical(start, 7)
    lane_start = start - top * LANES
    first = pltpu.roll(ref[pl.ds(top, rows), :], LANES - lane_start, 1)
    second = pltpu.roll(ref[pl.ds(top + 1, rows), :], LANES - lane_start, 1)
    lane = lax.broadcasted_iota(jnp.int32, (rows, LANES), 1)
    return jnp.where(lane < LANES - lane_start, first, second)


def load_old(refs, buf, sem):
    copies = [pltpu.make_async_copy(r, buf.at[i, pl.ds(FRONT, CROWS)], sem.at[i]) for i, r in enumerate(refs)]
    for c in copies:
        c.start()
    for i in range(3):
        buf[i, :FRONT, :] = jnp.zeros((FRONT, LANES), jnp.float32)
        buf[i, FRONT + CROWS :, :] = jnp.zeros((8, LANES), jnp.float32)
    for c in copies:
        c.wait()


def halo_kernel(place_ref, a_ref, b_ref, c_ref, right_ref, left_ref, buf, sem):
    load_old((a_ref, b_ref, c_ref), buf, sem)
    ahead = lax.axis_index("dp") * P_SIZE - place_ref[0]
    for i in range(3):
        right_ref[i] = shifted(buf.at[i], ahead + P_SIZE, HROWS)
        left_ref[i] = shifted(buf.at[i], jnp.maximum(ahead, 0) - HALF, HROWS)


def state_kernel(place_ref, a_ref, b_ref, c_ref, left_ref, right_ref, out_ref, buf, sem):
    load_old((a_ref, b_ref, c_ref), buf, sem)
    base = lax.axis_index("dp") * P_SIZE
    lower, upper = place_ref[0], place_ref[1]
    row = lax.broadcasted_iota(jnp.int32, (ROWS, LANES), 0)
    lane = lax.broadcasted_iota(jnp.int32, (ROWS, LANES), 1)
    pos = base + row * LANES + lane
    tail = ROWS - HROWS
    for i in range(3):
        own = shifted(buf.at[i], base - lower, ROWS)
        out_ref[i] = own
        out_ref[i, :HROWS, :] = jnp.where(pos[:HROWS] < lower, left_ref[i], own[:HROWS])
        out_ref[i, tail:, :] = jnp.where(pos[tail:] >= upper, right_ref[i], own[tail:])


OLD_SCRATCH = (
    pltpu.VMEM((3, FRONT + CROWS + 8, LANES), jnp.float32),
    pltpu.SemaphoreType.DMA((3,)),
)
SMEM_SPEC = pl.BlockSpec(memory_space=pltpu.SMEM)
ANY_SPEC = pl.BlockSpec(memory_space=pl.ANY)
VMEM_SPEC = pl.BlockSpec(memory_space=pltpu.VMEM)


def halos(place, old):
    shape = jax.ShapeDtypeStruct((3, HROWS, LANES), jnp.float32)
    return pl.pallas_call(
        halo_kernel,
        in_specs=[SMEM_SPEC, ANY_SPEC, ANY_SPEC, ANY_SPEC],
        out_specs=(VMEM_SPEC, VMEM_SPEC),
        out_shape=(shape, shape),
        scratch_shapes=list(OLD_SCRATCH),
        cost_estimate=pl.CostEstimate(flops=10**6, bytes_accessed=3 * 10**6, transcendentals=0),
    )(place, *old)


def new_state(place, old, left, right):
    return pl.pallas_call(
        state_kernel,
        in_specs=[SMEM_SPEC, ANY_SPEC, ANY_SPEC, ANY_SPEC, VMEM_SPEC, VMEM_SPEC],
        out_specs=VMEM_SPEC,
        out_shape=jax.ShapeDtypeStruct((3, ROWS, LANES), jnp.float32),
        scratch_shapes=list(OLD_SCRATCH),
        cost_estimate=pl.CostEstimate(flops=10**6, bytes_accessed=4 * 10**6, transcendentals=0),
    )(place, *old, left, right)


def adam_kernel(s0_ref, s1_ref, t0_ref, t1_ref, state_ref, master_ref, first_ref, second_ref, grad):
    tiles = COLS // LANES
    for half, (s, t) in enumerate(((s0_ref, t0_ref), (s1_ref, t1_ref))):
        for j in range(8):
            at = 8 * half + j
            piece = s[:, LANES * j : LANES * (j + 1)] + t[:, LANES * j : LANES * (j + 1)]
            for q in range(3):
                grad[pl.ds(16 * q + at, GROWS, stride=tiles), :] = piece[GROWS * q : GROWS * (q + 1)]
            k, c = at // 4, at % 4
            grad[pl.ds(tiles * k + 48 + c, 3, stride=4 * tiles), :] = piece[36:39]
    corr_one = 1.0 - BETA_ONE**ADAM_STEP
    corr_two = 1.0 - BETA_TWO**ADAM_STEP
    g = grad[...]
    first_new = BETA_ONE * state_ref[0] + (1.0 - BETA_ONE) * g
    second_new = BETA_TWO * state_ref[1] + (1.0 - BETA_TWO) * g * g
    master = state_ref[2]
    update = first_new / corr_one / (jnp.sqrt(second_new / corr_two) + EPSILON) + DECAY_RATE * master
    master_ref[...] = master - LEARN_RATE * update
    first_ref[...] = first_new
    second_ref[...] = second_new


def adam_step(parts, state):
    shape = jax.ShapeDtypeStruct((ROWS, LANES), jnp.float32)
    return pl.pallas_call(
        adam_kernel,
        in_specs=[VMEM_SPEC] * 5,
        out_specs=(VMEM_SPEC,) * 3,
        out_shape=(shape,) * 3,
        scratch_shapes=[pltpu.VMEM((ROWS, LANES), jnp.float32)],
        cost_estimate=pl.CostEstimate(flops=2 * 10**6, bytes_accessed=3 * 10**6, transcendentals=10**5),
    )(*parts, state)


def local(tokens, cotangent, token_counts, old_bounds, old_first, old_second, old_master):
    place = old_bounds.reshape(2)
    old = [a.reshape(CROWS, LANES) for a in (old_first, old_second, old_master)]
    to_right, to_left = halos(place, old)
    left_in = lax.ppermute(to_right, "dp", [(i, i + 1) for i in range(SHARDS - 1)])
    right_in = lax.ppermute(to_left, "dp", [(i + 1, i) for i in range(SHARDS - 1)])

    partial = local_gradient(tokens, cotangent, token_counts.reshape(1))
    shard = lax.psum_scatter(partial, "dp", scatter_dimension=0, tiled=True)
    shard = lax.optimization_barrier(shard)

    low = [(0, 1), (1, 0), (2, 3), (3, 2)]
    high = [(1, 2), (2, 1), (3, 0), (0, 3)]
    s0, s1 = shard[:, : SCOLS // 2], shard[:, SCOLS // 2 :]
    s0 = s0 + lax.ppermute(s0, "rep", low)
    s1 = s1 + lax.ppermute(s1, "rep", high)
    t0 = lax.ppermute(s0, "rep", high)
    t1 = lax.ppermute(s1, "rep", low)

    state = new_state(place, old, left_in, right_in)
    outs = adam_step((s0, s1, t0, t1), state)
    return tuple(a.reshape(1, P_SIZE) for a in outs)


def solution(mesh):
    placed = (
        P(("dp", "rep"), None),
        P(("dp", "rep"), "mp"),
        P("dp", "rep"),
        P("mp", "dp", None),
        P("mp", "dp"),
        P("mp", "dp"),
        P("mp", "dp"),
    )
    return jax.shard_map(
        local,
        mesh=mesh,
        in_specs=placed,
        out_specs=(P("mp", "dp"), P("mp", "dp"), P("mp", "dp")),
        check_vma=False,
    )
```

time: 293 us -> 115 us (0.39)
  the two profiles are of different devices: /device:TPU:56 before, /device:TPU:1 now
where the time goes in v1:
time: 115 us; the launch traced here: 114 us
  blocking collectives  64.3 us (56%)
  starting transfers between devices  20.7 us (18%)
  Pallas kernels  19.8 us (17%)
  waiting for transfers between devices  3.74 us (3%)
  local copies, waits for them, and re-layouts  3.64 us (3%)
  between operations  2.13 us (2%)
    unnamed x1, blocking collectives  64.3 us
    pallas_call x1, Pallas kernels, local_gradient(): pl.pallas_call(grad_kernel, grid=(4,), in_specs=[pl.BlockSpec(memory_spac...  9.57 us
    ppermute x1, starting transfers between devices, local(): s1 = s1 + lax.ppermute(s1, 'rep', high)  4.39 us
    pallas_call x1, Pallas kernels, new_state(): pl.pallas_call(state_kernel, in_specs=[SMEM_SPEC, ANY_SPEC, ANY_SPEC, ANY...  4.16 us
    ppermute x1, starting transfers between devices, local(): lax.ppermute(to_right, 'dp', [(i, i + 1) for i in range(SHARDS - 1)])  4.15 us
    unnamed x16, local copies, waits for them, and re-layouts  3.62 us
    pallas_call x1, Pallas kernels, halos(): pl.pallas_call(halo_kernel, in_specs=[SMEM_SPEC, ANY_SPEC, ANY_SPEC, ANY_...  3.46 us
    unnamed x1, starting transfers between devices  2.98 us
  transfers between devices with their start and end apart: 7, of which 2 were waited for; matrix products, arithmetic and copies ran while one was open for 1% of the time, Pallas kernels for 7%

profile of v1, /device:TPU:1, one launch (start us, length us, event | category | flops | bytes accessed | tf_op | source)
XLA Modules:
  0.0 114.4 jit_solution(5746715390776780420)
XLA Ops:
  1.3 9.6 %shard_map.94 = f32[936,2048]{1,0:T(8,128)} custom-call(s32[1]{0:T(128)} %bitcast.11.count_ref, bf16[256,256]{1,0:T(8,128)(2,1)} %tok_ref.1, bf16[256,6656]{1,0:T(8,128)(2,1)} %c3_ref.1, bf16[256,6656]{1,0:T(8,128)(2,1)} %c3_ref.1, bf16[256,6656]{1,0:T(8,128)(2,1)} %c3_ref.1, bf16[256,6656]{1,0:T(8,128)(2,1)} %c3_ref.1), custom_call_target="tpu_custom_call" | custom-call | flops 4000000000 | bytes 11000000 | tf_op jit(solution)/shard_map/pallas_call | solution.py:67
  10.9 64.3 %fusion = f32[40,2048]{1,0:T(8,128)S(1)} fusion(f32[936,2048]{1,0:T(8,128)} %shard_map.94), kind=kCustom, calls=%all-reduce-scatter | all-reduce-scatter fusion | flops 1966081 | bytes 7999488
  75.2 3.0 %collective-permute-start.6 = (f32[23,2048]{1,0:T(8,128)S(1)}, f32[23,2048]{1,0:T(8,128)S(1)}, u32[]{:S(2)}, u32[]{:S(2)}) collective-permute-start(f32[23,2048]{1,0:T(8,128)S(1)} %slice.10), channel_id=1, source_target_pairs={{0,32},{32,64},{64,96},{96,128},{128,160},{160,192},{192,224},{224... | collective-permute-start | bytes 565256
  78.2 1.3 %dynamic-slice.4 = u32[1]{0:T(128)} dynamic-slice(u32[768]{0:T(1024)} %constant.9, u32[]{:S(6)} %partition-id.4), dynamic_slice_sizes={1} | dynamic-slice | bytes 12
  80.1 1.4 %collective-permute-done.6 = f32[23,2048]{1,0:T(8,128)S(1)} collective-permute-done((f32[23,2048]{1,0:T(8,128)S(1)}, f32[23,2048]{1,0:T(8,128)S(1)}, u32[]{:S(2)}, u32[]{:S(2)}) %collective-permute-start.6) | collective-permute-done | bytes 188448
  81.5 0.2 concatenate
  81.8 4.4 %collective-permute-start.1 = (f32[39,1024]{1,0:T(8,128)S(1)}, f32[39,1024]{1,0:T(8,128)S(1)}, u32[]{:S(2)}, u32[]{:S(2)}) collective-permute-start(f32[39,1024]{1,0:T(8,128)S(1)} %get-tuple-element.15), channel_id=1, source_target_pairs={{1,2},{2,1},{3,0},{0,3},{5,6},{6,5},{7,4},{4,7},{9,10},{10,9},{11,... | collective-permute-start | bytes 479240 | tf_op jit(solution)/shard_map/ppermute | solution.py:211
  86.2 1.9 %collective-permute-start = (f32[39,1024]{1,0:T(8,128)S(1)}, f32[39,1024]{1,0:T(8,128)S(1)}, u32[]{:S(2)}, u32[]{:S(2)}) collective-permute-start(f32[39,1024]{1,0:T(8,128)S(1)} %get-tuple-element.16), channel_id=1, source_target_pairs={{0,1},{1,0},{2,3},{3,2},{4,5},{5,4},{6,7},{7,6},{8,9},{9,8},{10,11... | collective-permute-start | bytes 479240 | tf_op jit(solution)/shard_map/ppermute | solution.py:210
  88.2 3.5 %shard_map.95 = (f32[3,260,128]{2,1,0:T(8,128)}, f32[3,260,128]{2,1,0:T(8,128)}) custom-call(s32[2]{0:T(128)} %bitcast.18, f32[1248,128]{1,0:T(8,128)} %bitcast.12, f32[1248,128]{1,0:T(8,128)} %bitcast.14, f32[1248,128]{1,0:T(8,128)} %bitcast.16), custom_call_target="tpu_custom_call" | custom-call | flops 1000000 | bytes 3000000 | tf_op jit(solution)/shard_map/pallas_call | solution.py:141
  91.6 4.2 %collective-permute-start.4 = (f32[3,260,128]{2,1,0:T(8,128)}, f32[3,260,128]{2,1,0:T(8,128)S(1)}, u32[]{:S(2)}, u32[]{:S(2)}) collective-permute-start(f32[3,260,128]{2,1,0:T(8,128)} %get-tuple-element.8), channel_id=1, source_target_pairs={{0,32},{32,64},{64,96},{96,128},{128,160},{160,192},{192,224},{224... | collective-permute-start | bytes 1198088 | tf_op jit(solution)/shard_map/ppermute | solution.py:200
  95.8 1.9 %collective-permute-start.5 = (f32[3,260,128]{2,1,0:T(8,128)}, f32[3,260,128]{2,1,0:T(8,128)S(1)}, u32[]{:S(2)}, u32[]{:S(2)}) collective-permute-start(f32[3,260,128]{2,1,0:T(8,128)} %get-tuple-element.9), channel_id=1, source_target_pairs={{32,0},{64,32},{96,64},{128,96},{160,128},{192,160},{224,192},{256... | collective-permute-start | bytes 1198088 | tf_op jit(solution)/shard_map/ppermute | solution.py:201
  97.7 0.0 collective-permute-done.1
  97.7 0.0 collective-permute-done
  97.8 0.0 copy-start
  97.8 0.0 copy-start.1
  97.8 2.8 %collective-permute-start.2 = (f32[39,1024]{1,0:T(8,128)S(1)}, f32[39,1024]{1,0:T(8,128)S(1)}, u32[]{:S(2)}, u32[]{:S(2)}) collective-permute-start(f32[39,1024]{1,0:T(8,128)S(1)} %get-tuple-element.14.s0_ref), channel_id=1, source_target_pairs={{1,2},{2,1},{3,0},{0,3},{5,6},{6,5},{7,4},{4,7},{9,10},{10,9},{11,... | collective-permute-start | bytes 479240 | tf_op jit(solution)/shard_map/ppermute | solution.py:212
  100.6 2.6 %collective-permute-start.3 = (f32[39,1024]{1,0:T(8,128)S(1)}, f32[39,1024]{1,0:T(8,128)S(1)}, u32[]{:S(2)}, u32[]{:S(2)}) collective-permute-start(f32[39,1024]{1,0:T(8,128)S(1)} %get-tuple-element.13.s1_ref), channel_id=1, source_target_pairs={{0,1},{1,0},{2,3},{3,2},{4,5},{5,4},{6,7},{7,6},{8,9},{9,8},{10,11... | collective-permute-start | bytes 479240 | tf_op jit(solution)/shard_map/ppermute | solution.py:213
  103.2 0.0 collective-permute-done.4.left_ref
  103.2 0.0 copy-start.2
  103.2 2.3 %collective-permute-done.5.right_ref = f32[3,260,128]{2,1,0:T(8,128)S(1)} collective-permute-done((f32[3,260,128]{2,1,0:T(8,128)}, f32[3,260,128]{2,1,0:T(8,128)S(1)}, u32[]{:S(2)}, u32[]{:S(2)}) %collective-permute-start.5) | collective-permute-done | bytes 399392 | tf_op jit(solution)/shard_map/ppermute | solution.py:201
  105.5 0.0 copy-done.2
  105.5 0.0 copy-start.3
  105.5 0.8 copy-done.3
  106.3 4.2 %shard_map.96.state_ref = f32[3,624,128]{2,1,0:T(8,128)} custom-call(s32[2]{0:T(128)} %bitcast.19, f32[1248,128]{1,0:T(8,128)} %bitcast.13, f32[1248,128]{1,0:T(8,128)} %bitcast.15, f32[1248,128]{1,0:T(8,128)} %bitcast.17, f32[3,260,128]{2,1,0:T(8,128)} %copy-done.2, f32[3,260,128]{2,1,0:T(8,128)} %copy-done.3), custom_call_target="tpu_custom_call" | custom-call | flops 1000000 | bytes 4000000 | tf_op jit(solution)/shard_map/pallas_call | solution.py:152
  110.5 0.0 collective-permute-done.2.t0_ref
  110.5 0.0 copy-start.4
  110.5 0.0 collective-permute-done.3.t1_ref
  110.5 0.0 copy-done
  110.5 0.0 copy-done.1
  110.5 0.6 copy-done.4
  111.1 0.7 copy-done.5
  111.8 2.6 %shard_map.97 = (f32[624,128]{1,0:T(8,128)}, f32[624,128]{1,0:T(8,128)}, f32[624,128]{1,0:T(8,128)}) custom-call(f32[39,1024]{1,0:T(8,128)} %copy-done.1, f32[39,1024]{1,0:T(8,128)} %copy-done, f32[39,1024]{1,0:T(8,128)} %copy-done.4, f32[39,1024]{1,0:T(8,128)} %copy-done.5, f32[3,624,128]{2,1,0:T(8,128)} %shard_map.96.state_ref), custom_call_target="tpu_custom_call" | custom-call | flops 2000000 | bytes 3000000 | tf_op jit(solution)/shard_map/pallas_call | solution.py:186
  (5 shorter events, 0.1 us)
Async XLA Ops:
  75.2 6.3 %collective-permute-start.6 = (f32[23,2048]{1,0:T(8,128)S(1)}, f32[23,2048]{1,0:T(8,128)S(1)}, u32[]{:S(2)}, u32[]{:S(2)}) collective-permute-start(f32[23,2048]{1,0:T(8,128)S(1)} %slice.10), channel_id=1, source_target_pairs={{0,32},{32,64},{64,96},{96,128},{128,160},{160,192},{192,224},{224... | collective-permute-start | bytes 565256
  81.8 15.9 %collective-permute-start.1 = (f32[39,1024]{1,0:T(8,128)S(1)}, f32[39,1024]{1,0:T(8,128)S(1)}, u32[]{:S(2)}, u32[]{:S(2)}) collective-permute-start(f32[39,1024]{1,0:T(8,128)S(1)} %get-tuple-element.15), channel_id=1, source_target_pairs={{1,2},{2,1},{3,0},{0,3},{5,6},{6,5},{7,4},{4,7},{9,10},{10,9},{11,... | collective-permute-start | bytes 479240 | tf_op jit(solution)/shard_map/ppermute | solution.py:211
  86.2 11.5 %collective-permute-start = (f32[39,1024]{1,0:T(8,128)S(1)}, f32[39,1024]{1,0:T(8,128)S(1)}, u32[]{:S(2)}, u32[]{:S(2)}) collective-permute-start(f32[39,1024]{1,0:T(8,128)S(1)} %get-tuple-element.16), channel_id=1, source_target_pairs={{0,1},{1,0},{2,3},{3,2},{4,5},{5,4},{6,7},{7,6},{8,9},{9,8},{10,11... | collective-permute-start | bytes 479240 | tf_op jit(solution)/shard_map/ppermute | solution.py:210
  91.6 11.5 %collective-permute-start.4 = (f32[3,260,128]{2,1,0:T(8,128)}, f32[3,260,128]{2,1,0:T(8,128)S(1)}, u32[]{:S(2)}, u32[]{:S(2)}) collective-permute-start(f32[3,260,128]{2,1,0:T(8,128)} %get-tuple-element.8), channel_id=1, source_target_pairs={{0,32},{32,64},{64,96},{96,128},{128,160},{160,192},{192,224},{224... | collective-permute-start | bytes 1198088 | tf_op jit(solution)/shard_map/ppermute | solution.py:200
  95.8 9.7 %collective-permute-start.5 = (f32[3,260,128]{2,1,0:T(8,128)}, f32[3,260,128]{2,1,0:T(8,128)S(1)}, u32[]{:S(2)}, u32[]{:S(2)}) collective-permute-start(f32[3,260,128]{2,1,0:T(8,128)} %get-tuple-element.9), channel_id=1, source_target_pairs={{32,0},{64,32},{96,64},{128,96},{160,128},{192,160},{224,192},{256... | collective-permute-start | bytes 1198088 | tf_op jit(solution)/shard_map/ppermute | solution.py:201
  97.8 12.7 %copy-start = (f32[39,1024]{1,0:T(8,128)}, f32[39,1024]{1,0:T(8,128)S(1)}, u32[]{:S(2)}) copy-start(f32[39,1024]{1,0:T(8,128)S(1)} %get-tuple-element.13.s1_ref) | copy-start | bytes 479236
  97.8 12.7 %copy-start.1 = (f32[39,1024]{1,0:T(8,128)}, f32[39,1024]{1,0:T(8,128)S(1)}, u32[]{:S(2)}) copy-start(f32[39,1024]{1,0:T(8,128)S(1)} %get-tuple-element.14.s0_ref) | copy-start | bytes 479236
  97.8 12.7 %collective-permute-start.2 = (f32[39,1024]{1,0:T(8,128)S(1)}, f32[39,1024]{1,0:T(8,128)S(1)}, u32[]{:S(2)}, u32[]{:S(2)}) collective-permute-start(f32[39,1024]{1,0:T(8,128)S(1)} %get-tuple-element.14.s0_ref), channel_id=1, source_target_pairs={{1,2},{2,1},{3,0},{0,3},{5,6},{6,5},{7,4},{4,7},{9,10},{10,9},{11,... | collective-permute-start | bytes 479240 | tf_op jit(solution)/shard_map/ppermute | solution.py:212
  100.6 9.9 %collective-permute-start.3 = (f32[39,1024]{1,0:T(8,128)S(1)}, f32[39,1024]{1,0:T(8,128)S(1)}, u32[]{:S(2)}, u32[]{:S(2)}) collective-permute-start(f32[39,1024]{1,0:T(8,128)S(1)} %get-tuple-element.13.s1_ref), channel_id=1, source_target_pairs={{0,1},{1,0},{2,3},{3,2},{4,5},{5,4},{6,7},{7,6},{8,9},{9,8},{10,11... | collective-permute-start | bytes 479240 | tf_op jit(solution)/shard_map/ppermute | solution.py:213
  103.2 2.3 %copy-start.2 = (f32[3,260,128]{2,1,0:T(8,128)}, f32[3,260,128]{2,1,0:T(8,128)S(1)}, u32[]{:S(2)}) copy-start(f32[3,260,128]{2,1,0:T(8,128)S(1)} %collective-permute-done.4.left_ref) | copy-start | bytes 1198084
  105.5 0.8 copy-start.3
  110.5 0.7 copy-start.4
  111.1 0.7 copy-start.5

commit v2 on v1

v2 whole, which is shorter than its diff:
```python
import functools

import jax
import jax.numpy as jnp
import numpy as np
from jax import lax
from jax.experimental import pallas as pl
from jax.experimental.pallas import tpu as pltpu
from jax.sharding import PartitionSpec as P

ADAM_STEP = 1000
BETA_ONE = 0.9
BETA_TWO = 0.95
LEARN_RATE = 0.001
DECAY_RATE = 0.1
EPSILON = 1e-08

SHARDS = 24
COLS = 6656
BROWS = 256
LANES = 128
P_SIZE = 79872
HALF = 33280
CAP = 159744
ROWS = P_SIZE // LANES
HROWS = HALF // LANES
CROWS = CAP // LANES
FRONT = 264
SROWS = 39
SCOLS = 2048
STEP_COLS = 512
GROWS = P_SIZE // COLS


def row_class(row):
    return min(row % SROWS // GROWS, 3)


TOTAL = SHARDS * SROWS
TILES_OF = [sorted({row // 8 for row in range(TOTAL) if row_class(row) == c}) for c in range(4)]
PART_ROWS = [(8 * len(tiles) + 15) // 16 * 16 for tiles in TILES_OF]
PART_AT = [sum(PART_ROWS[:c]) for c in range(4)]
PICK_ROWS = sum(PART_ROWS) + 3 * PART_ROWS[3]


def row_picks():
    picks = np.zeros((PICK_ROWS, BROWS), np.float32)
    for c in range(4):
        for i, tile in enumerate(TILES_OF[c]):
            for row in range(8 * tile, 8 * tile + 8):
                if row_class(row) != c:
                    continue
                shard, inner = row // SROWS, row % SROWS
                at = PART_AT[c] + 8 * i + row % 8
                for step in range(4 if c == 3 else 1):
                    token_col = GROWS * shard + (4 * (inner - 36) + step if c == 3 else inner - GROWS * c)
                    if token_col < BROWS:
                        picks[at + step * PART_ROWS[3], token_col] = 1
    return picks.astype(jnp.bfloat16)


def grad_kernel(count_ref, tok_ref, pick_ref, c0_ref, c1_ref, c2_ref, c3_ref, out_ref, lhs_ref, part_ref):
    step = pl.program_id(0)

    @pl.when(step == 0)
    def _():
        tok_row = lax.broadcasted_iota(jnp.int32, (BROWS, BROWS), 0)
        tok = jnp.where(tok_row < count_ref[0], tok_ref[...], jnp.zeros_like(tok_ref))
        lhs_ref[...] = lax.dot_general(
            pick_ref[...], tok, (((1,), (1,)), ((), ())), preferred_element_type=jnp.float32
        ).astype(jnp.bfloat16)

    for c, cot in enumerate((c0_ref, c1_ref, c2_ref, c3_ref)):
        start = PART_AT[c] if c < 3 else pl.multiple_of(PART_AT[3] + step * PART_ROWS[3], 16)
        lhs = lhs_ref[pl.ds(start, PART_ROWS[c]), :]
        part_ref[pl.ds(PART_AT[c], PART_ROWS[c]), :] = jnp.dot(
            lhs, cot[...], preferred_element_type=jnp.float32
        )
    for tile in range(TOTAL // 8):
        found = [PART_AT[c] + 8 * TILES_OF[c].index(tile) for c in range(4) if tile in TILES_OF[c]]
        out_ref[8 * tile : 8 * tile + 8, :] = sum(part_ref[at : at + 8, :] for at in found)


def local_gradient(tokens, cotangent, count):
    block = (BROWS, STEP_COLS)
    return pl.pallas_call(
        grad_kernel,
        grid=(4,),
        in_specs=[
            pl.BlockSpec(memory_space=pltpu.SMEM),
            pl.BlockSpec((BROWS, BROWS), lambda k: (0, 0)),
            pl.BlockSpec((PICK_ROWS, BROWS), lambda k: (0, 0)),
            pl.BlockSpec(block, lambda k: (0, k)),
            pl.BlockSpec(block, lambda k: (0, 4 + k)),
            pl.BlockSpec(block, lambda k: (0, 8 + k)),
            pl.BlockSpec(block, lambda k: (0, 12)),
        ],
        out_specs=pl.BlockSpec((TOTAL, STEP_COLS), lambda k: (0, k)),
        out_shape=jax.ShapeDtypeStruct((TOTAL, SCOLS), jnp.float32),
        scratch_shapes=[
            pltpu.VMEM((PICK_ROWS, BROWS), jnp.bfloat16),
            pltpu.VMEM((sum(PART_ROWS), STEP_COLS), jnp.float32),
        ],
        compiler_params=pltpu.CompilerParams(vmem_limit_bytes=56 * 1024 * 1024),
        cost_estimate=pl.CostEstimate(flops=2 * 10**9, bytes_accessed=12 * 10**6, transcendentals=0),
    )(count, tokens, jnp.asarray(row_picks()), cotangent, cotangent, cotangent, cotangent)


def shifted(ref, start, rows):
    start = start + FRONT * LANES
    top = lax.shift_right_logical(start, 7)
    lane_start = start - top * LANES
    first = pltpu.roll(ref[pl.ds(top, rows), :], LANES - lane_start, 1)
    second = pltpu.roll(ref[pl.ds(top + 1, rows), :], LANES - lane_start, 1)
    lane = lax.broadcasted_iota(jnp.int32, (rows, LANES), 1)
    return jnp.where(lane < LANES - lane_start, first, second)


def load_old(refs, buf, sem):
    copies = [pltpu.make_async_copy(r, buf.at[i, pl.ds(FRONT, CROWS)], sem.at[i]) for i, r in enumerate(refs)]
    for c in copies:
        c.start()
    for i in range(3):
        buf[i, :FRONT, :] = jnp.zeros((FRONT, LANES), jnp.float32)
        buf[i, FRONT + CROWS :, :] = jnp.zeros((8, LANES), jnp.float32)
    for c in copies:
        c.wait()


def window_kernel(bounds_ref, a_ref, b_ref, c_ref, inner_ref, outer_ref, own_ref, buf, sem):
    load_old((a_ref, b_ref, c_ref), buf, sem)
    dp = lax.axis_index("dp")
    core = lax.bitwise_and(dp, 1)
    ahead = dp * P_SIZE - bounds_ref[0]
    to_right, to_left = ahead + P_SIZE, jnp.maximum(ahead, 0) - HALF
    for i in range(3):
        inner_ref[i] = shifted(buf.at[i], jnp.where(core == 0, to_right, to_left), HROWS)
        outer_ref[i] = shifted(buf.at[i], jnp.where(core == 0, to_left, to_right), HROWS)
        own_ref[i] = shifted(buf.at[i], ahead, ROWS)


OLD_SCRATCH = (
    pltpu.VMEM((3, FRONT + CROWS + 8, LANES), jnp.float32),
    pltpu.SemaphoreType.DMA((3,)),
)
SMEM_SPEC = pl.BlockSpec(memory_space=pltpu.SMEM)
ANY_SPEC = pl.BlockSpec(memory_space=pl.ANY)
VMEM_SPEC = pl.BlockSpec(memory_space=pltpu.VMEM)


def windows(bounds, old):
    halo = jax.ShapeDtypeStruct((3, HROWS, LANES), jnp.float32)
    own = jax.ShapeDtypeStruct((3, ROWS, LANES), jnp.float32)
    return pl.pallas_call(
        window_kernel,
        in_specs=[SMEM_SPEC, ANY_SPEC, ANY_SPEC, ANY_SPEC],
        out_specs=(VMEM_SPEC,) * 3,
        out_shape=(halo, halo, own),
        scratch_shapes=list(OLD_SCRATCH),
        cost_estimate=pl.CostEstimate(flops=10**6, bytes_accessed=16 * 10**6, transcendentals=0),
    )(bounds, *old)


def adam_kernel(
    bounds_ref, s_ref, t_ref, own_ref, inner_ref, outer_ref, master_ref, first_ref, second_ref, grad, state
):
    row = lax.broadcasted_iota(jnp.int32, (ROWS, LANES), 0)
    lane = lax.broadcasted_iota(jnp.int32, (ROWS, LANES), 1)
    pos = lax.axis_index("dp") * P_SIZE + row * LANES + lane
    tail = ROWS - HROWS
    first_core = lax.bitwise_and(lax.axis_index("dp"), 1) == 0
    below, above = pos[:HROWS] < bounds_ref[0], pos[tail:] >= bounds_ref[1]
    for i in range(3):
        left = jnp.where(first_core, outer_ref[i], inner_ref[i])
        right = jnp.where(first_core, inner_ref[i], outer_ref[i])
        state[i, :HROWS, :] = jnp.where(below, left, own_ref[i, :HROWS, :])
        state[i, HROWS:tail, :] = own_ref[i, HROWS:tail, :]
        state[i, tail:, :] = jnp.where(above, right, own_ref[i, tail:, :])
    tiles = COLS // LANES
    for at in range(16):
        cols = slice(LANES * at, LANES * (at + 1))
        piece = s_ref[:, cols] + t_ref[:, cols]
        for q in range(3):
            grad[pl.ds(16 * q + at, GROWS, stride=tiles), :] = piece[GROWS * q : GROWS * (q + 1)]
        k, c = at // 4, at % 4
        grad[pl.ds(tiles * k + 48 + c, 3, stride=4 * tiles), :] = piece[36:39]
    corr_one = 1.0 - BETA_ONE**ADAM_STEP
    corr_two = 1.0 - BETA_TWO**ADAM_STEP
    g = grad[...]
    first_new = BETA_ONE * state[0] + (1.0 - BETA_ONE) * g
    second_new = BETA_TWO * state[1] + (1.0 - BETA_TWO) * g * g
    master = state[2]
    update = first_new / corr_one / (jnp.sqrt(second_new / corr_two) + EPSILON) + DECAY_RATE * master
    master_ref[...] = master - LEARN_RATE * update
    first_ref[...] = first_new
    second_ref[...] = second_new


def adam_step(bounds, parts, own, left, right):
    shape = jax.ShapeDtypeStruct((ROWS, LANES), jnp.float32)
    return pl.pallas_call(
        adam_kernel,
        in_specs=[SMEM_SPEC] + [VMEM_SPEC] * 5,
        out_specs=(VMEM_SPEC,) * 3,
        out_shape=(shape,) * 3,
        scratch_shapes=[
            pltpu.VMEM((ROWS, LANES), jnp.float32),
            pltpu.VMEM((3, ROWS, LANES), jnp.float32),
        ],
        cost_estimate=pl.CostEstimate(flops=2 * 10**6, bytes_accessed=3 * 10**6, transcendentals=10**5),
    )(bounds, *parts, own, left, right)


def rep_pairs(move0, move1):
    return [(4 * d + r, 4 * d + (move1 if d % 2 else move0)(r)) for d in range(SHARDS) for r in range(4)]


def local(tokens, cotangent, token_counts, old_bounds, old_first, old_second, old_master):
    bounds = old_bounds.reshape(2)
    old = [a.reshape(CROWS, LANES) for a in (old_first, old_second, old_master)]
    inner, outer, own = windows(bounds, old)
    inner = lax.ppermute(inner, "dp", [(i, i ^ 1) for i in range(SHARDS)])
    outer = lax.ppermute(outer, "dp", [(i, i + 1 if i % 2 else i - 1) for i in range(1, SHARDS - 1)])
    partial = local_gradient(tokens, cotangent, token_counts.reshape(1))
    shard = lax.psum_scatter(partial, "dp", scatter_dimension=0, tiled=True)
    shard = lax.optimization_barrier(shard)
    one, three = (lambda r: r ^ 1), (lambda r: r ^ 3)
    half = shard + lax.ppermute(shard, ("dp", "rep"), rep_pairs(one, three))
    rest = lax.ppermute(half, ("dp", "rep"), rep_pairs(three, one))
    outs = adam_step(bounds, (half, rest), own, inner, outer)
    return tuple(a.reshape(1, P_SIZE) for a in outs)


def solution(mesh):
    placed = (
        P(("dp", "rep"), None),
        P(("dp", "rep"), "mp"),
        P("dp", "rep"),
        P("mp", "dp", None),
        P("mp", "dp"),
        P("mp", "dp"),
        P("mp", "dp"),
    )
    return jax.shard_map(
        local,
        mesh=mesh,
        in_specs=placed,
        out_specs=(P("mp", "dp"), P("mp", "dp"), P("mp", "dp")),
        check_vma=False,
    )
```

time: 115 us -> 105 us (0.913)
  the two profiles are of different devices: /device:TPU:1 before, /device:TPU:56 now
where the time goes in v2:
time: 105 us; the launch traced here: 104 us
  blocking collectives  66.9 us (64%)
  Pallas kernels  14.7 us (14%)
  starting transfers between devices  11.3 us (11%)
  waiting for transfers between devices  6.57 us (6%)
  local copies, waits for them, and re-layouts  2.28 us (2%)
  between operations  2.07 us (2%)
    unnamed x1, blocking collectives  66.9 us
    pallas_call x1, Pallas kernels, local_gradient(): pl.pallas_call(grad_kernel, grid=(4,), in_specs=[pl.BlockSpec(memory_spac...  7.53 us
    ppermute x1, waiting for transfers between devices, local(): rest = lax.ppermute(half, ('dp', 'rep'), rep_pairs(three, one))  6.56 us
    pallas_call x1, Pallas kernels, windows(): pl.pallas_call(window_kernel, in_specs=[SMEM_SPEC, ANY_SPEC, ANY_SPEC, AN...  4.16 us
    ppermute x1, starting transfers between devices, local(): rest = lax.ppermute(half, ('dp', 'rep'), rep_pairs(three, one))  3.57 us
    ppermute x1, starting transfers between devices, local(): half = shard + lax.ppermute(shard, ('dp', 'rep'), rep_pairs(one, three))  3.41 us
    pallas_call x1, Pallas kernels, adam_step(): pl.pallas_call(adam_kernel, in_specs=[SMEM_SPEC] + [VMEM_SPEC] * 5, out_s...  3.02 us
    ppermute x1, starting transfers between devices, local(): inner = lax.ppermute(inner, 'dp', [(i, i ^ 1) for i in range(SHARDS)])  2.36 us
  transfers between devices with their start and end apart: 5, of which 1 were waited for; matrix products, arithmetic and copies ran while one was open for 1% of the time, Pallas kernels for 4%

profile of v2, /device:TPU:56, one launch (start us, length us, event | category | flops | bytes accessed | tf_op | source)
XLA Modules:
  0.0 103.9 jit_solution(12311122674294058486)
XLA Ops:
  1.3 7.5 %shard_map.103 = f32[936,2048]{1,0:T(8,128)} custom-call(s32[1]{0:T(128)} %bitcast.11.count_ref, bf16[256,256]{1,0:T(8,128)(2,1)} %tok_ref.1, bf16[2352,256]{1,0:T(8,128)(2,1)} %constant.2.clone.pick_ref, bf16[256,6656]{1,0:T(8,128)(2,1)} %c3_ref.1, bf16[256,6656]{1,0:T(8,128)(2,1)} %c3_ref.1, bf16[256,6656]{1,0:T(8,128)(2,1)} %c3_ref.1, ...), custom_call_target="tpu_custom_call" | custom-call | flops 2000000000 | bytes 12000000 | tf_op jit(solution)/shard_map/pallas_call | solution.py:86
  8.8 66.9 %fusion = f32[40,2048]{1,0:T(8,128)S(1)} fusion(f32[936,2048]{1,0:T(8,128)} %shard_map.103), kind=kCustom, calls=%all-reduce-scatter | all-reduce-scatter fusion | flops 1966081 | bytes 7999488
  75.8 1.3 %collective-permute-start.4 = (f32[23,2048]{1,0:T(8,128)S(1)}, f32[23,2048]{1,0:T(8,128)S(1)}, u32[]{:S(2)}, u32[]{:S(2)}) collective-permute-start(f32[23,2048]{1,0:T(8,128)S(1)} %slice), channel_id=1, source_target_pairs={{0,32},{32,64},{64,96},{96,128},{128,160},{160,192},{192,224},{224... | collective-permute-start | bytes 565256
  77.1 1.3 %dynamic-slice.4 = u32[1]{0:T(128)} dynamic-slice(u32[768]{0:T(1024)} %constant.12, u32[]{:S(6)} %partition-id.4), dynamic_slice_sizes={1} | dynamic-slice | bytes 12
  79.0 0.0 collective-permute-done.4
  79.0 0.2 concatenate
  79.3 3.4 %collective-permute-start = (f32[39,2048]{1,0:T(8,128)S(1)}, f32[39,2048]{1,0:T(8,128)S(1)}, u32[]{:S(2)}, u32[]{:S(2)}) collective-permute-start(f32[39,2048]{1,0:T(8,128)S(1)} %constant_dynamic-slice_fusion), channel_id=1, source_target_pairs={{0,1},{1,0},{2,3},{3,2},{32,35},{33,34},{34,33},{35,32},{64,65},{6... | collective-permute-start | bytes 958472 | tf_op jit(solution)/shard_map/ppermute | solution.py:228
  82.7 4.2 %shard_map.104 = (f32[3,260,128]{2,1,0:T(8,128)}, f32[3,260,128]{2,1,0:T(8,128)}, f32[3,624,128]{2,1,0:T(8,128)}) custom-call(s32[2]{0:T(128)} %bitcast.15, f32[1248,128]{1,0:T(8,128)} %bitcast.12, f32[1248,128]{1,0:T(8,128)} %bitcast.13, f32[1248,128]{1,0:T(8,128)} %bitcast.14), custom_call_target="tpu_custom_call" | custom-call | flops 1000000 | bytes 16000000 | tf_op jit(solution)/shard_map/pallas_call | solution.py:154
  86.9 2.4 %collective-permute-start.2 = (f32[3,260,128]{2,1,0:T(8,128)}, f32[3,260,128]{2,1,0:T(8,128)S(1)}, u32[]{:S(2)}, u32[]{:S(2)}) collective-permute-start(f32[3,260,128]{2,1,0:T(8,128)} %get-tuple-element.10), channel_id=1, source_target_pairs={{0,32},{32,0},{64,96},{96,64},{128,160},{160,128},{192,224},{224,1... | collective-permute-start | bytes 1198088 | tf_op jit(solution)/shard_map/ppermute | solution.py:222
  89.3 0.7 collective-permute-start.3
  90.0 0.0 collective-permute-done
  90.0 0.0 copy-start
  90.0 3.6 %collective-permute-start.1 = (f32[39,2048]{1,0:T(8,128)S(1)}, f32[39,2048]{1,0:T(8,128)S(1)}, u32[]{:S(2)}, u32[]{:S(2)}) collective-permute-start(f32[39,2048]{1,0:T(8,128)S(1)} %add.5.s_ref), channel_id=1, source_target_pairs={{0,3},{1,2},{2,1},{3,0},{32,33},{33,32},{34,35},{35,34},{64,67},{6... | collective-permute-start | bytes 958472 | tf_op jit(solution)/shard_map/ppermute | solution.py:229
  93.6 0.0 collective-permute-done.2.inner_ref
  93.6 0.0 copy-start.1
  93.6 0.0 collective-permute-done.3.outer_ref
  93.6 0.0 copy-start.2
  93.6 6.6 %collective-permute-done.1.t_ref = f32[39,2048]{1,0:T(8,128)S(1)} collective-permute-done((f32[39,2048]{1,0:T(8,128)S(1)}, f32[39,2048]{1,0:T(8,128)S(1)}, u32[]{:S(2)}, u32[]{:S(2)}) %collective-permute-start.1) | collective-permute-done | bytes 319520 | tf_op jit(solution)/shard_map/ppermute | solution.py:229
  100.2 0.0 copy-start.3
  100.2 0.0 copy-done
  100.2 0.0 copy-done.1
  100.2 0.0 copy-done.2
  100.2 0.7 copy-done.3
  100.9 3.0 %shard_map.105 = (f32[624,128]{1,0:T(8,128)}, f32[624,128]{1,0:T(8,128)}, f32[624,128]{1,0:T(8,128)}) custom-call(s32[2]{0:T(128)} %bitcast.16, f32[39,2048]{1,0:T(8,128)} %copy-done, f32[39,2048]{1,0:T(8,128)} %copy-done.3, f32[3,624,128]{2,1,0:T(8,128)} %get-tuple-element.9.own_ref, f32[3,260,128]{2,1,0:T(8,128)} %copy-done.1, f32[3,260,128]{2,1,0:T(8,128)} %copy-done.2), custom_call_target="tpu_custom_call" | custom-call | flops 2000000 | bytes 3000000 | tf_op jit(solution)/shard_map/pallas_call | solution.py:201
  (3 shorter events, 0.1 us)
Async XLA Ops:
  75.8 3.2 %collective-permute-start.4 = (f32[23,2048]{1,0:T(8,128)S(1)}, f32[23,2048]{1,0:T(8,128)S(1)}, u32[]{:S(2)}, u32[]{:S(2)}) collective-permute-start(f32[23,2048]{1,0:T(8,128)S(1)} %slice), channel_id=1, source_target_pairs={{0,32},{32,64},{64,96},{96,128},{128,160},{160,192},{192,224},{224... | collective-permute-start | bytes 565256
  79.3 10.6 %collective-permute-start = (f32[39,2048]{1,0:T(8,128)S(1)}, f32[39,2048]{1,0:T(8,128)S(1)}, u32[]{:S(2)}, u32[]{:S(2)}) collective-permute-start(f32[39,2048]{1,0:T(8,128)S(1)} %constant_dynamic-slice_fusion), channel_id=1, source_target_pairs={{0,1},{1,0},{2,3},{3,2},{32,35},{33,34},{34,33},{35,32},{64,65},{6... | collective-permute-start | bytes 958472 | tf_op jit(solution)/shard_map/ppermute | solution.py:228
  86.9 6.7 %collective-permute-start.2 = (f32[3,260,128]{2,1,0:T(8,128)}, f32[3,260,128]{2,1,0:T(8,128)S(1)}, u32[]{:S(2)}, u32[]{:S(2)}) collective-permute-start(f32[3,260,128]{2,1,0:T(8,128)} %get-tuple-element.10), channel_id=1, source_target_pairs={{0,32},{32,0},{64,96},{96,64},{128,160},{160,128},{192,224},{224,1... | collective-permute-start | bytes 1198088 | tf_op jit(solution)/shard_map/ppermute | solution.py:222
  89.3 4.4 %collective-permute-start.3 = (f32[3,260,128]{2,1,0:T(8,128)}, f32[3,260,128]{2,1,0:T(8,128)S(1)}, u32[]{:S(2)}, u32[]{:S(2)}) collective-permute-start(f32[3,260,128]{2,1,0:T(8,128)} %get-tuple-element.11), channel_id=1, source_target_pairs={{32,64},{64,32},{96,128},{128,96},{160,192},{192,160},{224,256},{2... | collective-permute-start | bytes 1198088 | tf_op jit(solution)/shard_map/ppermute | solution.py:223
  90.0 10.2 %copy-start = (f32[39,2048]{1,0:T(8,128)}, f32[39,2048]{1,0:T(8,128)S(1)}, u32[]{:S(2)}) copy-start(f32[39,2048]{1,0:T(8,128)S(1)} %add.5.s_ref) | copy-start | bytes 958468
  90.0 10.2 %collective-permute-start.1 = (f32[39,2048]{1,0:T(8,128)S(1)}, f32[39,2048]{1,0:T(8,128)S(1)}, u32[]{:S(2)}, u32[]{:S(2)}) collective-permute-start(f32[39,2048]{1,0:T(8,128)S(1)} %add.5.s_ref), channel_id=1, source_target_pairs={{0,3},{1,2},{2,1},{3,0},{32,33},{33,32},{34,35},{35,34},{64,67},{6... | collective-permute-start | bytes 958472 | tf_op jit(solution)/shard_map/ppermute | solution.py:229
  93.6 6.6 %copy-start.1 = (f32[3,260,128]{2,1,0:T(8,128)}, f32[3,260,128]{2,1,0:T(8,128)S(1)}, u32[]{:S(2)}) copy-start(f32[3,260,128]{2,1,0:T(8,128)S(1)} %collective-permute-done.2.inner_ref) | copy-start | bytes 1198084
  93.6 6.6 %copy-start.2 = (f32[3,260,128]{2,1,0:T(8,128)}, f32[3,260,128]{2,1,0:T(8,128)S(1)}, u32[]{:S(2)}) copy-start(f32[3,260,128]{2,1,0:T(8,128)S(1)} %collective-permute-done.3.outer_ref) | copy-start | bytes 1198084
  100.2 0.7 copy-start.3

commit v3 on v2

--- a/solution.py
+++ b/solution.py
@@ -107,7 +107,6 @@
 
 
 def shifted(ref, start, rows):
-    start = start + FRONT * LANES
     top = lax.shift_right_logical(start, 7)
     lane_start = start - top * LANES
     first = pltpu.roll(ref[pl.ds(top, rows), :], LANES - lane_start, 1)
@@ -116,48 +115,89 @@
     return jnp.where(lane < LANES - lane_start, first, second)
 
 
-def load_old(refs, buf, sem):
-    copies = [pltpu.make_async_copy(r, buf.at[i, pl.ds(FRONT, CROWS)], sem.at[i]) for i, r in enumerate(refs)]
-    for c in copies:
-        c.start()
-    for i in range(3):
-        buf[i, :FRONT, :] = jnp.zeros((FRONT, LANES), jnp.float32)
-        buf[i, FRONT + CROWS :, :] = jnp.zeros((8, LANES), jnp.float32)
-    for c in copies:
-        c.wait()
-
-
-def window_kernel(bounds_ref, a_ref, b_ref, c_ref, inner_ref, outer_ref, own_ref, buf, sem):
-    load_old((a_ref, b_ref, c_ref), buf, sem)
+HALO_LOAD = HROWS + 12
+OWN_LOAD = ROWS + 8
+
+
+def tile_row(start):
+    return pl.multiple_of(lax.shift_left(lax.shift_right_arithmetic(start, 10), 3), 8)
+
+
+def halo_kernel(bounds_ref, a_ref, b_ref, c_ref, inner_ref, outer_ref, ahead_buf, behind_buf, sem):
     dp = lax.axis_index("dp")
     core = lax.bitwise_and(dp, 1)
     ahead = dp * P_SIZE - bounds_ref[0]
     to_right, to_left = ahead + P_SIZE, jnp.maximum(ahead, 0) - HALF
-    for i in range(3):
-        inner_ref[i] = shifted(buf.at[i], jnp.where(core == 0, to_right, to_left), HROWS)
-        outer_ref[i] = shifted(buf.at[i], jnp.where(core == 0, to_left, to_right), HROWS)
-        own_ref[i] = shifted(buf.at[i], ahead, ROWS)
-
-
-OLD_SCRATCH = (
-    pltpu.VMEM((3, FRONT + CROWS + 8, LANES), jnp.float32),
-    pltpu.SemaphoreType.DMA((3,)),
-)
+    right_row = tile_row(to_right)
+    copies = []
+    for i, old in enumerate((a_ref, b_ref, c_ref)):
+        copies.append(
+            pltpu.make_async_copy(old.at[pl.ds(right_row, HALO_LOAD)], ahead_buf.at[i, pl.ds(0, HALO_LOAD)], sem.at[2 * i])
+        )
+        copies.append(
+            pltpu.make_async_copy(old.at[pl.ds(0, HALO_LOAD)], behind_buf.at[i, pl.ds(FRONT, HALO_LOAD)], sem.at[2 * i + 1])
+        )
+    for copy in copies:
+        copy.start()
+    for i in range(3):
+        behind_buf[i, :FRONT, :] = jnp.zeros((FRONT, LANES), jnp.float32)
+    for i in range(3):
+        copies[2 * i].wait()
+        right = shifted(ahead_buf.at[i], to_right - right_row * LANES, HROWS)
+        copies[2 * i + 1].wait()
+        left = shifted(behind_buf.at[i], to_left + FRONT * LANES, HROWS)
+        inner_ref[i] = jnp.where(core == 0, right, left)
+        outer_ref[i] = jnp.where(core == 0, left, right)
+
+
+def own_kernel(bounds_ref, a_ref, b_ref, c_ref, own_ref, buf, sem):
+    ahead = lax.axis_index("dp") * P_SIZE - bounds_ref[0]
+    row = jnp.maximum(tile_row(ahead), 0)
+    copies = []
+    for i, old in enumerate((a_ref, b_ref, c_ref)):
+        copies.append(
+            pltpu.make_async_copy(old.at[pl.ds(pl.multiple_of(row, 8), OWN_LOAD)], buf.at[i, pl.ds(FRONT, OWN_LOAD)], sem.at[i])
+        )
+    for copy in copies:
+        copy.start()
+    for i in range(3):
+        copies[i].wait()
+        own_ref[i] = shifted(buf.at[i], ahead - row * LANES + FRONT * LANES, ROWS)
+
+
+SEMS = pltpu.SemaphoreType.DMA((6,))
 SMEM_SPEC = pl.BlockSpec(memory_space=pltpu.SMEM)
+SMALL = pltpu.CompilerParams(vmem_limit_bytes=12 * 1024 * 1024)
 ANY_SPEC = pl.BlockSpec(memory_space=pl.ANY)
 VMEM_SPEC = pl.BlockSpec(memory_space=pltpu.VMEM)
 
 
-def windows(bounds, old):
+def halos(bounds, old):
     halo = jax.ShapeDtypeStruct((3, HROWS, LANES), jnp.float32)
-    own = jax.ShapeDtypeStruct((3, ROWS, LANES), jnp.float32)
-    return pl.pallas_call(
-        window_kernel,
+    return pl.pallas_call(
+        halo_kernel,
         in_specs=[SMEM_SPEC, ANY_SPEC, ANY_SPEC, ANY_SPEC],
-        out_specs=(VMEM_SPEC,) * 3,
-        out_shape=(halo, halo, own),
-        scratch_shapes=list(OLD_SCRATCH),
-        cost_estimate=pl.CostEstimate(flops=10**6, bytes_accessed=16 * 10**6, transcendentals=0),
+        out_specs=(VMEM_SPEC,) * 2,
+        out_shape=(halo, halo),
+        scratch_shapes=[
+            pltpu.VMEM((3, HALO_LOAD + 8, LANES), jnp.float32),
+            pltpu.VMEM((3, FRONT + HALO_LOAD, LANES), jnp.float32),
+            SEMS,
+        ],
+        compiler_params=SMALL,
+        cost_estimate=pl.CostEstimate(flops=10**6, bytes_accessed=8 * 10**6, transcendentals=0),
+    )(bounds, *old)
+
+
+def own_window(bounds, old):
+    return pl.pallas_call(
+        own_kernel,
+        in_specs=[SMEM_SPEC, ANY_SPEC, ANY_SPEC, ANY_SPEC],
+        out_specs=VMEM_SPEC,
+        out_shape=jax.ShapeDtypeStruct((3, ROWS, LANES), jnp.float32),
+        scratch_shapes=[pltpu.VMEM((3, FRONT + OWN_LOAD + 8, LANES), jnp.float32), SEMS],
+        compiler_params=SMALL,
+        cost_estimate=pl.CostEstimate(flops=10**6, bytes_accessed=10 * 10**6, transcendentals=0),
     )(bounds, *old)
 
 
@@ -207,6 +247,7 @@
             pltpu.VMEM((ROWS, LANES), jnp.float32),
             pltpu.VMEM((3, ROWS, LANES), jnp.float32),
         ],
+        compiler_params=SMALL,
         cost_estimate=pl.CostEstimate(flops=2 * 10**6, bytes_accessed=3 * 10**6, transcendentals=10**5),
     )(bounds, *parts, own, left, right)
 
@@ -218,7 +259,8 @@
 def local(tokens, cotangent, token_counts, old_bounds, old_first, old_second, old_master):
     bounds = old_bounds.reshape(2)
     old = [a.reshape(CROWS, LANES) for a in (old_first, old_second, old_master)]
-    inner, outer, own = windows(bounds, old)
+    inner, outer = halos(bounds, old)
+    own = own_window(bounds, old)
     inner = lax.ppermute(inner, "dp", [(i, i ^ 1) for i in range(SHARDS)])
     outer = lax.ppermute(outer, "dp", [(i, i + 1 if i % 2 else i - 1) for i in range(1, SHARDS - 1)])
     partial = local_gradient(tokens, cotangent, token_counts.reshape(1))

time: 105 us -> 102 us (0.971)
  waiting for transfers between devices: 6.57 us -> 4 us
    ppermute x1, waiting for transfers between devices: 6.56 us -> 3.99 us  [local(): rest = lax.ppermute(half, ('dp', 'rep'), rep_pairs(three, one))]
    pallas_call x1 -> x2, Pallas kernels: 4.16 us -> 4.15 us  [the longest x1 2.55 us: halos(): pl.pallas_call(halo_kernel, in_specs=[SMEM_SPEC, ANY_SPEC, ANY_SPEC, ANY_...]
where the time goes in v3:
time: 102 us; the launch traced here: 101 us
  blocking collectives  67.1 us (66%)
  Pallas kernels  13.7 us (13%)
  starting transfers between devices  12.3 us (12%)
  waiting for transfers between devices  4 us (4%)
  between operations  2.1 us (2%)
  local copies, waits for them, and re-layouts  1.58 us (2%)
    unnamed x1, blocking collectives  67.1 us
    pallas_call x1, Pallas kernels, local_gradient(): pl.pallas_call(grad_kernel, grid=(4,), in_specs=[pl.BlockSpec(memory_spac...  7.53 us
    ppermute x1, starting transfers between devices, local(): rest = lax.ppermute(half, ('dp', 'rep'), rep_pairs(three, one))  4.55 us
    ppermute x1, waiting for transfers between devices, local(): rest = lax.ppermute(half, ('dp', 'rep'), rep_pairs(three, one))  3.99 us
    ppermute x1, starting transfers between devices, local(): half = shard + lax.ppermute(shard, ('dp', 'rep'), rep_pairs(one, three))  3.41 us
    pallas_call x1, Pallas kernels, halos(): pl.pallas_call(halo_kernel, in_specs=[SMEM_SPEC, ANY_SPEC, ANY_SPEC, ANY_...  2.55 us
    ppermute x1, starting transfers between devices, local(): inner = lax.ppermute(inner, 'dp', [(i, i ^ 1) for i in range(SHARDS)])  2.36 us
  transfers between devices with their start and end apart: 5, of which 1 were waited for; matrix products, arithmetic and copies ran while one was open for 1% of the time, Pallas kernels for 4%

profile of v3, /device:TPU:56, one launch (start us, length us, event | category | flops | bytes accessed | tf_op | source)
XLA Modules:
  0.0 100.8 jit_solution(2366390593196431804)
XLA Ops:
  1.3 7.5 %shard_map.103 = f32[936,2048]{1,0:T(8,128)} custom-call(s32[1]{0:T(128)} %bitcast.11.count_ref, bf16[256,256]{1,0:T(8,128)(2,1)} %tok_ref.1, bf16[2352,256]{1,0:T(8,128)(2,1)} %constant.2.clone.pick_ref, bf16[256,6656]{1,0:T(8,128)(2,1)} %c3_ref.1, bf16[256,6656]{1,0:T(8,128)(2,1)} %c3_ref.1, bf16[256,6656]{1,0:T(8,128)(2,1)} %c3_ref.1, ...), custom_call_target="tpu_custom_call" | custom-call | flops 2000000000 | bytes 12000000 | tf_op jit(solution)/shard_map/pallas_call | solution.py:86
  8.8 0.0 copy-start
  8.8 0.0 copy-start.1
  8.8 0.0 copy-start.2
  8.8 0.0 copy-start.3
  8.8 67.1 %fusion = f32[40,2048]{1,0:T(8,128)S(1)} fusion(f32[936,2048]{1,0:T(8,128)} %shard_map.103), kind=kCustom, calls=%all-reduce-scatter | all-reduce-scatter fusion | flops 1966081 | bytes 7999488
  76.0 1.3 %collective-permute-start.4 = (f32[23,2048]{1,0:T(8,128)S(1)}, f32[23,2048]{1,0:T(8,128)S(1)}, u32[]{:S(2)}, u32[]{:S(2)}) collective-permute-start(f32[23,2048]{1,0:T(8,128)S(1)} %slice), channel_id=1, source_target_pairs={{0,32},{32,64},{64,96},{96,128},{128,160},{160,192},{192,224},{224... | collective-permute-start | bytes 565256
  77.3 1.3 %dynamic-slice.4 = u32[1]{0:T(128)} dynamic-slice(u32[768]{0:T(1024)} %constant.12, u32[]{:S(6)} %partition-id.4), dynamic_slice_sizes={1} | dynamic-slice | bytes 12
  79.2 0.0 collective-permute-done.4
  79.2 0.2 concatenate
  79.5 3.4 %collective-permute-start = (f32[39,2048]{1,0:T(8,128)S(1)}, f32[39,2048]{1,0:T(8,128)S(1)}, u32[]{:S(2)}, u32[]{:S(2)}) collective-permute-start(f32[39,2048]{1,0:T(8,128)S(1)} %constant_dynamic-slice_fusion), channel_id=1, source_target_pairs={{0,1},{1,0},{2,3},{3,2},{32,35},{33,34},{34,33},{35,32},{64,65},{6... | collective-permute-start | bytes 958472 | tf_op jit(solution)/shard_map/ppermute | solution.py:270
  82.9 0.0 copy-done
  82.9 0.0 copy-done.1
  82.9 0.0 copy-done.2
  82.9 0.0 copy-done.3
  82.9 2.5 %shard_map.105 = (f32[3,260,128]{2,1,0:T(8,128)S(1)}, f32[3,260,128]{2,1,0:T(8,128)S(1)}) custom-call(s32[2]{0:T(128)S(1)} %bitcast.18, f32[1248,128]{1,0:T(8,128)S(1)} %bitcast.12, f32[1248,128]{1,0:T(8,128)S(1)} %bitcast.14, f32[1248,128]{1,0:T(8,128)S(1)} %bitcast.16), custom_call_target="tpu_custom_call" | custom-call | flops 1000000 | bytes 8000000 | tf_op jit(solution)/shard_map/pallas_call | solution.py:177
  85.5 2.4 %collective-permute-start.2 = (f32[3,260,128]{2,1,0:T(8,128)S(1)}, f32[3,260,128]{2,1,0:T(8,128)S(1)}, u32[]{:S(2)}, u32[]{:S(2)}) collective-permute-start(f32[3,260,128]{2,1,0:T(8,128)S(1)} %get-tuple-element.8), channel_id=1, source_target_pairs={{0,32},{32,0},{64,96},{96,64},{128,160},{160,128},{192,224},{224,1... | collective-permute-start | bytes 1198088 | tf_op jit(solution)/shard_map/ppermute | solution.py:264
  87.9 0.7 collective-permute-start.3
  88.6 0.0 collective-permute-done
  88.6 4.5 %collective-permute-start.1 = (f32[39,2048]{1,0:T(8,128)S(1)}, f32[39,2048]{1,0:T(8,128)S(1)}, u32[]{:S(2)}, u32[]{:S(2)}) collective-permute-start(f32[39,2048]{1,0:T(8,128)S(1)} %add.5.s_ref), channel_id=1, source_target_pairs={{0,3},{1,2},{2,1},{3,0},{32,33},{33,32},{34,35},{35,34},{64,67},{6... | collective-permute-start | bytes 958472 | tf_op jit(solution)/shard_map/ppermute | solution.py:271
  93.2 1.6 %shard_map.104.own_ref = f32[3,624,128]{2,1,0:T(8,128)S(1)} custom-call(s32[2]{0:T(128)S(1)} %bitcast.19, f32[1248,128]{1,0:T(8,128)S(1)} %bitcast.13, f32[1248,128]{1,0:T(8,128)S(1)} %bitcast.15, f32[1248,128]{1,0:T(8,128)S(1)} %bitcast.17), custom_call_target="tpu_custom_call" | custom-call | flops 1000000 | bytes 10000000 | tf_op jit(solution)/shard_map/pallas_call | solution.py:193
  94.8 0.0 collective-permute-done.2.inner_ref
  94.8 0.0 collective-permute-done.3.outer_ref
  94.8 4.0 %collective-permute-done.1.t_ref = f32[39,2048]{1,0:T(8,128)S(1)} collective-permute-done((f32[39,2048]{1,0:T(8,128)S(1)}, f32[39,2048]{1,0:T(8,128)S(1)}, u32[]{:S(2)}, u32[]{:S(2)}) %collective-permute-start.1) | collective-permute-done | bytes 319520 | tf_op jit(solution)/shard_map/ppermute | solution.py:271
  98.8 2.0 %shard_map.106 = (f32[624,128]{1,0:T(8,128)}, f32[624,128]{1,0:T(8,128)}, f32[624,128]{1,0:T(8,128)}) custom-call(s32[2]{0:T(128)S(1)} %bitcast.20, f32[39,2048]{1,0:T(8,128)S(1)} %add.5.s_ref, f32[39,2048]{1,0:T(8,128)S(1)} %collective-permute-done.1.t_ref, f32[3,624,128]{2,1,0:T(8,128)S(1)} %shard_map.104.own_ref, ...), custom_call_target="tpu_custom_call" | custom-call | flops 2000000 | bytes 3000000 | tf_op jit(solution)/shard_map/pallas_call | solution.py:241
  (3 shorter events, 0.1 us)
Async XLA Ops:
  8.8 74.1 %copy-start = (f32[1,159744]{1,0:T(1,128)S(1)}, f32[1,159744]{1,0:T(1,128)}, u32[]{:S(2)}) copy-start(f32[1,159744]{1,0:T(1,128)} %param.12) | copy-start | bytes 1916932
  8.8 74.1 %copy-start.1 = (f32[1,159744]{1,0:T(1,128)S(1)}, f32[1,159744]{1,0:T(1,128)}, u32[]{:S(2)}) copy-start(f32[1,159744]{1,0:T(1,128)} %param.13) | copy-start | bytes 1916932
  8.8 74.1 %copy-start.2 = (f32[1,159744]{1,0:T(1,128)S(1)}, f32[1,159744]{1,0:T(1,128)}, u32[]{:S(2)}) copy-start(f32[1,159744]{1,0:T(1,128)} %param.14) | copy-start | bytes 1916932
  8.8 74.1 %copy-start.3 = (s32[1,1,2]{2,1,0:T(1,128)S(1)}, s32[1,1,2]{2,1,0:T(1,128)}, u32[]{:S(2)}) copy-start(s32[1,1,2]{2,1,0:T(1,128)} %param.11) | copy-start | bytes 28
  76.0 3.2 %collective-permute-start.4 = (f32[23,2048]{1,0:T(8,128)S(1)}, f32[23,2048]{1,0:T(8,128)S(1)}, u32[]{:S(2)}, u32[]{:S(2)}) collective-permute-start(f32[23,2048]{1,0:T(8,128)S(1)} %slice), channel_id=1, source_target_pairs={{0,32},{32,64},{64,96},{96,128},{128,160},{160,192},{192,224},{224... | collective-permute-start | bytes 565256
  79.5 9.1 %collective-permute-start = (f32[39,2048]{1,0:T(8,128)S(1)}, f32[39,2048]{1,0:T(8,128)S(1)}, u32[]{:S(2)}, u32[]{:S(2)}) collective-permute-start(f32[39,2048]{1,0:T(8,128)S(1)} %constant_dynamic-slice_fusion), channel_id=1, source_target_pairs={{0,1},{1,0},{2,3},{3,2},{32,35},{33,34},{34,33},{35,32},{64,65},{6... | collective-permute-start | bytes 958472 | tf_op jit(solution)/shard_map/ppermute | solution.py:270
  85.5 9.3 %collective-permute-start.2 = (f32[3,260,128]{2,1,0:T(8,128)S(1)}, f32[3,260,128]{2,1,0:T(8,128)S(1)}, u32[]{:S(2)}, u32[]{:S(2)}) collective-permute-start(f32[3,260,128]{2,1,0:T(8,128)S(1)} %get-tuple-element.8), channel_id=1, source_target_pairs={{0,32},{32,0},{64,96},{96,64},{128,160},{160,128},{192,224},{224,1... | collective-permute-start | bytes 1198088 | tf_op jit(solution)/shard_map/ppermute | solution.py:264
  87.9 6.9 %collective-permute-start.3 = (f32[3,260,128]{2,1,0:T(8,128)S(1)}, f32[3,260,128]{2,1,0:T(8,128)S(1)}, u32[]{:S(2)}, u32[]{:S(2)}) collective-permute-start(f32[3,260,128]{2,1,0:T(8,128)S(1)} %get-tuple-element.9), channel_id=1, source_target_pairs={{32,64},{64,32},{96,128},{128,96},{160,192},{192,160},{224,256},{2... | collective-permute-start | bytes 1198088 | tf_op jit(solution)/shard_map/ppermute | solution.py:265
  88.6 10.2 %collective-permute-start.1 = (f32[39,2048]{1,0:T(8,128)S(1)}, f32[39,2048]{1,0:T(8,128)S(1)}, u32[]{:S(2)}, u32[]{:S(2)}) collective-permute-start(f32[39,2048]{1,0:T(8,128)S(1)} %add.5.s_ref), channel_id=1, source_target_pairs={{0,3},{1,2},{2,1},{3,0},{32,33},{33,32},{34,35},{35,34},{64,67},{6... | collective-permute-start | bytes 958472 | tf_op jit(solution)/shard_map/ppermute | solution.py:271

commit v4 on v3

--- a/solution.py
+++ b/solution.py
@@ -123,7 +123,9 @@
     return pl.multiple_of(lax.shift_left(lax.shift_right_arithmetic(start, 10), 3), 8)
 
 
-def halo_kernel(bounds_ref, a_ref, b_ref, c_ref, inner_ref, outer_ref, ahead_buf, behind_buf, sem):
+def halo_kernel(
+    bounds_ref, a_ref, b_ref, c_ref, inner_hbm, outer_hbm, ahead_buf, behind_buf, inner_ref, outer_ref, sem, out_sem
+):
     dp = lax.axis_index("dp")
     core = lax.bitwise_and(dp, 1)
     ahead = dp * P_SIZE - bounds_ref[0]
@@ -141,6 +143,7 @@
         copy.start()
     for i in range(3):
         behind_buf[i, :FRONT, :] = jnp.zeros((FRONT, LANES), jnp.float32)
+    sends = []
     for i in range(3):
         copies[2 * i].wait()
         right = shifted(ahead_buf.at[i], to_right - right_row * LANES, HROWS)
@@ -148,6 +151,11 @@
         left = shifted(behind_buf.at[i], to_left + FRONT * LANES, HROWS)
         inner_ref[i] = jnp.where(core == 0, right, left)
         outer_ref[i] = jnp.where(core == 0, left, right)
+        for k, (held, out) in enumerate(((inner_ref, inner_hbm), (outer_ref, outer_hbm))):
+            sends.append(pltpu.make_async_copy(held.at[i], out.at[i], out_sem.at[2 * i + k]))
+            sends[-1].start()
+    for send in sends:
+        send.wait()
 
 
 def own_kernel(bounds_ref, a_ref, b_ref, c_ref, own_ref, buf, sem):
@@ -173,15 +181,18 @@
 
 
 def halos(bounds, old):
-    halo = jax.ShapeDtypeStruct((3, HROWS, LANES), jnp.float32)
+    halo = pltpu.HBM((3, HROWS, LANES), jnp.float32)
     return pl.pallas_call(
         halo_kernel,
         in_specs=[SMEM_SPEC, ANY_SPEC, ANY_SPEC, ANY_SPEC],
-        out_specs=(VMEM_SPEC,) * 2,
+        out_specs=(ANY_SPEC,) * 2,
         out_shape=(halo, halo),
         scratch_shapes=[
             pltpu.VMEM((3, HALO_LOAD + 8, LANES), jnp.float32),
             pltpu.VMEM((3, FRONT + HALO_LOAD, LANES), jnp.float32),
+            pltpu.VMEM((3, HROWS, LANES), jnp.float32),
+            pltpu.VMEM((3, HROWS, LANES), jnp.float32),
+            SEMS,
             SEMS,
         ],
         compiler_params=SMALL,
@@ -259,13 +270,12 @@
 def local(tokens, cotangent, token_counts, old_bounds, old_first, old_second, old_master):
     bounds = old_bounds.reshape(2)
     old = [a.reshape(CROWS, LANES) for a in (old_first, old_second, old_master)]
-    inner, outer = halos(bounds, old)
     own = own_window(bounds, old)
-    inner = lax.ppermute(inner, "dp", [(i, i ^ 1) for i in range(SHARDS)])
-    outer = lax.ppermute(outer, "dp", [(i, i + 1 if i % 2 else i - 1) for i in range(1, SHARDS - 1)])
     partial = local_gradient(tokens, cotangent, token_counts.reshape(1))
     shard = lax.psum_scatter(partial, "dp", scatter_dimension=0, tiled=True)
-    shard = lax.optimization_barrier(shard)
+    shard, inner_out, outer_out = lax.optimization_barrier((shard, *halos(bounds, old)))
+    inner = lax.ppermute(inner_out, "dp", [(i, i ^ 1) for i in range(SHARDS)])
+    outer = lax.ppermute(outer_out, "dp", [(i, i + 1 if i % 2 else i - 1) for i in range(1, SHARDS - 1)])
     one, three = (lambda r: r ^ 1), (lambda r: r ^ 3)
     half = shard + lax.ppermute(shard, ("dp", "rep"), rep_pairs(one, three))
     rest = lax.ppermute(half, ("dp", "rep"), rep_pairs(three, one))

time: 102 us -> 104 us (1.020); the launches traced: 101 us -> 104 us
  waiting for transfers between devices: 4 us -> 6.81 us
    ppermute x1, waiting for transfers between devices: 0.01 us -> 2.93 us  [local(): half = shard + lax.ppermute(shard, ('dp', 'rep'), rep_pairs(one, three))]
  transfers between devices with their start and end apart: 5 -> 5, of which waited for: 1 -> 2; matrix products, arithmetic and copies ran while one was open for 1% -> 1% of each run, Pallas kernels for 4% -> 5%
where the time goes in v4:
time: 104 us
  blocking collectives  67.1 us (65%)
  Pallas kernels  14.4 us (14%)
  starting transfers between devices  12 us (12%)
  waiting for transfers between devices  6.81 us (7%)
  between operations  2.09 us (2%)
  local copies, waits for them, and re-layouts  1.58 us (2%)
    unnamed x1, blocking collectives  67.1 us
    pallas_call x1, Pallas kernels, local_gradient(): pl.pallas_call(grad_kernel, grid=(4,), in_specs=[pl.BlockSpec(memory_spac...  7.53 us
    ppermute x1, starting transfers between devices, local(): rest = lax.ppermute(half, ('dp', 'rep'), rep_pairs(three, one))  4.66 us
    ppermute x1, waiting for transfers between devices, local(): rest = lax.ppermute(half, ('dp', 'rep'), rep_pairs(three, one))  3.87 us
    ppermute x1, starting transfers between devices, local(): half = shard + lax.ppermute(shard, ('dp', 'rep'), rep_pairs(one, three))  3.41 us
    pallas_call x1, Pallas kernels, halos(): pl.pallas_call(halo_kernel, in_specs=[SMEM_SPEC, ANY_SPEC, ANY_SPEC, ANY_...  3.3 us
    ppermute x1, waiting for transfers between devices, local(): half = shard + lax.ppermute(shard, ('dp', 'rep'), rep_pairs(one, three))  2.93 us
  transfers between devices with their start and end apart: 5, of which 2 were waited for; matrix products, arithmetic and copies ran while one was open for 1% of the time, Pallas kernels for 5%

profile of v4, /device:TPU:56, one launch (start us, length us, event | category | flops | bytes accessed | tf_op | source)
XLA Modules:
  0.0 104.0 jit_solution(14478834709534088077)
XLA Ops:
  1.3 7.5 %shard_map.103 = f32[936,2048]{1,0:T(8,128)} custom-call(s32[1]{0:T(128)} %bitcast.11.count_ref, bf16[256,256]{1,0:T(8,128)(2,1)} %tok_ref.1, bf16[2352,256]{1,0:T(8,128)(2,1)} %constant.2.clone.pick_ref, bf16[256,6656]{1,0:T(8,128)(2,1)} %c3_ref.1, bf16[256,6656]{1,0:T(8,128)(2,1)} %c3_ref.1, bf16[256,6656]{1,0:T(8,128)(2,1)} %c3_ref.1, ...), custom_call_target="tpu_custom_call" | custom-call | flops 2000000000 | bytes 12000000 | tf_op jit(solution)/shard_map/pallas_call | solution.py:86
  8.8 0.0 copy-start
  8.8 0.0 copy-start.1
  8.8 0.0 copy-start.2
  8.8 0.0 copy-start.3
  8.8 67.1 %fusion = f32[40,2048]{1,0:T(8,128)S(1)} fusion(f32[936,2048]{1,0:T(8,128)} %shard_map.103), kind=kCustom, calls=%all-reduce-scatter | all-reduce-scatter fusion | flops 1966081 | bytes 7999488
  76.0 1.3 %collective-permute-start.4 = (f32[23,2048]{1,0:T(8,128)S(1)}, f32[23,2048]{1,0:T(8,128)S(1)}, u32[]{:S(2)}, u32[]{:S(2)}) collective-permute-start(f32[23,2048]{1,0:T(8,128)S(1)} %slice), channel_id=1, source_target_pairs={{0,32},{32,64},{64,96},{96,128},{128,160},{160,192},{192,224},{224... | collective-permute-start | bytes 565256
  77.3 1.3 %dynamic-slice.4 = u32[1]{0:T(128)} dynamic-slice(u32[768]{0:T(1024)} %constant.12, u32[]{:S(6)} %partition-id.4), dynamic_slice_sizes={1} | dynamic-slice | bytes 12
  79.2 0.0 copy-done
  79.2 0.0 copy-done.1
  79.2 0.0 copy-done.2
  79.2 0.0 copy-done.3
  79.2 3.3 %shard_map.104 = (f32[3,260,128]{2,1,0:T(8,128)}, f32[3,260,128]{2,1,0:T(8,128)}) custom-call(s32[2]{0:T(128)S(1)} %bitcast.18, f32[1248,128]{1,0:T(8,128)S(1)} %bitcast.12, f32[1248,128]{1,0:T(8,128)S(1)} %bitcast.14, f32[1248,128]{1,0:T(8,128)S(1)} %bitcast.16), custom_call_target="tpu_custom_call" | custom-call | flops 1000000 | bytes 8000000 | tf_op jit(solution)/shard_map/pallas_call | solution.py:185
  82.5 0.0 collective-permute-done.4
  82.6 0.2 concatenate
  82.8 3.4 %collective-permute-start = (f32[39,2048]{1,0:T(8,128)S(1)}, f32[39,2048]{1,0:T(8,128)S(1)}, u32[]{:S(2)}, u32[]{:S(2)}) collective-permute-start(f32[39,2048]{1,0:T(8,128)S(1)} %constant_dynamic-slice_fusion), channel_id=1, source_target_pairs={{0,1},{1,0},{2,3},{3,2},{32,35},{33,34},{34,33},{35,32},{64,65},{6... | collective-permute-start | bytes 958472 | tf_op jit(solution)/shard_map/ppermute | solution.py:280
  86.3 1.9 %collective-permute-start.2 = (f32[3,260,128]{2,1,0:T(8,128)}, f32[3,260,128]{2,1,0:T(8,128)S(1)}, u32[]{:S(2)}, u32[]{:S(2)}) collective-permute-start(f32[3,260,128]{2,1,0:T(8,128)} %get-tuple-element.14), channel_id=1, source_target_pairs={{0,32},{32,0},{64,96},{96,64},{128,160},{160,128},{192,224},{224,1... | collective-permute-start | bytes 1198088 | tf_op jit(solution)/shard_map/ppermute | solution.py:277
  88.2 0.7 collective-permute-start.3
  88.9 2.9 %collective-permute-done = f32[39,2048]{1,0:T(8,128)S(1)} collective-permute-done((f32[39,2048]{1,0:T(8,128)S(1)}, f32[39,2048]{1,0:T(8,128)S(1)}, u32[]{:S(2)}, u32[]{:S(2)}) %collective-permute-start) | collective-permute-done | bytes 319520 | tf_op jit(solution)/shard_map/ppermute | solution.py:280
  91.8 0.1 add.5.s_ref
  91.9 4.7 %collective-permute-start.1 = (f32[39,2048]{1,0:T(8,128)S(1)}, f32[39,2048]{1,0:T(8,128)S(1)}, u32[]{:S(2)}, u32[]{:S(2)}) collective-permute-start(f32[39,2048]{1,0:T(8,128)S(1)} %add.5.s_ref), channel_id=1, source_target_pairs={{0,3},{1,2},{2,1},{3,0},{32,33},{33,32},{34,35},{35,34},{64,67},{6... | collective-permute-start | bytes 958472 | tf_op jit(solution)/shard_map/ppermute | solution.py:281
  96.5 1.6 %shard_map.105.own_ref = f32[3,624,128]{2,1,0:T(8,128)S(1)} custom-call(s32[2]{0:T(128)S(1)} %bitcast.19, f32[1248,128]{1,0:T(8,128)S(1)} %bitcast.13, f32[1248,128]{1,0:T(8,128)S(1)} %bitcast.15, f32[1248,128]{1,0:T(8,128)S(1)} %bitcast.17), custom_call_target="tpu_custom_call" | custom-call | flops 1000000 | bytes 10000000 | tf_op jit(solution)/shard_map/pallas_call | solution.py:204
  98.1 0.0 collective-permute-done.2.inner_ref
  98.2 0.0 collective-permute-done.3.outer_ref
  98.2 3.9 %collective-permute-done.1.t_ref = f32[39,2048]{1,0:T(8,128)S(1)} collective-permute-done((f32[39,2048]{1,0:T(8,128)S(1)}, f32[39,2048]{1,0:T(8,128)S(1)}, u32[]{:S(2)}, u32[]{:S(2)}) %collective-permute-start.1) | collective-permute-done | bytes 319520 | tf_op jit(solution)/shard_map/ppermute | solution.py:281
  102.0 2.0 %shard_map.106 = (f32[624,128]{1,0:T(8,128)}, f32[624,128]{1,0:T(8,128)}, f32[624,128]{1,0:T(8,128)}) custom-call(s32[2]{0:T(128)S(1)} %bitcast.20, f32[39,2048]{1,0:T(8,128)S(1)} %add.5.s_ref, f32[39,2048]{1,0:T(8,128)S(1)} %collective-permute-done.1.t_ref, f32[3,624,128]{2,1,0:T(8,128)S(1)} %shard_map.105.own_ref, ...), custom_call_target="tpu_custom_call" | custom-call | flops 2000000 | bytes 3000000 | tf_op jit(solution)/shard_map/pallas_call | solution.py:252
  (2 shorter events, 0.1 us)
Async XLA Ops:
  8.8 70.4 %copy-start = (f32[1,159744]{1,0:T(1,128)S(1)}, f32[1,159744]{1,0:T(1,128)}, u32[]{:S(2)}) copy-start(f32[1,159744]{1,0:T(1,128)} %param.12) | copy-start | bytes 1916932
  8.8 70.4 %copy-start.1 = (f32[1,159744]{1,0:T(1,128)S(1)}, f32[1,159744]{1,0:T(1,128)}, u32[]{:S(2)}) copy-start(f32[1,159744]{1,0:T(1,128)} %param.13) | copy-start | bytes 1916932
  8.8 70.4 %copy-start.2 = (f32[1,159744]{1,0:T(1,128)S(1)}, f32[1,159744]{1,0:T(1,128)}, u32[]{:S(2)}) copy-start(f32[1,159744]{1,0:T(1,128)} %param.14) | copy-start | bytes 1916932
  8.8 70.4 %copy-start.3 = (s32[1,1,2]{2,1,0:T(1,128)S(1)}, s32[1,1,2]{2,1,0:T(1,128)}, u32[]{:S(2)}) copy-start(s32[1,1,2]{2,1,0:T(1,128)} %param.11) | copy-start | bytes 28
  76.0 6.6 %collective-permute-start.4 = (f32[23,2048]{1,0:T(8,128)S(1)}, f32[23,2048]{1,0:T(8,128)S(1)}, u32[]{:S(2)}, u32[]{:S(2)}) collective-permute-start(f32[23,2048]{1,0:T(8,128)S(1)} %slice), channel_id=1, source_target_pairs={{0,32},{32,64},{64,96},{96,128},{128,160},{160,192},{192,224},{224... | collective-permute-start | bytes 565256
  82.8 9.0 %collective-permute-start = (f32[39,2048]{1,0:T(8,128)S(1)}, f32[39,2048]{1,0:T(8,128)S(1)}, u32[]{:S(2)}, u32[]{:S(2)}) collective-permute-start(f32[39,2048]{1,0:T(8,128)S(1)} %constant_dynamic-slice_fusion), channel_id=1, source_target_pairs={{0,1},{1,0},{2,3},{3,2},{32,35},{33,34},{34,33},{35,32},{64,65},{6... | collective-permute-start | bytes 958472 | tf_op jit(solution)/shard_map/ppermute | solution.py:280
  86.3 11.9 %collective-permute-start.2 = (f32[3,260,128]{2,1,0:T(8,128)}, f32[3,260,128]{2,1,0:T(8,128)S(1)}, u32[]{:S(2)}, u32[]{:S(2)}) collective-permute-start(f32[3,260,128]{2,1,0:T(8,128)} %get-tuple-element.14), channel_id=1, source_target_pairs={{0,32},{32,0},{64,96},{96,64},{128,160},{160,128},{192,224},{224,1... | collective-permute-start | bytes 1198088 | tf_op jit(solution)/shard_map/ppermute | solution.py:277
  88.2 10.0 %collective-permute-start.3 = (f32[3,260,128]{2,1,0:T(8,128)}, f32[3,260,128]{2,1,0:T(8,128)S(1)}, u32[]{:S(2)}, u32[]{:S(2)}) collective-permute-start(f32[3,260,128]{2,1,0:T(8,128)} %get-tuple-element.15), channel_id=1, source_target_pairs={{32,64},{64,32},{96,128},{128,96},{160,192},{192,160},{224,256},{2... | collective-permute-start | bytes 1198088 | tf_op jit(solution)/shard_map/ppermute | solution.py:278
  91.9 10.2 %collective-permute-start.1 = (f32[39,2048]{1,0:T(8,128)S(1)}, f32[39,2048]{1,0:T(8,128)S(1)}, u32[]{:S(2)}, u32[]{:S(2)}) collective-permute-start(f32[39,2048]{1,0:T(8,128)S(1)} %add.5.s_ref), channel_id=1, source_target_pairs={{0,3},{1,2},{2,1},{3,0},{32,33},{33,32},{34,35},{35,34},{64,67},{6... | collective-permute-start | bytes 958472 | tf_op jit(solution)/shard_map/ppermute | solution.py:281

commit v5 on v2

v5 whole, which is shorter than its diff:
```python
import functools

import jax
import jax.numpy as jnp
from jax import lax
from jax.experimental import pallas as pl
from jax.experimental.pallas import tpu as pltpu
from jax.sharding import PartitionSpec as P

ADAM_STEP = 1000
BETA_ONE = 0.9
BETA_TWO = 0.95
LEARN_RATE = 0.001
DECAY_RATE = 0.1
EPSILON = 1e-08

SHARDS = 24
COLS = 6656
BROWS = 256
LANES = 128
P_SIZE = 79872
HALF = 33280
CAP = 159744
ROWS = P_SIZE // LANES
HROWS = HALF // LANES
CROWS = CAP // LANES
FRONT = 264
GROWS = P_SIZE // COLS

SMEM_SPEC = pl.BlockSpec(memory_space=pltpu.SMEM)
SMALL = pltpu.CompilerParams(vmem_limit_bytes=12 * 1024 * 1024)
ANY_SPEC = pl.BlockSpec(memory_space=pl.ANY)
HBM_SPEC = pl.BlockSpec(memory_space=pltpu.HBM)
VMEM_SPEC = pl.BlockSpec(memory_space=pltpu.VMEM)
UNIT = 1280
SHARD_COLS = 8 * UNIT
MAIN = COLS
EXTRA = COLS // 2
BLOCKS = 48
PARITY_ROWS = 96


def other(z):
    step = z + 1 if z % 2 else z - 1
    return step % 12


def block_places(chain, core, z, x):
    def side(v):
        w = v + 2 * lax.bitwise_and(v, 1) - 1
        return jnp.where(w < 0, w + 12, jnp.where(w >= 12, w - 12, w))

    def flip(v):
        return lax.bitwise_xor(v, 1)

    xs = later_xs = [x, x ^ 3, x ^ 1, x ^ 2]
    zs = later_zs = [z, side(z), flip(z), side(flip(z))]
    if chain == 1:
        xs = [x, x ^ 1, x ^ 3, x ^ 2]
        zs = [z, flip(z), side(z), flip(side(z))]
    places = []
    for pos in range(BLOCKS):
        a, b, j = pos // 12, (pos % 12) // 3, pos % 3
        x_to = jnp.where(core == 0, xs[a], later_xs[b])
        z_to = jnp.where(core == 0, later_zs[b], zs[a]) + 4 * j
        places.append((jnp.where(z_to >= 12, z_to - 12, z_to), x_to))
    return places


def grad_kernel(count_ref, tok_hbm, cot_hbm, own0_ref, own1_ref, send0_ref, send1_ref, held, tok_ref, cot_ref, sem):
    copies = [pltpu.make_async_copy(tok_hbm, tok_ref, sem.at[0])]
    for i in range(4):
        cols = pl.ds(1664 * i, 1664)
        copies.append(pltpu.make_async_copy(cot_hbm.at[:, cols], cot_ref.at[:, cols], sem.at[1 + i]))
    for copy in copies:
        copy.start()
    dp, x = lax.axis_index("dp"), lax.axis_index("rep")
    z, core = lax.shift_right_logical(dp, 1), lax.bitwise_and(dp, 1)
    copies[0].wait()
    tok_row = lax.broadcasted_iota(jnp.int32, (BROWS, BROWS), 0)
    tok = jnp.where(tok_row < count_ref[0], tok_ref[...], jnp.zeros_like(tok_ref))
    row = lax.broadcasted_iota(jnp.int32, (2 * PARITY_ROWS, BROWS), 0)
    col = lax.broadcasted_iota(jnp.int32, (2 * PARITY_ROWS, BROWS), 1)
    far = row >= PARITY_ROWS
    row = jnp.where(far, row - PARITY_ROWS, row)
    parity = jnp.where(far, 1 - core, core)
    j = lax.bitwise_and(row, 7)
    lead = col - 24 * lax.shift_right_logical(row, 3) - GROWS * parity

    def picked(match):
        one = jnp.where(match, jnp.float32(1), jnp.float32(0)).astype(jnp.bfloat16)
        out = lax.dot_general(one, tok, (((1,), (1,)), ((), ())), preferred_element_type=jnp.float32)
        return out.astype(jnp.bfloat16)

    def dot(a, b):
        return jnp.dot(a, b, preferred_element_type=jnp.float32)

    main = picked(lead == j)
    half_row = lead == 8 + lax.shift_right_logical(j, 1)
    even = picked(half_row & (lax.bitwise_and(j, 1) == 0))
    odd = picked(half_row & (lax.bitwise_and(j, 1) == 1))
    for at in range(0, MAIN, 1664):
        copies[1 + at // 1664].wait()
        held[:, at : at + 1664] = dot(main, cot_ref[:, at : at + 1664])
    for at in range(0, EXTRA, 1664):
        low, high = cot_ref[:, at : at + 1664], cot_ref[:, EXTRA + at : EXTRA + at + 1664]
        held[:, MAIN + at : MAIN + at + 1664] = dot(even, low) + dot(odd, high)
    held[:, MAIN + EXTRA :] = jnp.zeros((2 * PARITY_ROWS, SHARD_COLS - MAIN - EXTRA), jnp.float32)

    for chain, (own, send) in enumerate(((own0_ref, send0_ref), (own1_ref, send1_ref))):
        for far_rows, out, role in ((0, own, core), (PARITY_ROWS, send, 1 - core)):
            for pos, (z_to, x_to) in enumerate(block_places(chain, role, z, x)):
                rows = pl.ds(pl.multiple_of(far_rows + 8 * z_to, 8), 8)
                cols = pl.ds(pl.multiple_of(UNIT * (4 * chain + x_to), LANES), UNIT)
                out[pos] = held[rows, cols]


def local_gradient(tokens, cotangent, count):
    shape = jax.ShapeDtypeStruct((BLOCKS, 8, UNIT), jnp.float32)
    return pl.pallas_call(
        grad_kernel,
        in_specs=[SMEM_SPEC, HBM_SPEC, HBM_SPEC],
        out_specs=(VMEM_SPEC,) * 4,
        out_shape=(shape,) * 4,
        scratch_shapes=[
            pltpu.VMEM((2 * PARITY_ROWS, SHARD_COLS), jnp.float32),
            pltpu.VMEM((BROWS, BROWS), jnp.bfloat16),
            pltpu.VMEM((BROWS, COLS), jnp.bfloat16),
            pltpu.SemaphoreType.DMA((5,)),
        ],
        compiler_params=pltpu.CompilerParams(vmem_limit_bytes=32 * 1024 * 1024),
        cost_estimate=pl.CostEstimate(flops=2 * 10**9, bytes_accessed=11 * 10**6, transcendentals=0),
    )(count, *(pltpu.with_memory_space_constraint(a, pltpu.HBM) for a in (tokens, cotangent)))


def pairs(move0, move1):
    out = []
    for dp in range(SHARDS):
        for x in range(4):
            z, core = dp // 2, dp % 2
            z_to, x_to = (move1 if core else move0)(z, x)
            out.append((4 * dp + x, 4 * (2 * z_to + core) + x_to))
    return out


def reduced(own, send, bounds, old):
    def x1(z, x):
        return z, x ^ 1

    def x2(z, x):
        return z, x ^ 2

    def x3(z, x):
        return z, x ^ 3

    def z1(z, x):
        return z ^ 1, x

    def zo(z, x):
        return other(z), x

    def zt(z, x):
        return other(z ^ 1), x

    axes = ("dp", "rep")
    first, second = ((x1, z1), (x3, zo)), ((x3, zo), (x1, z1))
    swap = [(i, i ^ 1) for i in range(SHARDS)]
    held = []
    for c in range(2):
        got = lax.ppermute(send[c], "dp", swap)
        far = lax.ppermute(own[c][24:] + got[24:], axes, pairs(*first[c]))
        held.append([own[c][i : i + 12] + got[i : i + 12] + far[i : i + 12] for i in (0, 12)])
        if c == 0:
            inner, outer, state = windows(bounds, old)
            *held[0], inner, outer, state = lax.optimization_barrier((*held[0], inner, outer, state))
    held = [held[c][0] + lax.ppermute(held[c][1], axes, pairs(*second[c])) for c in range(2)]
    got = [
        lax.ppermute(jnp.stack([h[3 * i : 3 * i + 3] for h in held]), axes, pairs(*to))
        for i, to in ((1, (zo, x3)), (2, (z1, x1)), (3, (zt, x2)))
    ]
    rest = [
        jnp.stack([h[i] for h in held]) + got[0][:, i] + got[1][:, i] + got[2][:, i] for i in range(3)
    ]
    *rest, inner, outer = lax.optimization_barrier((*rest, inner, outer))
    inner = lax.ppermute(inner, "dp", swap)
    outer = lax.ppermute(outer, "dp", [(i, i + 1 if i % 2 else i - 1) for i in range(1, SHARDS - 1)])
    ahead = [(i, (i + 8) % SHARDS) for i in range(SHARDS)]
    behind = [(i, (i - 8) % SHARDS) for i in range(SHARDS)]
    mine = rest[0] + lax.ppermute(rest[1], "dp", ahead) + lax.ppermute(rest[2], "dp", behind)
    return lax.all_gather(mine, "rep", axis=0, tiled=False), (state, inner, outer)


def shifted(ref, start, rows):
    start = start + FRONT * LANES
    top = lax.shift_right_logical(start, 7)
    lane_start = start - top * LANES
    first = pltpu.roll(ref[pl.ds(top, rows), :], LANES - lane_start, 1)
    second = pltpu.roll(ref[pl.ds(top + 1, rows), :], LANES - lane_start, 1)
    lane = lax.broadcasted_iota(jnp.int32, (rows, LANES), 1)
    return jnp.where(lane < LANES - lane_start, first, second)


def load_old(refs, buf, sem):
    copies = [pltpu.make_async_copy(r, buf.at[i, pl.ds(FRONT, CROWS)], sem.at[i]) for i, r in enumerate(refs)]
    for c in copies:
        c.start()
    for i in range(3):
        buf[i, :FRONT, :] = jnp.zeros((FRONT, LANES), jnp.float32)
        buf[i, FRONT + CROWS :, :] = jnp.zeros((8, LANES), jnp.float32)
    for c in copies:
        c.wait()


def window_kernel(bounds_ref, a_ref, b_ref, c_ref, inner_ref, outer_ref, own_ref, buf, sem):
    load_old((a_ref, b_ref, c_ref), buf, sem)
    dp = lax.axis_index("dp")
    core = lax.bitwise_and(dp, 1)
    ahead = dp * P_SIZE - bounds_ref[0]
    to_right, to_left = ahead + P_SIZE, jnp.maximum(ahead, 0) - HALF
    for i in range(3):
        inner_ref[i] = shifted(buf.at[i], jnp.where(core == 0, to_right, to_left), HROWS)
        outer_ref[i] = shifted(buf.at[i], jnp.where(core == 0, to_left, to_right), HROWS)
        own_ref[i] = shifted(buf.at[i], ahead, ROWS)


OLD_SCRATCH = (
    pltpu.VMEM((3, FRONT + CROWS + 8, LANES), jnp.float32),
    pltpu.SemaphoreType.DMA((3,)),
)


def windows(bounds, old):
    halo = jax.ShapeDtypeStruct((3, HROWS, LANES), jnp.float32)
    own = jax.ShapeDtypeStruct((3, ROWS, LANES), jnp.float32)
    return pl.pallas_call(
        window_kernel,
        in_specs=[SMEM_SPEC, ANY_SPEC, ANY_SPEC, ANY_SPEC],
        out_specs=(VMEM_SPEC,) * 3,
        out_shape=(halo, halo, own),
        scratch_shapes=list(OLD_SCRATCH),
        compiler_params=SMALL,
        cost_estimate=pl.CostEstimate(flops=10**6, bytes_accessed=16 * 10**6, transcendentals=0),
    )(bounds, *old)


def adam_kernel(
    bounds_ref, parts_ref, own_ref, inner_ref, outer_ref,
    master_ref, first_ref, second_ref, shard, grad, state,
):
    row = lax.broadcasted_iota(jnp.int32, (ROWS, LANES), 0)
    lane = lax.broadcasted_iota(jnp.int32, (ROWS, LANES), 1)
    pos = lax.axis_index("dp") * P_SIZE + row * LANES + lane
    tail = ROWS - HROWS
    first_core = lax.bitwise_and(lax.axis_index("dp"), 1) == 0
    below, above = pos[:HROWS] < bounds_ref[0], pos[tail:] >= bounds_ref[1]
    for i in range(3):
        left = jnp.where(first_core, outer_ref[i], inner_ref[i])
        right = jnp.where(first_core, inner_ref[i], outer_ref[i])
        state[i, :HROWS, :] = jnp.where(below, left, own_ref[i, :HROWS, :])
        state[i, HROWS:tail, :] = own_ref[i, HROWS:tail, :]
        state[i, tail:, :] = jnp.where(above, right, own_ref[i, tail:, :])
    for place in range(4):
        for chain in range(2):
            at = UNIT * (4 * chain + place)
            shard[:, at : at + UNIT] = parts_ref[place, chain]
    tiles = COLS // LANES
    for at in range(tiles):
        grad[pl.ds(at, 8, stride=tiles), :] = shard[:, LANES * at : LANES * (at + 1)]
    for at in range(tiles // 2):
        col = MAIN + LANES * at
        grad[pl.ds(8 * tiles + at, 8, stride=tiles // 2), :] = shard[:, col : col + LANES]
    corr_one = 1.0 - BETA_ONE**ADAM_STEP
    corr_two = 1.0 - BETA_TWO**ADAM_STEP
    g = grad[...]
    first_new = BETA_ONE * state[0] + (1.0 - BETA_ONE) * g
    second_new = BETA_TWO * state[1] + (1.0 - BETA_TWO) * g * g
    master = state[2]
    update = first_new / corr_one / (jnp.sqrt(second_new / corr_two) + EPSILON) + DECAY_RATE * master
    master_ref[...] = master - LEARN_RATE * update
    first_ref[...] = first_new
    second_ref[...] = second_new


def adam_step(bounds, parts, own, left, right):
    shape = jax.ShapeDtypeStruct((ROWS, LANES), jnp.float32)
    return pl.pallas_call(
        adam_kernel,
        in_specs=[SMEM_SPEC] + [VMEM_SPEC] * 4,
        out_specs=(VMEM_SPEC,) * 3,
        out_shape=(shape,) * 3,
        scratch_shapes=[
            pltpu.VMEM((8, SHARD_COLS), jnp.float32),
            pltpu.VMEM((ROWS, LANES), jnp.float32),
            pltpu.VMEM((3, ROWS, LANES), jnp.float32),
        ],
        compiler_params=SMALL,
        cost_estimate=pl.CostEstimate(flops=2 * 10**6, bytes_accessed=3 * 10**6, transcendentals=10**5),
    )(bounds, parts, own, left, right)


def local(tokens, cotangent, token_counts, old_bounds, old_first, old_second, old_master):
    bounds = old_bounds.reshape(2)
    old = [a.reshape(CROWS, LANES) for a in (old_first, old_second, old_master)]
    own0, own1, send0, send1 = local_gradient(tokens, cotangent, token_counts.reshape(1))
    parts, state = reduced((own0, own1), (send0, send1), bounds, old)
    outs = adam_step(bounds, parts, *state)
    return tuple(a.reshape(1, P_SIZE) for a in outs)


def solution(mesh):
    placed = (
        P(("dp", "rep"), None),
        P(("dp", "rep"), "mp"),
        P("dp", "rep"),
        P("mp", "dp", None),
        P("mp", "dp"),
        P("mp", "dp"),
        P("mp", "dp"),
    )
    return jax.shard_map(
        local,
        mesh=mesh,
        in_specs=placed,
        out_specs=(P("mp", "dp"), P("mp", "dp"), P("mp", "dp")),
        check_vma=False,
    )
```

time: 105 us -> 101 us (0.962)
  blocking collectives: 66.9 us -> 12.6 us
  starting transfers between devices: 11.3 us -> 49.5 us
  waiting for transfers between devices: 6.57 us -> 27.8 us
  Pallas kernels: 14.7 us -> 8.13 us
  local copies, waits for them, and re-layouts: 2.28 us -> 0.15 us
    unnamed x1 -> x0, blocking collectives: 66.9 us -> none
    ppermute x4 -> x13, starting transfers between devices: 10 us -> 49.5 us  [the longest x3 18.4 us: reduced(): lax.ppermute(jnp.stack([h[3 * i:3 * i + 3] for h in held]), axes, pairs(*...]
    ppermute x4 -> x13, waiting for transfers between devices: 6.57 us -> 27.8 us  [the longest x2 8.45 us: reduced(): lax.ppermute(held[c][1], axes, pairs(*second[c]))]
    all_gather x0 -> x1, blocking collectives: none -> 12.6 us  [reduced(): lax.all_gather(mine, 'rep', axis=0, tiled=False)]
    pallas_call x2, Pallas kernels: 10.6 us -> 5.98 us  [the longest x1 4.05 us: local_gradient(): pl.pallas_call(grad_kernel, in_specs=[SMEM_SPEC, HBM_SPEC, HBM_SPEC], out...]
    unnamed x12 -> x8, local copies, waits for them, and re-layouts: 2.28 us -> 0.03 us
    pallas_call x1, Pallas kernels: 4.16 us -> 2.15 us  [windows(): pl.pallas_call(window_kernel, in_specs=[SMEM_SPEC, ANY_SPEC, ANY_SPEC, AN...]
    unnamed x1 -> x0, starting transfers between devices: 1.3 us -> none
  transfers between devices with their start and end apart: 5 -> 13, of which waited for: 1 -> 8; matrix products, arithmetic and copies ran while one was open for 1% -> 1% of each run, Pallas kernels for 4% -> 2%
where the time goes in v5:
time: 101 us; the launch traced here: 100 us
  starting transfers between devices  49.5 us (49%)
  waiting for transfers between devices  27.8 us (28%)
  blocking collectives  12.6 us (12%)
  Pallas kernels  8.13 us (8%)
  between operations  1.59 us (2%)
    ppermute x3, starting transfers between devices, reduced(): lax.ppermute(jnp.stack([h[3 * i:3 * i + 3] for h in held]), axes, pairs(*...  18.4 us
    all_gather x1, blocking collectives, reduced(): lax.all_gather(mine, 'rep', axis=0, tiled=False)  12.6 us
    ppermute x2, waiting for transfers between devices, reduced(): lax.ppermute(held[c][1], axes, pairs(*second[c]))  8.45 us
    ppermute x3, waiting for transfers between devices, reduced(): lax.ppermute(jnp.stack([h[3 * i:3 * i + 3] for h in held]), axes, pairs(*...  8.25 us
    ppermute x2, starting transfers between devices, reduced(): far = lax.ppermute(own[c][24:] + got[24:], axes, pairs(*first[c]))  7.54 us
    ppermute x2, starting transfers between devices, reduced(): lax.ppermute(held[c][1], axes, pairs(*second[c]))  6.8 us
    ppermute x2, waiting for transfers between devices, reduced(): far = lax.ppermute(own[c][24:] + got[24:], axes, pairs(*first[c]))  6.24 us
    ppermute x1, starting transfers between devices, reduced(): lax.ppermute(rest[1], 'dp', ahead)  4.94 us
  transfers between devices with their start and end apart: 13, of which 8 were waited for; matrix products, arithmetic and copies ran while one was open for 1% of the time, Pallas kernels for 2%

profile of v5, /device:TPU:56, one launch (start us, length us, event | category | flops | bytes accessed | tf_op | source)
XLA Modules:
  0.0 100.5 jit_solution(10371809842957916648)
XLA Ops:
  1.3 4.0 %shard_map.94 = (f32[48,8,1280]{2,1,0:T(8,128)S(1)}, f32[48,8,1280]{2,1,0:T(8,128)S(1)}, f32[48,8,1280]{2,1,0:T(8,128)S(1)}, f32[48,8,1280]{2,1,0:T(8,128)S(1)}) custom-call(s32[1]{0:T(128)} %bitcast.69.count_ref, bf16[256,256]{1,0:T(8,128)(2,1)} %tok_hbm.1, bf16[256,6656]{1,0:T(8,128)(2,1)} %cot_hbm.1), custom_call_target="tpu_custom_call" | custom-call | flops 2000000000 | bytes 11000000 | tf_op jit(solution)/shard_map/pallas_call | solution.py:120
  5.3 1.9 %collective-permute-start = (f32[48,8,1280]{2,1,0:T(8,128)S(1)}, f32[48,8,1280]{2,1,0:T(8,128)S(1)}, u32[]{:S(2)}, u32[]{:S(2)}) collective-permute-start(f32[48,8,1280]{2,1,0:T(8,128)S(1)} %get-tuple-element.24), channel_id=1, source_target_pairs={{0,32},{32,0},{64,96},{96,64},{128,160},{160,128},{192,224},{224,1... | collective-permute-start | bytes 5898248 | tf_op jit(solution)/shard_map/ppermute | solution.py:170
  7.3 2.4 %collective-permute-start.3 = (f32[48,8,1280]{2,1,0:T(8,128)S(1)}, f32[48,8,1280]{2,1,0:T(8,128)S(1)}, u32[]{:S(2)}, u32[]{:S(2)}) collective-permute-start(f32[48,8,1280]{2,1,0:T(8,128)S(1)} %get-tuple-element.31), channel_id=1, source_target_pairs={{0,32},{32,0},{64,96},{96,64},{128,160},{160,128},{192,224},{224,1... | collective-permute-start | bytes 5898248 | tf_op jit(solution)/shard_map/ppermute | solution.py:170
  9.7 1.5 %collective-permute-done = f32[48,8,1280]{2,1,0:T(8,128)S(1)} collective-permute-done((f32[48,8,1280]{2,1,0:T(8,128)S(1)}, f32[48,8,1280]{2,1,0:T(8,128)S(1)}, u32[]{:S(2)}, u32[]{:S(2)}) %collective-permute-start) | collective-permute-done | bytes 1966112 | tf_op jit(solution)/shard_map/ppermute | solution.py:170
  11.2 0.1 slice_add_fusion.1
  11.4 3.5 %collective-permute-start.1 = (f32[24,8,1280]{2,1,0:T(8,128)S(1)}, f32[24,8,1280]{2,1,0:T(8,128)S(1)}, u32[]{:S(2)}, u32[]{:S(2)}) collective-permute-start(f32[24,8,1280]{2,1,0:T(8,128)S(1)} %slice_add_fusion.1), channel_id=1, source_target_pairs={{0,1},{1,0},{2,3},{3,2},{32,96},{33,97},{34,98},{35,99},{64,65},{6... | collective-permute-start | bytes 2949128 | tf_op jit(solution)/shard_map/ppermute | solution.py:171
  14.9 0.1 slice_add_fusion
  15.0 4.0 %collective-permute-start.4 = (f32[24,8,1280]{2,1,0:T(8,128)S(1)}, f32[24,8,1280]{2,1,0:T(8,128)S(1)}, u32[]{:S(2)}, u32[]{:S(2)}) collective-permute-start(f32[24,8,1280]{2,1,0:T(8,128)S(1)} %slice_add_fusion), channel_id=1, source_target_pairs={{0,3},{1,2},{2,1},{3,0},{32,736},{33,737},{34,738},{35,739},{64,67... | collective-permute-start | bytes 2949128 | tf_op jit(solution)/shard_map/ppermute | solution.py:171
  19.1 2.2 %shard_map.95 = (f32[3,260,128]{2,1,0:T(8,128)S(1)}, f32[3,260,128]{2,1,0:T(8,128)S(1)}, f32[3,624,128]{2,1,0:T(8,128)S(1)}) custom-call(s32[2]{0:T(128)S(1)} %bitcast.74, f32[1248,128]{1,0:T(8,128)S(1)} %bitcast.71, f32[1248,128]{1,0:T(8,128)S(1)} %bitcast.72, f32[1248,128]{1,0:T(8,128)S(1)} %bitcast.73), custom_call_target="tpu_custom_call" | custom-call | flops 1000000 | bytes 16000000 | tf_op jit(solution)/shard_map/pallas_call | solution.py:235
  21.2 6.2 %collective-permute-done.1 = f32[24,8,1280]{2,1,0:T(8,128)S(1)} collective-permute-done((f32[24,8,1280]{2,1,0:T(8,128)S(1)}, f32[24,8,1280]{2,1,0:T(8,128)S(1)}, u32[]{:S(2)}, u32[]{:S(2)}) %collective-permute-start.1) | collective-permute-done | bytes 983072 | tf_op jit(solution)/shard_map/ppermute | solution.py:171
  27.5 0.2 slice_add_fusion.6
  27.6 4.7 %collective-permute-start.2 = (f32[12,8,1280]{2,1,0:T(8,128)S(1)}, f32[12,8,1280]{2,1,0:T(8,128)S(1)}, u32[]{:S(2)}, u32[]{:S(2)}) collective-permute-start(f32[12,8,1280]{2,1,0:T(8,128)S(1)} %get-tuple-element.29), channel_id=1, source_target_pairs={{0,3},{1,2},{2,1},{3,0},{32,736},{33,737},{34,738},{35,739},{64,67... | collective-permute-start | bytes 1474568 | tf_op jit(solution)/shard_map/ppermute | solution.py:176
  32.3 0.1 slice_add_fusion.2
  32.4 2.1 %collective-permute-start.5 = (f32[12,8,1280]{2,1,0:T(8,128)S(1)}, f32[12,8,1280]{2,1,0:T(8,128)S(1)}, u32[]{:S(2)}, u32[]{:S(2)}) collective-permute-start(f32[12,8,1280]{2,1,0:T(8,128)S(1)} %slice_add_fusion.2), channel_id=1, source_target_pairs={{0,1},{1,0},{2,3},{3,2},{32,96},{33,97},{34,98},{35,99},{64,65},{6... | collective-permute-start | bytes 1474568 | tf_op jit(solution)/shard_map/ppermute | solution.py:176
  34.5 5.0 %collective-permute-done.2 = f32[12,8,1280]{2,1,0:T(8,128)S(1)} collective-permute-done((f32[12,8,1280]{2,1,0:T(8,128)S(1)}, f32[12,8,1280]{2,1,0:T(8,128)S(1)}, u32[]{:S(2)}, u32[]{:S(2)}) %collective-permute-start.2) | collective-permute-done | bytes 491552 | tf_op jit(solution)/shard_map/ppermute | solution.py:176
  39.6 0.1 add.74
  39.7 3.4 %collective-permute-done.5 = f32[12,8,1280]{2,1,0:T(8,128)S(1)} collective-permute-done((f32[12,8,1280]{2,1,0:T(8,128)S(1)}, f32[12,8,1280]{2,1,0:T(8,128)S(1)}, u32[]{:S(2)}, u32[]{:S(2)}) %collective-permute-start.5) | collective-permute-done | bytes 491552 | tf_op jit(solution)/shard_map/ppermute | solution.py:176
  43.1 0.1 fusion
  43.3 14.6 %collective-permute-start.6 = (f32[2,3,8,1280]{3,2,0,1:T(8,128)S(1)}, f32[2,3,8,1280]{3,2,0,1:T(8,128)S(1)}, u32[]{:S(2)}, u32[]{:S(2)}) collective-permute-start(f32[2,3,8,1280]{3,2,0,1:T(8,128)S(1)} %copy.13), channel_id=1, source_target_pairs={{0,704},{1,705},{2,706},{3,707},{32,35},{33,34},{34,33},{35,32},{6... | collective-permute-start | bytes 737288 | tf_op jit(solution)/shard_map/ppermute | solution.py:178
  58.0 1.9 %collective-permute-start.7 = (f32[2,3,8,1280]{3,2,0,1:T(8,128)S(1)}, f32[2,3,8,1280]{3,2,0,1:T(8,128)S(1)}, u32[]{:S(2)}, u32[]{:S(2)}) collective-permute-start(f32[2,3,8,1280]{3,2,0,1:T(8,128)S(1)} %copy.14), channel_id=1, source_target_pairs={{0,64},{1,65},{2,66},{3,67},{32,33},{33,32},{34,35},{35,34},{64,0}... | collective-permute-start | bytes 737288 | tf_op jit(solution)/shard_map/ppermute | solution.py:178
  59.9 1.9 %collective-permute-start.8 = (f32[2,3,8,1280]{3,2,0,1:T(8,128)S(1)}, f32[2,3,8,1280]{3,2,0,1:T(8,128)S(1)}, u32[]{:S(2)}, u32[]{:S(2)}) collective-permute-start(f32[2,3,8,1280]{3,2,0,1:T(8,128)S(1)} %copy.15), channel_id=1, source_target_pairs={{0,128},{1,129},{2,130},{3,131},{32,34},{33,35},{34,32},{35,33},{6... | collective-permute-start | bytes 737288 | tf_op jit(solution)/shard_map/ppermute | solution.py:178
  61.9 0.2 collective-permute-done.6
  62.1 4.0 %collective-permute-done.7 = f32[2,3,8,1280]{3,2,0,1:T(8,128)S(1)} collective-permute-done((f32[2,3,8,1280]{3,2,0,1:T(8,128)S(1)}, f32[2,3,8,1280]{3,2,0,1:T(8,128)S(1)}, u32[]{:S(2)}, u32[]{:S(2)}) %collective-permute-start.7) | collective-permute-done | bytes 245792 | tf_op jit(solution)/shard_map/ppermute | solution.py:178
  66.1 4.1 %collective-permute-done.8 = f32[2,3,8,1280]{3,2,0,1:T(8,128)S(1)} collective-permute-done((f32[2,3,8,1280]{3,2,0,1:T(8,128)S(1)}, f32[2,3,8,1280]{3,2,0,1:T(8,128)S(1)}, u32[]{:S(2)}, u32[]{:S(2)}) %collective-permute-start.8) | collective-permute-done | bytes 245792 | tf_op jit(solution)/shard_map/ppermute | solution.py:178
  70.1 0.1 fusion.1
  70.2 4.8 %collective-permute-start.10 = (f32[2,8,1280]{2,1,0:T(8,128)S(1)}, f32[2,8,1280]{2,1,0:T(8,128)S(1)}, u32[]{:S(2)}, u32[]{:S(2)}) collective-permute-start(f32[2,8,1280]{2,1,0:T(8,128)S(1)} %get-tuple-element.36), channel_id=1, source_target_pairs={{0,512},{32,544},{64,576},{96,608},{128,640},{160,672},{192,704},{... | collective-permute-start | bytes 245768 | tf_op jit(solution)/shard_map/ppermute | solution.py:189
  75.0 4.9 %collective-permute-start.9 = (f32[2,8,1280]{2,1,0:T(8,128)S(1)}, f32[2,8,1280]{2,1,0:T(8,128)S(1)}, u32[]{:S(2)}, u32[]{:S(2)}) collective-permute-start(f32[2,8,1280]{2,1,0:T(8,128)S(1)} %get-tuple-element.35), channel_id=1, source_target_pairs={{0,256},{32,288},{64,320},{96,352},{128,384},{160,416},{192,448},{... | collective-permute-start | bytes 245768 | tf_op jit(solution)/shard_map/ppermute | solution.py:189
  80.0 1.9 %collective-permute-start.11 = (f32[3,260,128]{2,1,0:T(8,128)S(1)}, f32[3,260,128]{2,1,0:T(8,128)S(1)}, u32[]{:S(2)}, u32[]{:S(2)}) collective-permute-start(f32[3,260,128]{2,1,0:T(8,128)S(1)} %get-tuple-element.38), channel_id=1, source_target_pairs={{0,32},{32,0},{64,96},{96,64},{128,160},{160,128},{192,224},{224,1... | collective-permute-start | bytes 1198088 | tf_op jit(solution)/shard_map/ppermute | solution.py:185
  81.9 0.7 collective-permute-start.12
  82.6 3.3 %collective-permute-done.9 = f32[2,8,1280]{2,1,0:T(8,128)S(1)} collective-permute-done((f32[2,8,1280]{2,1,0:T(8,128)S(1)}, f32[2,8,1280]{2,1,0:T(8,128)S(1)}, u32[]{:S(2)}, u32[]{:S(2)}) %collective-permute-start.9) | collective-permute-done | bytes 81952 | tf_op jit(solution)/shard_map/ppermute | solution.py:189
  85.9 12.6 %all-gather = f32[8,8,1280]{2,1,0:T(8,128)S(1)} all-gather(f32[2,8,1280]{2,1,0:T(8,128)S(1)} %add_add_fusion), channel_id=2, replica_groups=mesh['dp'=24,'mp'=8,'rep'=4] {'rep'}, dimensions={0}, use_global_device_ids=true | all-gather | bytes 409600 | tf_op jit(solution)/shard_map/all_gather | solution.py:190
  98.5 1.9 %shard_map.96 = (f32[624,128]{1,0:T(8,128)}, f32[624,128]{1,0:T(8,128)}, f32[624,128]{1,0:T(8,128)}) custom-call(s32[2]{0:T(128)S(1)} %bitcast.75, f32[4,2,8,1280]{3,2,1,0:T(8,128)S(1)} %bitcast.70, f32[3,624,128]{2,1,0:T(8,128)S(1)} %get-tuple-element.37.own_ref, f32[3,260,128]{2,1,0:T(8,128)S(1)} %collective-permute-done.11.inner_ref, ...), custom_call_target="tpu_custom_call" | custom-call | flops 2000000 | bytes 3000000 | tf_op jit(solution)/shard_map/pallas_call | solution.py:286
  (24 shorter events, 0.2 us)
Async XLA Ops:
  5.3 5.9 %collective-permute-start = (f32[48,8,1280]{2,1,0:T(8,128)S(1)}, f32[48,8,1280]{2,1,0:T(8,128)S(1)}, u32[]{:S(2)}, u32[]{:S(2)}) collective-permute-start(f32[48,8,1280]{2,1,0:T(8,128)S(1)} %get-tuple-element.24), channel_id=1, source_target_pairs={{0,32},{32,0},{64,96},{96,64},{128,160},{160,128},{192,224},{224,1... | collective-permute-start | bytes 5898248 | tf_op jit(solution)/shard_map/ppermute | solution.py:170
  7.3 7.6 %collective-permute-start.3 = (f32[48,8,1280]{2,1,0:T(8,128)S(1)}, f32[48,8,1280]{2,1,0:T(8,128)S(1)}, u32[]{:S(2)}, u32[]{:S(2)}) collective-permute-start(f32[48,8,1280]{2,1,0:T(8,128)S(1)} %get-tuple-element.31), channel_id=1, source_target_pairs={{0,32},{32,0},{64,96},{96,64},{128,160},{160,128},{192,224},{224,1... | collective-permute-start | bytes 5898248 | tf_op jit(solution)/shard_map/ppermute | solution.py:170
  11.3 7.7 %copy-start = (f32[1,159744]{1,0:T(1,128)S(1)}, f32[1,159744]{1,0:T(1,128)}, u32[]{:S(2)}) copy-start(f32[1,159744]{1,0:T(1,128)} %param.11) | copy-start | bytes 1916932
  11.3 7.7 %copy-start.1 = (f32[1,159744]{1,0:T(1,128)S(1)}, f32[1,159744]{1,0:T(1,128)}, u32[]{:S(2)}) copy-start(f32[1,159744]{1,0:T(1,128)} %param.12) | copy-start | bytes 1916932
  11.3 7.7 %copy-start.2 = (f32[1,159744]{1,0:T(1,128)S(1)}, f32[1,159744]{1,0:T(1,128)}, u32[]{:S(2)}) copy-start(f32[1,159744]{1,0:T(1,128)} %param.13) | copy-start | bytes 1916932
  11.3 7.7 %copy-start.3 = (s32[1,1,2]{2,1,0:T(1,128)S(1)}, s32[1,1,2]{2,1,0:T(1,128)}, u32[]{:S(2)}) copy-start(s32[1,1,2]{2,1,0:T(1,128)} %param.10) | copy-start | bytes 28
  11.4 16.1 %collective-permute-start.1 = (f32[24,8,1280]{2,1,0:T(8,128)S(1)}, f32[24,8,1280]{2,1,0:T(8,128)S(1)}, u32[]{:S(2)}, u32[]{:S(2)}) collective-permute-start(f32[24,8,1280]{2,1,0:T(8,128)S(1)} %slice_add_fusion.1), channel_id=1, source_target_pairs={{0,1},{1,0},{2,3},{3,2},{32,96},{33,97},{34,98},{35,99},{64,65},{6... | collective-permute-start | bytes 2949128 | tf_op jit(solution)/shard_map/ppermute | solution.py:171
  15.0 17.3 %collective-permute-start.4 = (f32[24,8,1280]{2,1,0:T(8,128)S(1)}, f32[24,8,1280]{2,1,0:T(8,128)S(1)}, u32[]{:S(2)}, u32[]{:S(2)}) collective-permute-start(f32[24,8,1280]{2,1,0:T(8,128)S(1)} %slice_add_fusion), channel_id=1, source_target_pairs={{0,3},{1,2},{2,1},{3,0},{32,736},{33,737},{34,738},{35,739},{64,67... | collective-permute-start | bytes 2949128 | tf_op jit(solution)/shard_map/ppermute | solution.py:171
  27.6 11.9 %collective-permute-start.2 = (f32[12,8,1280]{2,1,0:T(8,128)S(1)}, f32[12,8,1280]{2,1,0:T(8,128)S(1)}, u32[]{:S(2)}, u32[]{:S(2)}) collective-permute-start(f32[12,8,1280]{2,1,0:T(8,128)S(1)} %get-tuple-element.29), channel_id=1, source_target_pairs={{0,3},{1,2},{2,1},{3,0},{32,736},{33,737},{34,738},{35,739},{64,67... | collective-permute-start | bytes 1474568 | tf_op jit(solution)/shard_map/ppermute | solution.py:176
  32.4 10.7 %collective-permute-start.5 = (f32[12,8,1280]{2,1,0:T(8,128)S(1)}, f32[12,8,1280]{2,1,0:T(8,128)S(1)}, u32[]{:S(2)}, u32[]{:S(2)}) collective-permute-start(f32[12,8,1280]{2,1,0:T(8,128)S(1)} %slice_add_fusion.2), channel_id=1, source_target_pairs={{0,1},{1,0},{2,3},{3,2},{32,96},{33,97},{34,98},{35,99},{64,65},{6... | collective-permute-start | bytes 1474568 | tf_op jit(solution)/shard_map/ppermute | solution.py:176
  43.3 18.8 %collective-permute-start.6 = (f32[2,3,8,1280]{3,2,0,1:T(8,128)S(1)}, f32[2,3,8,1280]{3,2,0,1:T(8,128)S(1)}, u32[]{:S(2)}, u32[]{:S(2)}) collective-permute-start(f32[2,3,8,1280]{3,2,0,1:T(8,128)S(1)} %copy.13), channel_id=1, source_target_pairs={{0,704},{1,705},{2,706},{3,707},{32,35},{33,34},{34,33},{35,32},{6... | collective-permute-start | bytes 737288 | tf_op jit(solution)/shard_map/ppermute | solution.py:178
  58.0 8.1 %collective-permute-start.7 = (f32[2,3,8,1280]{3,2,0,1:T(8,128)S(1)}, f32[2,3,8,1280]{3,2,0,1:T(8,128)S(1)}, u32[]{:S(2)}, u32[]{:S(2)}) collective-permute-start(f32[2,3,8,1280]{3,2,0,1:T(8,128)S(1)} %copy.14), channel_id=1, source_target_pairs={{0,64},{1,65},{2,66},{3,67},{32,33},{33,32},{34,35},{35,34},{64,0}... | collective-permute-start | bytes 737288 | tf_op jit(solution)/shard_map/ppermute | solution.py:178
  59.9 10.2 %collective-permute-start.8 = (f32[2,3,8,1280]{3,2,0,1:T(8,128)S(1)}, f32[2,3,8,1280]{3,2,0,1:T(8,128)S(1)}, u32[]{:S(2)}, u32[]{:S(2)}) collective-permute-start(f32[2,3,8,1280]{3,2,0,1:T(8,128)S(1)} %copy.15), channel_id=1, source_target_pairs={{0,128},{1,129},{2,130},{3,131},{32,34},{33,35},{34,32},{35,33},{6... | collective-permute-start | bytes 737288 | tf_op jit(solution)/shard_map/ppermute | solution.py:178
  70.2 12.4 %collective-permute-start.10 = (f32[2,8,1280]{2,1,0:T(8,128)S(1)}, f32[2,8,1280]{2,1,0:T(8,128)S(1)}, u32[]{:S(2)}, u32[]{:S(2)}) collective-permute-start(f32[2,8,1280]{2,1,0:T(8,128)S(1)} %get-tuple-element.36), channel_id=1, source_target_pairs={{0,512},{32,544},{64,576},{96,608},{128,640},{160,672},{192,704},{... | collective-permute-start | bytes 245768 | tf_op jit(solution)/shard_map/ppermute | solution.py:189
  75.0 10.9 %collective-permute-start.9 = (f32[2,8,1280]{2,1,0:T(8,128)S(1)}, f32[2,8,1280]{2,1,0:T(8,128)S(1)}, u32[]{:S(2)}, u32[]{:S(2)}) collective-permute-start(f32[2,8,1280]{2,1,0:T(8,128)S(1)} %get-tuple-element.35), channel_id=1, source_target_pairs={{0,256},{32,288},{64,320},{96,352},{128,384},{160,416},{192,448},{... | collective-permute-start | bytes 245768 | tf_op jit(solution)/shard_map/ppermute | solution.py:189
  80.0 18.6 %collective-permute-start.11 = (f32[3,260,128]{2,1,0:T(8,128)S(1)}, f32[3,260,128]{2,1,0:T(8,128)S(1)}, u32[]{:S(2)}, u32[]{:S(2)}) collective-permute-start(f32[3,260,128]{2,1,0:T(8,128)S(1)} %get-tuple-element.38), channel_id=1, source_target_pairs={{0,32},{32,0},{64,96},{96,64},{128,160},{160,128},{192,224},{224,1... | collective-permute-start | bytes 1198088 | tf_op jit(solution)/shard_map/ppermute | solution.py:185
  81.9 16.6 %collective-permute-start.12 = (f32[3,260,128]{2,1,0:T(8,128)S(1)}, f32[3,260,128]{2,1,0:T(8,128)S(1)}, u32[]{:S(2)}, u32[]{:S(2)}) collective-permute-start(f32[3,260,128]{2,1,0:T(8,128)S(1)} %get-tuple-element.39), channel_id=1, source_target_pairs={{32,64},{64,32},{96,128},{128,96},{160,192},{192,160},{224,256},{2... | collective-permute-start | bytes 1198088 | tf_op jit(solution)/shard_map/ppermute | solution.py:186

commit v6 on v5

--- a/solution.py
+++ b/solution.py
@@ -172,7 +172,9 @@
         held.append([own[c][i : i + 12] + got[i : i + 12] + far[i : i + 12] for i in (0, 12)])
         if c == 0:
             inner, outer, state = windows(bounds, old)
-            *held[0], inner, outer, state = lax.optimization_barrier((*held[0], inner, outer, state))
+            inner = lax.ppermute(inner, "dp", swap)
+            *held[0], outer, state = lax.optimization_barrier((*held[0], outer, state))
+    *held[1], inner = lax.optimization_barrier((*held[1], inner))
     held = [held[c][0] + lax.ppermute(held[c][1], axes, pairs(*second[c])) for c in range(2)]
     got = [
         lax.ppermute(jnp.stack([h[3 * i : 3 * i + 3] for h in held]), axes, pairs(*to))
@@ -181,8 +183,7 @@
     rest = [
         jnp.stack([h[i] for h in held]) + got[0][:, i] + got[1][:, i] + got[2][:, i] for i in range(3)
     ]
-    *rest, inner, outer = lax.optimization_barrier((*rest, inner, outer))
-    inner = lax.ppermute(inner, "dp", swap)
+    *rest, outer = lax.optimization_barrier((*rest, outer))
     outer = lax.ppermute(outer, "dp", [(i, i + 1 if i % 2 else i - 1) for i in range(1, SHARDS - 1)])
     ahead = [(i, (i + 8) % SHARDS) for i in range(SHARDS)]
     behind = [(i, (i - 8) % SHARDS) for i in range(SHARDS)]

time: 101 us -> 99.1 us (0.981)
  waiting for transfers between devices: 27.8 us -> 21.5 us
  starting transfers between devices: 49.5 us -> 53.7 us
    ppermute x1, starting transfers between devices: 1.92 us -> 11.4 us  [reduced(): inner = lax.ppermute(inner, 'dp', swap)]
    ppermute x2, waiting for transfers between devices: 6.24 us -> 0.01 us  [reduced(): far = lax.ppermute(own[c][24:] + got[24:], axes, pairs(*first[c]))]
    ppermute x3, starting transfers between devices: 18.4 us -> 13.2 us  [reduced(): lax.ppermute(jnp.stack([h[3 * i:3 * i + 3] for h in held]), axes, pairs(*...]
    ppermute x1, starting transfers between devices: 4.94 us -> 2.96 us  [reduced(): lax.ppermute(rest[1], 'dp', ahead)]
    ppermute x1, starting transfers between devices: 4.81 us -> 6.79 us  [reduced(): lax.ppermute(rest[2], 'dp', behind)]
    ppermute x1, waiting for transfers between devices: 3.33 us -> 2.32 us  [reduced(): lax.ppermute(rest[1], 'dp', ahead)]
where the time goes in v6:
time: 99.1 us; the launch traced here: 98.6 us
  starting transfers between devices  53.7 us (54%)
  waiting for transfers between devices  21.5 us (22%)
  blocking collectives  12.7 us (13%)
  Pallas kernels  8.13 us (8%)
  between operations  1.59 us (2%)
    ppermute x3, starting transfers between devices, reduced(): lax.ppermute(jnp.stack([h[3 * i:3 * i + 3] for h in held]), axes, pairs(*...  13.2 us
    all_gather x1, blocking collectives, reduced(): lax.all_gather(mine, 'rep', axis=0, tiled=False)  12.7 us
    ppermute x1, starting transfers between devices, reduced(): inner = lax.ppermute(inner, 'dp', swap)  11.4 us
    ppermute x2, waiting for transfers between devices, reduced(): lax.ppermute(held[c][1], axes, pairs(*second[c]))  8.48 us
    ppermute x3, waiting for transfers between devices, reduced(): lax.ppermute(jnp.stack([h[3 * i:3 * i + 3] for h in held]), axes, pairs(*...  8.25 us
    ppermute x2, starting transfers between devices, reduced(): far = lax.ppermute(own[c][24:] + got[24:], axes, pairs(*first[c]))  7.54 us
    ppermute x2, starting transfers between devices, reduced(): lax.ppermute(held[c][1], axes, pairs(*second[c]))  6.79 us
    ppermute x1, starting transfers between devices, reduced(): lax.ppermute(rest[2], 'dp', behind)  6.79 us
  transfers between devices with their start and end apart: 13, of which 8 were waited for; matrix products, arithmetic and copies ran while one was open for 1% of the time, Pallas kernels for 2%

profile of v6, /device:TPU:56, one launch (start us, length us, event | category | flops | bytes accessed | tf_op | source)
XLA Modules:
  0.0 98.6 jit_solution(15067395424881940144)
XLA Ops:
  1.3 4.0 %shard_map.94 = (f32[48,8,1280]{2,1,0:T(8,128)S(1)}, f32[48,8,1280]{2,1,0:T(8,128)S(1)}, f32[48,8,1280]{2,1,0:T(8,128)S(1)}, f32[48,8,1280]{2,1,0:T(8,128)S(1)}) custom-call(s32[1]{0:T(128)} %bitcast.69.count_ref, bf16[256,256]{1,0:T(8,128)(2,1)} %tok_hbm.1, bf16[256,6656]{1,0:T(8,128)(2,1)} %cot_hbm.1), custom_call_target="tpu_custom_call" | custom-call | flops 2000000000 | bytes 11000000 | tf_op jit(solution)/shard_map/pallas_call | solution.py:120
  5.3 1.9 %collective-permute-start = (f32[48,8,1280]{2,1,0:T(8,128)S(1)}, f32[48,8,1280]{2,1,0:T(8,128)S(1)}, u32[]{:S(2)}, u32[]{:S(2)}) collective-permute-start(f32[48,8,1280]{2,1,0:T(8,128)S(1)} %get-tuple-element.25), channel_id=1, source_target_pairs={{0,32},{32,0},{64,96},{96,64},{128,160},{160,128},{192,224},{224,1... | collective-permute-start | bytes 5898248 | tf_op jit(solution)/shard_map/ppermute | solution.py:170
  7.3 2.4 %collective-permute-start.3 = (f32[48,8,1280]{2,1,0:T(8,128)S(1)}, f32[48,8,1280]{2,1,0:T(8,128)S(1)}, u32[]{:S(2)}, u32[]{:S(2)}) collective-permute-start(f32[48,8,1280]{2,1,0:T(8,128)S(1)} %get-tuple-element.31), channel_id=1, source_target_pairs={{0,32},{32,0},{64,96},{96,64},{128,160},{160,128},{192,224},{224,1... | collective-permute-start | bytes 5898248 | tf_op jit(solution)/shard_map/ppermute | solution.py:170
  9.7 1.5 %collective-permute-done = f32[48,8,1280]{2,1,0:T(8,128)S(1)} collective-permute-done((f32[48,8,1280]{2,1,0:T(8,128)S(1)}, f32[48,8,1280]{2,1,0:T(8,128)S(1)}, u32[]{:S(2)}, u32[]{:S(2)}) %collective-permute-start) | collective-permute-done | bytes 1966112 | tf_op jit(solution)/shard_map/ppermute | solution.py:170
  11.2 0.1 slice_add_fusion.1
  11.4 3.5 %collective-permute-start.1 = (f32[24,8,1280]{2,1,0:T(8,128)S(1)}, f32[24,8,1280]{2,1,0:T(8,128)S(1)}, u32[]{:S(2)}, u32[]{:S(2)}) collective-permute-start(f32[24,8,1280]{2,1,0:T(8,128)S(1)} %slice_add_fusion.1), channel_id=1, source_target_pairs={{0,1},{1,0},{2,3},{3,2},{32,96},{33,97},{34,98},{35,99},{64,65},{6... | collective-permute-start | bytes 2949128 | tf_op jit(solution)/shard_map/ppermute | solution.py:171
  14.9 0.1 slice_add_fusion
  15.0 4.0 %collective-permute-start.4 = (f32[24,8,1280]{2,1,0:T(8,128)S(1)}, f32[24,8,1280]{2,1,0:T(8,128)S(1)}, u32[]{:S(2)}, u32[]{:S(2)}) collective-permute-start(f32[24,8,1280]{2,1,0:T(8,128)S(1)} %slice_add_fusion), channel_id=1, source_target_pairs={{0,3},{1,2},{2,1},{3,0},{32,736},{33,737},{34,738},{35,739},{64,67... | collective-permute-start | bytes 2949128 | tf_op jit(solution)/shard_map/ppermute | solution.py:171
  19.1 2.2 %shard_map.95 = (f32[3,260,128]{2,1,0:T(8,128)S(1)}, f32[3,260,128]{2,1,0:T(8,128)S(1)}, f32[3,624,128]{2,1,0:T(8,128)S(1)}) custom-call(s32[2]{0:T(128)S(1)} %bitcast.74, f32[1248,128]{1,0:T(8,128)S(1)} %bitcast.71, f32[1248,128]{1,0:T(8,128)S(1)} %bitcast.72, f32[1248,128]{1,0:T(8,128)S(1)} %bitcast.73), custom_call_target="tpu_custom_call" | custom-call | flops 1000000 | bytes 16000000 | tf_op jit(solution)/shard_map/pallas_call | solution.py:236
  21.2 11.4 %collective-permute-start.5 = (f32[3,260,128]{2,1,0:T(8,128)S(1)}, f32[3,260,128]{2,1,0:T(8,128)S(1)}, u32[]{:S(2)}, u32[]{:S(2)}) collective-permute-start(f32[3,260,128]{2,1,0:T(8,128)S(1)} %get-tuple-element.32), channel_id=1, source_target_pairs={{0,32},{32,0},{64,96},{96,64},{128,160},{160,128},{192,224},{224,1... | collective-permute-start | bytes 1198088 | tf_op jit(solution)/shard_map/ppermute | solution.py:175
  32.7 0.2 slice_add_fusion.6
  32.9 4.7 %collective-permute-start.2 = (f32[12,8,1280]{2,1,0:T(8,128)S(1)}, f32[12,8,1280]{2,1,0:T(8,128)S(1)}, u32[]{:S(2)}, u32[]{:S(2)}) collective-permute-start(f32[12,8,1280]{2,1,0:T(8,128)S(1)} %get-tuple-element.29), channel_id=1, source_target_pairs={{0,3},{1,2},{2,1},{3,0},{32,736},{33,737},{34,738},{35,739},{64,67... | collective-permute-start | bytes 1474568 | tf_op jit(solution)/shard_map/ppermute | solution.py:178
  37.5 0.2 slice_add_fusion.2
  37.7 2.1 %collective-permute-start.6 = (f32[12,8,1280]{2,1,0:T(8,128)S(1)}, f32[12,8,1280]{2,1,0:T(8,128)S(1)}, u32[]{:S(2)}, u32[]{:S(2)}) collective-permute-start(f32[12,8,1280]{2,1,0:T(8,128)S(1)} %get-tuple-element.34), channel_id=1, source_target_pairs={{0,1},{1,0},{2,3},{3,2},{32,96},{33,97},{34,98},{35,99},{64,65},{6... | collective-permute-start | bytes 1474568 | tf_op jit(solution)/shard_map/ppermute | solution.py:178
  39.9 4.9 %collective-permute-done.2 = f32[12,8,1280]{2,1,0:T(8,128)S(1)} collective-permute-done((f32[12,8,1280]{2,1,0:T(8,128)S(1)}, f32[12,8,1280]{2,1,0:T(8,128)S(1)}, u32[]{:S(2)}, u32[]{:S(2)}) %collective-permute-start.2) | collective-permute-done | bytes 491552 | tf_op jit(solution)/shard_map/ppermute | solution.py:178
  44.8 0.1 add.74
  44.9 3.5 %collective-permute-done.6 = f32[12,8,1280]{2,1,0:T(8,128)S(1)} collective-permute-done((f32[12,8,1280]{2,1,0:T(8,128)S(1)}, f32[12,8,1280]{2,1,0:T(8,128)S(1)}, u32[]{:S(2)}, u32[]{:S(2)}) %collective-permute-start.6) | collective-permute-done | bytes 491552 | tf_op jit(solution)/shard_map/ppermute | solution.py:178
  48.4 0.1 add.80
  48.6 9.4 %collective-permute-start.7 = (f32[2,3,8,1280]{3,2,0,1:T(8,128)S(1)}, f32[2,3,8,1280]{3,2,0,1:T(8,128)S(1)}, u32[]{:S(2)}, u32[]{:S(2)}) collective-permute-start(f32[2,3,8,1280]{3,2,0,1:T(8,128)S(1)} %copy.13), channel_id=1, source_target_pairs={{0,704},{1,705},{2,706},{3,707},{32,35},{33,34},{34,33},{35,32},{6... | collective-permute-start | bytes 737288 | tf_op jit(solution)/shard_map/ppermute | solution.py:180
  58.0 1.9 %collective-permute-start.8 = (f32[2,3,8,1280]{3,2,0,1:T(8,128)S(1)}, f32[2,3,8,1280]{3,2,0,1:T(8,128)S(1)}, u32[]{:S(2)}, u32[]{:S(2)}) collective-permute-start(f32[2,3,8,1280]{3,2,0,1:T(8,128)S(1)} %copy.14), channel_id=1, source_target_pairs={{0,64},{1,65},{2,66},{3,67},{32,33},{33,32},{34,35},{35,34},{64,0}... | collective-permute-start | bytes 737288 | tf_op jit(solution)/shard_map/ppermute | solution.py:180
  60.0 1.9 %collective-permute-start.9 = (f32[2,3,8,1280]{3,2,0,1:T(8,128)S(1)}, f32[2,3,8,1280]{3,2,0,1:T(8,128)S(1)}, u32[]{:S(2)}, u32[]{:S(2)}) collective-permute-start(f32[2,3,8,1280]{3,2,0,1:T(8,128)S(1)} %copy.15), channel_id=1, source_target_pairs={{0,128},{1,129},{2,130},{3,131},{32,34},{33,35},{34,32},{35,33},{6... | collective-permute-start | bytes 737288 | tf_op jit(solution)/shard_map/ppermute | solution.py:180
  61.9 0.2 collective-permute-done.7
  62.1 4.0 %collective-permute-done.8 = f32[2,3,8,1280]{3,2,0,1:T(8,128)S(1)} collective-permute-done((f32[2,3,8,1280]{3,2,0,1:T(8,128)S(1)}, f32[2,3,8,1280]{3,2,0,1:T(8,128)S(1)}, u32[]{:S(2)}, u32[]{:S(2)}) %collective-permute-start.8) | collective-permute-done | bytes 245792 | tf_op jit(solution)/shard_map/ppermute | solution.py:180
  66.1 4.1 %collective-permute-done.9 = f32[2,3,8,1280]{3,2,0,1:T(8,128)S(1)} collective-permute-done((f32[2,3,8,1280]{3,2,0,1:T(8,128)S(1)}, f32[2,3,8,1280]{3,2,0,1:T(8,128)S(1)}, u32[]{:S(2)}, u32[]{:S(2)}) %collective-permute-start.9) | collective-permute-done | bytes 245792 | tf_op jit(solution)/shard_map/ppermute | solution.py:180
  70.2 0.1 fusion
  70.3 3.0 %collective-permute-start.10 = (f32[2,8,1280]{2,1,0:T(8,128)S(1)}, f32[2,8,1280]{2,1,0:T(8,128)S(1)}, u32[]{:S(2)}, u32[]{:S(2)}) collective-permute-start(f32[2,8,1280]{2,1,0:T(8,128)S(1)} %get-tuple-element.37), channel_id=1, source_target_pairs={{0,256},{32,288},{64,320},{96,352},{128,384},{160,416},{192,448},{... | collective-permute-start | bytes 245768 | tf_op jit(solution)/shard_map/ppermute | solution.py:190
  73.2 6.8 %collective-permute-start.11 = (f32[2,8,1280]{2,1,0:T(8,128)S(1)}, f32[2,8,1280]{2,1,0:T(8,128)S(1)}, u32[]{:S(2)}, u32[]{:S(2)}) collective-permute-start(f32[2,8,1280]{2,1,0:T(8,128)S(1)} %get-tuple-element.38), channel_id=1, source_target_pairs={{0,512},{32,544},{64,576},{96,608},{128,640},{160,672},{192,704},{... | collective-permute-start | bytes 245768 | tf_op jit(solution)/shard_map/ppermute | solution.py:190
  80.0 0.7 collective-permute-start.12
  80.7 2.3 %collective-permute-done.10 = f32[2,8,1280]{2,1,0:T(8,128)S(1)} collective-permute-done((f32[2,8,1280]{2,1,0:T(8,128)S(1)}, f32[2,8,1280]{2,1,0:T(8,128)S(1)}, u32[]{:S(2)}, u32[]{:S(2)}) %collective-permute-start.10) | collective-permute-done | bytes 81952 | tf_op jit(solution)/shard_map/ppermute | solution.py:190
  83.0 0.9 collective-permute-done.11
  83.9 12.7 %all-gather = f32[8,8,1280]{2,1,0:T(8,128)S(1)} all-gather(f32[2,8,1280]{2,1,0:T(8,128)S(1)} %add_add_fusion), channel_id=2, replica_groups=mesh['dp'=24,'mp'=8,'rep'=4] {'rep'}, dimensions={0}, use_global_device_ids=true | all-gather | bytes 409600 | tf_op jit(solution)/shard_map/all_gather | solution.py:191
  96.7 1.9 %shard_map.96 = (f32[624,128]{1,0:T(8,128)}, f32[624,128]{1,0:T(8,128)}, f32[624,128]{1,0:T(8,128)}) custom-call(s32[2]{0:T(128)S(1)} %bitcast.75, f32[4,2,8,1280]{3,2,1,0:T(8,128)S(1)} %bitcast.70, f32[3,624,128]{2,1,0:T(8,128)S(1)} %get-tuple-element.39.own_ref, f32[3,260,128]{2,1,0:T(8,128)S(1)} %collective-permute-done.5.inner_ref, ...), custom_call_target="tpu_custom_call" | custom-call | flops 2000000 | bytes 3000000 | tf_op jit(solution)/shard_map/pallas_call | solution.py:287
  (24 shorter events, 0.3 us)
Async XLA Ops:
  5.3 5.9 %collective-permute-start = (f32[48,8,1280]{2,1,0:T(8,128)S(1)}, f32[48,8,1280]{2,1,0:T(8,128)S(1)}, u32[]{:S(2)}, u32[]{:S(2)}) collective-permute-start(f32[48,8,1280]{2,1,0:T(8,128)S(1)} %get-tuple-element.25), channel_id=1, source_target_pairs={{0,32},{32,0},{64,96},{96,64},{128,160},{160,128},{192,224},{224,1... | collective-permute-start | bytes 5898248 | tf_op jit(solution)/shard_map/ppermute | solution.py:170
  7.3 7.6 %collective-permute-start.3 = (f32[48,8,1280]{2,1,0:T(8,128)S(1)}, f32[48,8,1280]{2,1,0:T(8,128)S(1)}, u32[]{:S(2)}, u32[]{:S(2)}) collective-permute-start(f32[48,8,1280]{2,1,0:T(8,128)S(1)} %get-tuple-element.31), channel_id=1, source_target_pairs={{0,32},{32,0},{64,96},{96,64},{128,160},{160,128},{192,224},{224,1... | collective-permute-start | bytes 5898248 | tf_op jit(solution)/shard_map/ppermute | solution.py:170
  11.3 7.7 %copy-start = (f32[1,159744]{1,0:T(1,128)S(1)}, f32[1,159744]{1,0:T(1,128)}, u32[]{:S(2)}) copy-start(f32[1,159744]{1,0:T(1,128)} %param.11) | copy-start | bytes 1916932
  11.3 7.7 %copy-start.1 = (f32[1,159744]{1,0:T(1,128)S(1)}, f32[1,159744]{1,0:T(1,128)}, u32[]{:S(2)}) copy-start(f32[1,159744]{1,0:T(1,128)} %param.12) | copy-start | bytes 1916932
  11.3 7.7 %copy-start.2 = (f32[1,159744]{1,0:T(1,128)S(1)}, f32[1,159744]{1,0:T(1,128)}, u32[]{:S(2)}) copy-start(f32[1,159744]{1,0:T(1,128)} %param.13) | copy-start | bytes 1916932
  11.3 7.7 %copy-start.3 = (s32[1,1,2]{2,1,0:T(1,128)S(1)}, s32[1,1,2]{2,1,0:T(1,128)}, u32[]{:S(2)}) copy-start(s32[1,1,2]{2,1,0:T(1,128)} %param.10) | copy-start | bytes 28
  11.4 21.3 %collective-permute-start.1 = (f32[24,8,1280]{2,1,0:T(8,128)S(1)}, f32[24,8,1280]{2,1,0:T(8,128)S(1)}, u32[]{:S(2)}, u32[]{:S(2)}) collective-permute-start(f32[24,8,1280]{2,1,0:T(8,128)S(1)} %slice_add_fusion.1), channel_id=1, source_target_pairs={{0,1},{1,0},{2,3},{3,2},{32,96},{33,97},{34,98},{35,99},{64,65},{6... | collective-permute-start | bytes 2949128 | tf_op jit(solution)/shard_map/ppermute | solution.py:171
  15.0 22.5 %collective-permute-start.4 = (f32[24,8,1280]{2,1,0:T(8,128)S(1)}, f32[24,8,1280]{2,1,0:T(8,128)S(1)}, u32[]{:S(2)}, u32[]{:S(2)}) collective-permute-start(f32[24,8,1280]{2,1,0:T(8,128)S(1)} %slice_add_fusion), channel_id=1, source_target_pairs={{0,3},{1,2},{2,1},{3,0},{32,736},{33,737},{34,738},{35,739},{64,67... | collective-permute-start | bytes 2949128 | tf_op jit(solution)/shard_map/ppermute | solution.py:171
  21.2 16.5 %collective-permute-start.5 = (f32[3,260,128]{2,1,0:T(8,128)S(1)}, f32[3,260,128]{2,1,0:T(8,128)S(1)}, u32[]{:S(2)}, u32[]{:S(2)}) collective-permute-start(f32[3,260,128]{2,1,0:T(8,128)S(1)} %get-tuple-element.32), channel_id=1, source_target_pairs={{0,32},{32,0},{64,96},{96,64},{128,160},{160,128},{192,224},{224,1... | collective-permute-start | bytes 1198088 | tf_op jit(solution)/shard_map/ppermute | solution.py:175
  32.9 11.9 %collective-permute-start.2 = (f32[12,8,1280]{2,1,0:T(8,128)S(1)}, f32[12,8,1280]{2,1,0:T(8,128)S(1)}, u32[]{:S(2)}, u32[]{:S(2)}) collective-permute-start(f32[12,8,1280]{2,1,0:T(8,128)S(1)} %get-tuple-element.29), channel_id=1, source_target_pairs={{0,3},{1,2},{2,1},{3,0},{32,736},{33,737},{34,738},{35,739},{64,67... | collective-permute-start | bytes 1474568 | tf_op jit(solution)/shard_map/ppermute | solution.py:178
  37.7 10.7 %collective-permute-start.6 = (f32[12,8,1280]{2,1,0:T(8,128)S(1)}, f32[12,8,1280]{2,1,0:T(8,128)S(1)}, u32[]{:S(2)}, u32[]{:S(2)}) collective-permute-start(f32[12,8,1280]{2,1,0:T(8,128)S(1)} %get-tuple-element.34), channel_id=1, source_target_pairs={{0,1},{1,0},{2,3},{3,2},{32,96},{33,97},{34,98},{35,99},{64,65},{6... | collective-permute-start | bytes 1474568 | tf_op jit(solution)/shard_map/ppermute | solution.py:178
  48.6 13.5 %collective-permute-start.7 = (f32[2,3,8,1280]{3,2,0,1:T(8,128)S(1)}, f32[2,3,8,1280]{3,2,0,1:T(8,128)S(1)}, u32[]{:S(2)}, u32[]{:S(2)}) collective-permute-start(f32[2,3,8,1280]{3,2,0,1:T(8,128)S(1)} %copy.13), channel_id=1, source_target_pairs={{0,704},{1,705},{2,706},{3,707},{32,35},{33,34},{34,33},{35,32},{6... | collective-permute-start | bytes 737288 | tf_op jit(solution)/shard_map/ppermute | solution.py:180
  58.0 8.1 %collective-permute-start.8 = (f32[2,3,8,1280]{3,2,0,1:T(8,128)S(1)}, f32[2,3,8,1280]{3,2,0,1:T(8,128)S(1)}, u32[]{:S(2)}, u32[]{:S(2)}) collective-permute-start(f32[2,3,8,1280]{3,2,0,1:T(8,128)S(1)} %copy.14), channel_id=1, source_target_pairs={{0,64},{1,65},{2,66},{3,67},{32,33},{33,32},{34,35},{35,34},{64,0}... | collective-permute-start | bytes 737288 | tf_op jit(solution)/shard_map/ppermute | solution.py:180
  60.0 10.2 %collective-permute-start.9 = (f32[2,3,8,1280]{3,2,0,1:T(8,128)S(1)}, f32[2,3,8,1280]{3,2,0,1:T(8,128)S(1)}, u32[]{:S(2)}, u32[]{:S(2)}) collective-permute-start(f32[2,3,8,1280]{3,2,0,1:T(8,128)S(1)} %copy.15), channel_id=1, source_target_pairs={{0,128},{1,129},{2,130},{3,131},{32,34},{33,35},{34,32},{35,33},{6... | collective-permute-start | bytes 737288 | tf_op jit(solution)/shard_map/ppermute | solution.py:180
  70.3 12.8 %collective-permute-start.10 = (f32[2,8,1280]{2,1,0:T(8,128)S(1)}, f32[2,8,1280]{2,1,0:T(8,128)S(1)}, u32[]{:S(2)}, u32[]{:S(2)}) collective-permute-start(f32[2,8,1280]{2,1,0:T(8,128)S(1)} %get-tuple-element.37), channel_id=1, source_target_pairs={{0,256},{32,288},{64,320},{96,352},{128,384},{160,416},{192,448},{... | collective-permute-start | bytes 245768 | tf_op jit(solution)/shard_map/ppermute | solution.py:190
  73.2 10.7 %collective-permute-start.11 = (f32[2,8,1280]{2,1,0:T(8,128)S(1)}, f32[2,8,1280]{2,1,0:T(8,128)S(1)}, u32[]{:S(2)}, u32[]{:S(2)}) collective-permute-start(f32[2,8,1280]{2,1,0:T(8,128)S(1)} %get-tuple-element.38), channel_id=1, source_target_pairs={{0,512},{32,544},{64,576},{96,608},{128,640},{160,672},{192,704},{... | collective-permute-start | bytes 245768 | tf_op jit(solution)/shard_map/ppermute | solution.py:190
  80.0 16.6 %collective-permute-start.12 = (f32[3,260,128]{2,1,0:T(8,128)S(1)}, f32[3,260,128]{2,1,0:T(8,128)S(1)}, u32[]{:S(2)}, u32[]{:S(2)}) collective-permute-start(f32[3,260,128]{2,1,0:T(8,128)S(1)} %get-tuple-element.41), channel_id=1, source_target_pairs={{32,64},{64,32},{96,128},{128,96},{160,192},{192,160},{224,256},{2... | collective-permute-start | bytes 1198088 | tf_op jit(solution)/shard_map/ppermute | solution.py:187

commit v7 on v6

--- a/solution.py
+++ b/solution.py
@@ -173,8 +173,9 @@
         if c == 0:
             inner, outer, state = windows(bounds, old)
             inner = lax.ppermute(inner, "dp", swap)
-            *held[0], outer, state = lax.optimization_barrier((*held[0], outer, state))
-    *held[1], inner = lax.optimization_barrier((*held[1], inner))
+            outer = lax.ppermute(outer, "dp", [(i, i + 1 if i % 2 else i - 1) for i in range(1, SHARDS - 1)])
+            *held[0], state = lax.optimization_barrier((*held[0], state))
+    *held[1], inner, outer = lax.optimization_barrier((*held[1], inner, outer))
     held = [held[c][0] + lax.ppermute(held[c][1], axes, pairs(*second[c])) for c in range(2)]
     got = [
         lax.ppermute(jnp.stack([h[3 * i : 3 * i + 3] for h in held]), axes, pairs(*to))
@@ -183,8 +184,6 @@
     rest = [
         jnp.stack([h[i] for h in held]) + got[0][:, i] + got[1][:, i] + got[2][:, i] for i in range(3)
     ]
-    *rest, outer = lax.optimization_barrier((*rest, outer))
-    outer = lax.ppermute(outer, "dp", [(i, i + 1 if i % 2 else i - 1) for i in range(1, SHARDS - 1)])
     ahead = [(i, (i + 8) % SHARDS) for i in range(SHARDS)]
     behind = [(i, (i - 8) % SHARDS) for i in range(SHARDS)]
     mine = rest[0] + lax.ppermute(rest[1], "dp", ahead) + lax.ppermute(rest[2], "dp", behind)

time: 99.1 us -> 106 us (1.070)
  starting transfers between devices: 53.7 us -> 60 us
    ppermute x3, starting transfers between devices: 13.2 us -> 19.5 us  [reduced(): lax.ppermute(jnp.stack([h[3 * i:3 * i + 3] for h in held]), axes, pairs(*...]
    ppermute x1, waiting for transfers between devices: 0.88 us -> 2.04 us  [reduced(): lax.ppermute(rest[2], 'dp', behind)]
where the time goes in v7:
time: 106 us
  starting transfers between devices  60 us (57%)
  waiting for transfers between devices  22.1 us (21%)
  blocking collectives  12.7 us (12%)
  Pallas kernels  8.12 us (8%)
  between operations  1.6 us (2%)
    ppermute x3, starting transfers between devices, reduced(): lax.ppermute(jnp.stack([h[3 * i:3 * i + 3] for h in held]), axes, pairs(*...  19.5 us
    all_gather x1, blocking collectives, reduced(): lax.all_gather(mine, 'rep', axis=0, tiled=False)  12.7 us
    ppermute x1, starting transfers between devices, reduced(): inner = lax.ppermute(inner, 'dp', swap)  11.5 us
    ppermute x2, waiting for transfers between devices, reduced(): lax.ppermute(held[c][1], axes, pairs(*second[c]))  7.82 us
    ppermute x2, starting transfers between devices, reduced(): lax.ppermute(held[c][1], axes, pairs(*second[c]))  7.39 us
    ppermute x3, waiting for transfers between devices, reduced(): lax.ppermute(jnp.stack([h[3 * i:3 * i + 3] for h in held]), axes, pairs(*...  7.37 us
    ppermute x2, starting transfers between devices, reduced(): far = lax.ppermute(own[c][24:] + got[24:], axes, pairs(*first[c]))  6.94 us
    ppermute x1, starting transfers between devices, reduced(): lax.ppermute(rest[2], 'dp', behind)  6.86 us
  transfers between devices with their start and end apart: 13, of which 8 were waited for; matrix products, arithmetic and copies ran while one was open for 1% of the time, Pallas kernels for 2%

profile of v7, /device:TPU:56, one launch (start us, length us, event | category | flops | bytes accessed | tf_op | source)
XLA Modules:
  0.0 105.6 jit_solution(17316983626513277817)
XLA Ops:
  1.3 4.0 %shard_map.94 = (f32[48,8,1280]{2,1,0:T(8,128)S(1)}, f32[48,8,1280]{2,1,0:T(8,128)S(1)}, f32[48,8,1280]{2,1,0:T(8,128)S(1)}, f32[48,8,1280]{2,1,0:T(8,128)S(1)}) custom-call(s32[1]{0:T(128)} %bitcast.73.count_ref, bf16[256,256]{1,0:T(8,128)(2,1)} %tok_hbm.1, bf16[256,6656]{1,0:T(8,128)(2,1)} %cot_hbm.1), custom_call_target="tpu_custom_call" | custom-call | flops 2000000000 | bytes 11000000 | tf_op jit(solution)/shard_map/pallas_call | solution.py:120
  5.3 1.9 %collective-permute-start.3 = (f32[48,8,1280]{2,1,0:T(8,128)S(1)}, f32[48,8,1280]{2,1,0:T(8,128)S(1)}, u32[]{:S(2)}, u32[]{:S(2)}) collective-permute-start(f32[48,8,1280]{2,1,0:T(8,128)S(1)} %get-tuple-element.26), channel_id=1, source_target_pairs={{0,32},{32,0},{64,96},{96,64},{128,160},{160,128},{192,224},{224,1... | collective-permute-start | bytes 5898248 | tf_op jit(solution)/shard_map/ppermute | solution.py:170
  7.3 2.4 %collective-permute-start = (f32[48,8,1280]{2,1,0:T(8,128)S(1)}, f32[48,8,1280]{2,1,0:T(8,128)S(1)}, u32[]{:S(2)}, u32[]{:S(2)}) collective-permute-start(f32[48,8,1280]{2,1,0:T(8,128)S(1)} %get-tuple-element.21), channel_id=1, source_target_pairs={{0,32},{32,0},{64,96},{96,64},{128,160},{160,128},{192,224},{224,1... | collective-permute-start | bytes 5898248 | tf_op jit(solution)/shard_map/ppermute | solution.py:170
  9.7 1.5 %collective-permute-done.3 = f32[48,8,1280]{2,1,0:T(8,128)S(1)} collective-permute-done((f32[48,8,1280]{2,1,0:T(8,128)S(1)}, f32[48,8,1280]{2,1,0:T(8,128)S(1)}, u32[]{:S(2)}, u32[]{:S(2)}) %collective-permute-start.3) | collective-permute-done | bytes 1966112 | tf_op jit(solution)/shard_map/ppermute | solution.py:170
  11.2 0.1 slice_add_fusion
  11.3 0.0 copy-start.2
  11.4 4.8 %collective-permute-start.4 = (f32[24,8,1280]{2,1,0:T(8,128)S(1)}, f32[24,8,1280]{2,1,0:T(8,128)S(1)}, u32[]{:S(2)}, u32[]{:S(2)}) collective-permute-start(f32[24,8,1280]{2,1,0:T(8,128)S(1)} %slice_add_fusion), channel_id=1, source_target_pairs={{0,3},{1,2},{2,1},{3,0},{32,736},{33,737},{34,738},{35,739},{64,67... | collective-permute-start | bytes 2949128 | tf_op jit(solution)/shard_map/ppermute | solution.py:171
  16.2 0.1 slice_add_fusion.1
  16.3 2.1 %collective-permute-start.1 = (f32[24,8,1280]{2,1,0:T(8,128)S(1)}, f32[24,8,1280]{2,1,0:T(8,128)S(1)}, u32[]{:S(2)}, u32[]{:S(2)}) collective-permute-start(f32[24,8,1280]{2,1,0:T(8,128)S(1)} %slice_add_fusion.1), channel_id=1, source_target_pairs={{0,1},{1,0},{2,3},{3,2},{32,96},{33,97},{34,98},{35,99},{64,65},{6... | collective-permute-start | bytes 2949128 | tf_op jit(solution)/shard_map/ppermute | solution.py:171
  18.5 2.2 %shard_map.95 = (f32[3,260,128]{2,1,0:T(8,128)S(1)}, f32[3,260,128]{2,1,0:T(8,128)S(1)}, f32[3,624,128]{2,1,0:T(8,128)S(1)}) custom-call(s32[2]{0:T(128)S(1)} %bitcast.78, f32[1248,128]{1,0:T(8,128)S(1)} %bitcast.75, f32[1248,128]{1,0:T(8,128)S(1)} %bitcast.76, f32[1248,128]{1,0:T(8,128)S(1)} %bitcast.77), custom_call_target="tpu_custom_call" | custom-call | flops 1000000 | bytes 16000000 | tf_op jit(solution)/shard_map/pallas_call | solution.py:235
  20.6 11.5 %collective-permute-start.5 = (f32[3,260,128]{2,1,0:T(8,128)S(1)}, f32[3,260,128]{2,1,0:T(8,128)S(1)}, u32[]{:S(2)}, u32[]{:S(2)}) collective-permute-start(f32[3,260,128]{2,1,0:T(8,128)S(1)} %get-tuple-element.27), channel_id=1, source_target_pairs={{0,32},{32,0},{64,96},{96,64},{128,160},{160,128},{192,224},{224,1... | collective-permute-start | bytes 1198088 | tf_op jit(solution)/shard_map/ppermute | solution.py:175
  32.1 0.7 collective-permute-start.6
  32.8 0.2 slice_add_fusion.2
  33.0 0.4 collective-permute-done.5.inner_ref
  33.5 3.4 %collective-permute-start.7 = (f32[12,8,1280]{2,1,0:T(8,128)S(1)}, f32[12,8,1280]{2,1,0:T(8,128)S(1)}, u32[]{:S(2)}, u32[]{:S(2)}) collective-permute-start(f32[12,8,1280]{2,1,0:T(8,128)S(1)} %get-tuple-element.30), channel_id=1, source_target_pairs={{0,1},{1,0},{2,3},{3,2},{32,96},{33,97},{34,98},{35,99},{64,65},{6... | collective-permute-start | bytes 1474568 | tf_op jit(solution)/shard_map/ppermute | solution.py:179
  36.9 0.2 slice_add_fusion.6
  37.1 4.0 %collective-permute-start.2 = (f32[12,8,1280]{2,1,0:T(8,128)S(1)}, f32[12,8,1280]{2,1,0:T(8,128)S(1)}, u32[]{:S(2)}, u32[]{:S(2)}) collective-permute-start(f32[12,8,1280]{2,1,0:T(8,128)S(1)} %get-tuple-element.24), channel_id=1, source_target_pairs={{0,3},{1,2},{2,1},{3,0},{32,736},{33,737},{34,738},{35,739},{64,67... | collective-permute-start | bytes 1474568 | tf_op jit(solution)/shard_map/ppermute | solution.py:179
  41.1 3.1 %collective-permute-done.7 = f32[12,8,1280]{2,1,0:T(8,128)S(1)} collective-permute-done((f32[12,8,1280]{2,1,0:T(8,128)S(1)}, f32[12,8,1280]{2,1,0:T(8,128)S(1)}, u32[]{:S(2)}, u32[]{:S(2)}) %collective-permute-start.7) | collective-permute-done | bytes 491552 | tf_op jit(solution)/shard_map/ppermute | solution.py:179
  44.2 0.1 add.80
  44.3 4.7 %collective-permute-done.2 = f32[12,8,1280]{2,1,0:T(8,128)S(1)} collective-permute-done((f32[12,8,1280]{2,1,0:T(8,128)S(1)}, f32[12,8,1280]{2,1,0:T(8,128)S(1)}, u32[]{:S(2)}, u32[]{:S(2)}) %collective-permute-start.2) | collective-permute-done | bytes 491552 | tf_op jit(solution)/shard_map/ppermute | solution.py:179
  49.0 0.1 add.74
  49.2 14.8 %collective-permute-start.8 = (f32[2,3,8,1280]{3,2,0,1:T(8,128)S(1)}, f32[2,3,8,1280]{3,2,0,1:T(8,128)S(1)}, u32[]{:S(2)}, u32[]{:S(2)}) collective-permute-start(f32[2,3,8,1280]{3,2,0,1:T(8,128)S(1)} %copy.13), channel_id=1, source_target_pairs={{0,704},{1,705},{2,706},{3,707},{32,35},{33,34},{34,33},{35,32},{6... | collective-permute-start | bytes 737288 | tf_op jit(solution)/shard_map/ppermute | solution.py:181
  64.0 1.9 %collective-permute-start.9 = (f32[2,3,8,1280]{3,2,0,1:T(8,128)S(1)}, f32[2,3,8,1280]{3,2,0,1:T(8,128)S(1)}, u32[]{:S(2)}, u32[]{:S(2)}) collective-permute-start(f32[2,3,8,1280]{3,2,0,1:T(8,128)S(1)} %copy.14), channel_id=1, source_target_pairs={{0,64},{1,65},{2,66},{3,67},{32,33},{33,32},{34,35},{35,34},{64,0}... | collective-permute-start | bytes 737288 | tf_op jit(solution)/shard_map/ppermute | solution.py:181
  66.0 2.8 %collective-permute-start.10 = (f32[2,3,8,1280]{3,2,0,1:T(8,128)S(1)}, f32[2,3,8,1280]{3,2,0,1:T(8,128)S(1)}, u32[]{:S(2)}, u32[]{:S(2)}) collective-permute-start(f32[2,3,8,1280]{3,2,0,1:T(8,128)S(1)} %copy.15), channel_id=1, source_target_pairs={{0,128},{1,129},{2,130},{3,131},{32,34},{33,35},{34,32},{35,33},{6... | collective-permute-start | bytes 737288 | tf_op jit(solution)/shard_map/ppermute | solution.py:181
  68.8 3.3 %collective-permute-done.9 = f32[2,3,8,1280]{3,2,0,1:T(8,128)S(1)} collective-permute-done((f32[2,3,8,1280]{3,2,0,1:T(8,128)S(1)}, f32[2,3,8,1280]{3,2,0,1:T(8,128)S(1)}, u32[]{:S(2)}, u32[]{:S(2)}) %collective-permute-start.9) | collective-permute-done | bytes 245792 | tf_op jit(solution)/shard_map/ppermute | solution.py:181
  72.1 4.1 %collective-permute-done.10 = f32[2,3,8,1280]{3,2,0,1:T(8,128)S(1)} collective-permute-done((f32[2,3,8,1280]{3,2,0,1:T(8,128)S(1)}, f32[2,3,8,1280]{3,2,0,1:T(8,128)S(1)}, u32[]{:S(2)}, u32[]{:S(2)}) %collective-permute-start.10) | collective-permute-done | bytes 245792 | tf_op jit(solution)/shard_map/ppermute | solution.py:181
  76.2 2.9 %collective-permute-start.11 = (f32[2,8,1280]{2,1,0:T(8,128)S(1)}, f32[2,8,1280]{2,1,0:T(8,128)S(1)}, u32[]{:S(2)}, u32[]{:S(2)}) collective-permute-start(f32[2,8,1280]{2,1,0:T(8,128)S(1)} %get-tuple-element.41), channel_id=1, source_target_pairs={{0,256},{32,288},{64,320},{96,352},{128,384},{160,416},{192,448},{... | collective-permute-start | bytes 245768 | tf_op jit(solution)/shard_map/ppermute | solution.py:189
  79.1 6.9 %collective-permute-start.12 = (f32[2,8,1280]{2,1,0:T(8,128)S(1)}, f32[2,8,1280]{2,1,0:T(8,128)S(1)}, u32[]{:S(2)}, u32[]{:S(2)}) collective-permute-start(f32[2,8,1280]{2,1,0:T(8,128)S(1)} %get-tuple-element.42), channel_id=1, source_target_pairs={{0,512},{32,544},{64,576},{96,608},{128,640},{160,672},{192,704},{... | collective-permute-start | bytes 245768 | tf_op jit(solution)/shard_map/ppermute | solution.py:189
  86.0 2.9 %collective-permute-done.11 = f32[2,8,1280]{2,1,0:T(8,128)S(1)} collective-permute-done((f32[2,8,1280]{2,1,0:T(8,128)S(1)}, f32[2,8,1280]{2,1,0:T(8,128)S(1)}, u32[]{:S(2)}, u32[]{:S(2)}) %collective-permute-start.11) | collective-permute-done | bytes 81952 | tf_op jit(solution)/shard_map/ppermute | solution.py:189
  88.9 2.0 %collective-permute-done.12 = f32[2,8,1280]{2,1,0:T(8,128)S(1)} collective-permute-done((f32[2,8,1280]{2,1,0:T(8,128)S(1)}, f32[2,8,1280]{2,1,0:T(8,128)S(1)}, u32[]{:S(2)}, u32[]{:S(2)}) %collective-permute-start.12) | collective-permute-done | bytes 81952 | tf_op jit(solution)/shard_map/ppermute | solution.py:189
  91.0 12.7 %all-gather = f32[8,8,1280]{2,1,0:T(8,128)S(1)} all-gather(f32[2,8,1280]{2,1,0:T(8,128)S(1)} %fusion.8), channel_id=2, replica_groups=mesh['dp'=24,'mp'=8,'rep'=4] {'rep'}, dimensions={0}, use_global_device_ids=true | all-gather | bytes 409600 | tf_op jit(solution)/shard_map/all_gather | solution.py:190
  103.7 1.9 %shard_map.96 = (f32[624,128]{1,0:T(8,128)}, f32[624,128]{1,0:T(8,128)}, f32[624,128]{1,0:T(8,128)}) custom-call(s32[2]{0:T(128)S(1)} %bitcast.79, f32[4,2,8,1280]{3,2,1,0:T(8,128)S(1)} %bitcast.74, f32[3,624,128]{2,1,0:T(8,128)S(1)} %get-tuple-element.31.own_ref, f32[3,260,128]{2,1,0:T(8,128)S(1)} %collective-permute-done.5.inner_ref, ...), custom_call_target="tpu_custom_call" | custom-call | flops 2000000 | bytes 3000000 | tf_op jit(solution)/shard_map/pallas_call | solution.py:286
  (24 shorter events, 0.3 us)
Async XLA Ops:
  5.3 5.9 %collective-permute-start.3 = (f32[48,8,1280]{2,1,0:T(8,128)S(1)}, f32[48,8,1280]{2,1,0:T(8,128)S(1)}, u32[]{:S(2)}, u32[]{:S(2)}) collective-permute-start(f32[48,8,1280]{2,1,0:T(8,128)S(1)} %get-tuple-element.26), channel_id=1, source_target_pairs={{0,32},{32,0},{64,96},{96,64},{128,160},{160,128},{192,224},{224,1... | collective-permute-start | bytes 5898248 | tf_op jit(solution)/shard_map/ppermute | solution.py:170
  7.3 8.9 %collective-permute-start = (f32[48,8,1280]{2,1,0:T(8,128)S(1)}, f32[48,8,1280]{2,1,0:T(8,128)S(1)}, u32[]{:S(2)}, u32[]{:S(2)}) collective-permute-start(f32[48,8,1280]{2,1,0:T(8,128)S(1)} %get-tuple-element.21), channel_id=1, source_target_pairs={{0,32},{32,0},{64,96},{96,64},{128,160},{160,128},{192,224},{224,1... | collective-permute-start | bytes 5898248 | tf_op jit(solution)/shard_map/ppermute | solution.py:170
  11.3 7.1 %copy-start = (f32[1,159744]{1,0:T(1,128)S(1)}, f32[1,159744]{1,0:T(1,128)}, u32[]{:S(2)}) copy-start(f32[1,159744]{1,0:T(1,128)} %param.11) | copy-start | bytes 1916932
  11.3 7.1 %copy-start.1 = (f32[1,159744]{1,0:T(1,128)S(1)}, f32[1,159744]{1,0:T(1,128)}, u32[]{:S(2)}) copy-start(f32[1,159744]{1,0:T(1,128)} %param.12) | copy-start | bytes 1916932
  11.3 7.1 %copy-start.2 = (f32[1,159744]{1,0:T(1,128)S(1)}, f32[1,159744]{1,0:T(1,128)}, u32[]{:S(2)}) copy-start(f32[1,159744]{1,0:T(1,128)} %param.13) | copy-start | bytes 1916932
  11.3 7.1 %copy-start.3 = (s32[1,1,2]{2,1,0:T(1,128)S(1)}, s32[1,1,2]{2,1,0:T(1,128)}, u32[]{:S(2)}) copy-start(s32[1,1,2]{2,1,0:T(1,128)} %param.10) | copy-start | bytes 28
  11.4 21.5 %collective-permute-start.4 = (f32[24,8,1280]{2,1,0:T(8,128)S(1)}, f32[24,8,1280]{2,1,0:T(8,128)S(1)}, u32[]{:S(2)}, u32[]{:S(2)}) collective-permute-start(f32[24,8,1280]{2,1,0:T(8,128)S(1)} %slice_add_fusion), channel_id=1, source_target_pairs={{0,3},{1,2},{2,1},{3,0},{32,736},{33,737},{34,738},{35,739},{64,67... | collective-permute-start | bytes 2949128 | tf_op jit(solution)/shard_map/ppermute | solution.py:171
  16.3 20.6 %collective-permute-start.1 = (f32[24,8,1280]{2,1,0:T(8,128)S(1)}, f32[24,8,1280]{2,1,0:T(8,128)S(1)}, u32[]{:S(2)}, u32[]{:S(2)}) collective-permute-start(f32[24,8,1280]{2,1,0:T(8,128)S(1)} %slice_add_fusion.1), channel_id=1, source_target_pairs={{0,1},{1,0},{2,3},{3,2},{32,96},{33,97},{34,98},{35,99},{64,65},{6... | collective-permute-start | bytes 2949128 | tf_op jit(solution)/shard_map/ppermute | solution.py:171
  20.6 12.8 %collective-permute-start.5 = (f32[3,260,128]{2,1,0:T(8,128)S(1)}, f32[3,260,128]{2,1,0:T(8,128)S(1)}, u32[]{:S(2)}, u32[]{:S(2)}) collective-permute-start(f32[3,260,128]{2,1,0:T(8,128)S(1)} %get-tuple-element.27), channel_id=1, source_target_pairs={{0,32},{32,0},{64,96},{96,64},{128,160},{160,128},{192,224},{224,1... | collective-permute-start | bytes 1198088 | tf_op jit(solution)/shard_map/ppermute | solution.py:175
  32.1 1.3 %collective-permute-start.6 = (f32[3,260,128]{2,1,0:T(8,128)S(1)}, f32[3,260,128]{2,1,0:T(8,128)S(1)}, u32[]{:S(2)}, u32[]{:S(2)}) collective-permute-start(f32[3,260,128]{2,1,0:T(8,128)S(1)} %get-tuple-element.28), channel_id=1, source_target_pairs={{32,64},{64,32},{96,128},{128,96},{160,192},{192,160},{224,256},{2... | collective-permute-start | bytes 1198088 | tf_op jit(solution)/shard_map/ppermute | solution.py:176
  33.5 10.7 %collective-permute-start.7 = (f32[12,8,1280]{2,1,0:T(8,128)S(1)}, f32[12,8,1280]{2,1,0:T(8,128)S(1)}, u32[]{:S(2)}, u32[]{:S(2)}) collective-permute-start(f32[12,8,1280]{2,1,0:T(8,128)S(1)} %get-tuple-element.30), channel_id=1, source_target_pairs={{0,1},{1,0},{2,3},{3,2},{32,96},{33,97},{34,98},{35,99},{64,65},{6... | collective-permute-start | bytes 1474568 | tf_op jit(solution)/shard_map/ppermute | solution.py:179
  37.1 11.9 %collective-permute-start.2 = (f32[12,8,1280]{2,1,0:T(8,128)S(1)}, f32[12,8,1280]{2,1,0:T(8,128)S(1)}, u32[]{:S(2)}, u32[]{:S(2)}) collective-permute-start(f32[12,8,1280]{2,1,0:T(8,128)S(1)} %get-tuple-element.24), channel_id=1, source_target_pairs={{0,3},{1,2},{2,1},{3,0},{32,736},{33,737},{34,738},{35,739},{64,67... | collective-permute-start | bytes 1474568 | tf_op jit(solution)/shard_map/ppermute | solution.py:179
  49.2 19.6 %collective-permute-start.8 = (f32[2,3,8,1280]{3,2,0,1:T(8,128)S(1)}, f32[2,3,8,1280]{3,2,0,1:T(8,128)S(1)}, u32[]{:S(2)}, u32[]{:S(2)}) collective-permute-start(f32[2,3,8,1280]{3,2,0,1:T(8,128)S(1)} %copy.13), channel_id=1, source_target_pairs={{0,704},{1,705},{2,706},{3,707},{32,35},{33,34},{34,33},{35,32},{6... | collective-permute-start | bytes 737288 | tf_op jit(solution)/shard_map/ppermute | solution.py:181
  64.0 8.1 %collective-permute-start.9 = (f32[2,3,8,1280]{3,2,0,1:T(8,128)S(1)}, f32[2,3,8,1280]{3,2,0,1:T(8,128)S(1)}, u32[]{:S(2)}, u32[]{:S(2)}) collective-permute-start(f32[2,3,8,1280]{3,2,0,1:T(8,128)S(1)} %copy.14), channel_id=1, source_target_pairs={{0,64},{1,65},{2,66},{3,67},{32,33},{33,32},{34,35},{35,34},{64,0}... | collective-permute-start | bytes 737288 | tf_op jit(solution)/shard_map/ppermute | solution.py:181
  66.0 10.2 %collective-permute-start.10 = (f32[2,3,8,1280]{3,2,0,1:T(8,128)S(1)}, f32[2,3,8,1280]{3,2,0,1:T(8,128)S(1)}, u32[]{:S(2)}, u32[]{:S(2)}) collective-permute-start(f32[2,3,8,1280]{3,2,0,1:T(8,128)S(1)} %copy.15), channel_id=1, source_target_pairs={{0,128},{1,129},{2,130},{3,131},{32,34},{33,35},{34,32},{35,33},{6... | collective-permute-start | bytes 737288 | tf_op jit(solution)/shard_map/ppermute | solution.py:181
  76.2 12.7 %collective-permute-start.11 = (f32[2,8,1280]{2,1,0:T(8,128)S(1)}, f32[2,8,1280]{2,1,0:T(8,128)S(1)}, u32[]{:S(2)}, u32[]{:S(2)}) collective-permute-start(f32[2,8,1280]{2,1,0:T(8,128)S(1)} %get-tuple-element.41), channel_id=1, source_target_pairs={{0,256},{32,288},{64,320},{96,352},{128,384},{160,416},{192,448},{... | collective-permute-start | bytes 245768 | tf_op jit(solution)/shard_map/ppermute | solution.py:189
  79.1 11.8 %collective-permute-start.12 = (f32[2,8,1280]{2,1,0:T(8,128)S(1)}, f32[2,8,1280]{2,1,0:T(8,128)S(1)}, u32[]{:S(2)}, u32[]{:S(2)}) collective-permute-start(f32[2,8,1280]{2,1,0:T(8,128)S(1)} %get-tuple-element.42), channel_id=1, source_target_pairs={{0,512},{32,544},{64,576},{96,608},{128,640},{160,672},{192,704},{... | collective-permute-start | bytes 245768 | tf_op jit(solution)/shard_map/ppermute | solution.py:189
